TPU v7x, 32 devices: a whole 2x2x4 slice. The times are simulated.
32 devices in a mesh: grp: 2 (over y), tchunk: 2 (over x), ha: 4 (over z), wa: 2 (over core).
Axes of the slice: x: 2, y: 2, z: 4, core: 2. Of those that a mesh axis runs over, the one named last changes fastest.
Arguments:
- features: bfloat16 [32, 32, 16, 192], P(('grp', 'tchunk'), 'ha', 'wa'), parts along dimension 0, may hold values from -6 to 6
- frame_counts: int32 [4], P(('grp', 'tchunk')), parts along dimension 0, may hold values from 0 to 8, as said below
- gain_first: float32 [192], replicated, may hold values from 0.25 to 1.75
- conv_first: bfloat16 [3, 3, 3, 192, 192], replicated, may hold values from -0.078125 to 0.078125
- bias_first: float32 [192], replicated, may hold values from -1.8 to 1.8
- gain_second: float32 [192], replicated, may hold values from 0.25 to 1.75
- conv_second: bfloat16 [3, 3, 3, 192, 192], replicated, may hold values from -0.078125 to 0.078125
- bias_second: float32 [192], replicated, may hold values from -1.8 to 1.8
Outputs:
- decoded: bfloat16 [32, 32, 16, 192], P(('grp', 'tchunk'), 'ha', 'wa'), parts along dimension 0
There are 2 independent parts, one for each index of `grp`. A program takes and returns all parts, laid end to end along the dimension named above; an argument that names none is the same for every part. Nothing has to cross between parts.
Inputs may be any that keep to these rules, and one draw needn't show every extreme that they name: `frame_counts`: in every draw some temporal block has all 8 slots live; any block may have none.
All inputs are finite; a program needn't handle non-finite values.
Results may differ from a plain program's by a relative error of at most 0.0039.
Values may be sent and summed in bfloat16 or wider, within the bound.
No kernel may reach another device: no remote copies, remote signals or barrier semaphores. Data moves between devices by JAX's collectives and lax.ppermute only.
A program may use at most 64 MiB of HBM per device.

v0:
```python
import jax
import jax.numpy as jnp
from jax import lax
from jax.experimental import pallas as pl
from jax.experimental.pallas import tpu as pltpu
from jax.sharding import PartitionSpec as P

epsilon = 1e-06
CACHE = 4
TAPS = 3
LANES = 128
PRODUCT = 192


def slots_kernel(slots_ref):
    slots_ref[...] = lax.broadcasted_iota(jnp.int32, slots_ref.shape, 0)


def prepare_kernel(total_ref, slots_ref, raw, tail_ref, mine_ref, theirs_ref, marks_ref, pack):
    frames, rows = raw.shape[:2]
    pairs, held = rows // 2, mine_ref.shape[1]
    core = lax.axis_index("wa")
    total = total_ref[0]
    for frame in range(frames):
        for pair in range(pairs):
            first, second = raw[frame, 2 * pair], raw[frame, 2 * pair + 1]
            packed = jnp.concatenate(
                [first[:, :LANES], second[:, :LANES], first[:, LANES:], second[:, LANES:]], axis=-1
            )
            pack[frame, pair] = packed
    for slot in range(CACHE):
        frame = total - CACHE + slot
        value = pack[jnp.maximum(frame, 0)]
        tail_ref[slot * pairs:(slot + 1) * pairs] = jnp.where(frame >= 0, value, jnp.zeros_like(value))
        value = pack[jnp.maximum(frame, 0), pl.ds((1 - core) * (pairs - held), held)]
        theirs_ref[slot * held:(slot + 1) * held] = jnp.where(frame >= 0, value, jnp.zeros_like(value))
    for frame in range(frames):
        start = (CACHE + frame) * held
        value = pack[frame, pl.ds(core * (pairs - held), held)]
        mine_ref[frame] = jnp.where(frame < total, value, jnp.zeros_like(value))
        value = pack[frame, pl.ds((1 - core) * (pairs - held), held)]
        theirs_ref[start:start + held] = jnp.where(frame < total, value, jnp.zeros_like(value))
    slot = slots_ref[...]
    tail_ref[CACHE * pairs] = jnp.where(
        (slot < CACHE) & (total - CACHE + slot >= 0), 1.0, 0.0
    ).astype(tail_ref.dtype)
    marks_ref[...] = jnp.where(slot < total, 1.0, 0.0).astype(marks_ref.dtype)


def joined_tail(tail):
    count = lax.axis_size("tchunk")

    def pushed(value, held):
        return lax.dynamic_slice_in_dim(jnp.concatenate([value, jnp.zeros_like(value)], axis=0), held, CACHE, 0)

    step = 1
    while step < count - 1:
        early = lax.ppermute(tail, "tchunk", [(k, k + step) for k in range(count - step)])
        held = jnp.sum(tail[-1, :CACHE, 0].astype(jnp.int32))
        body = pushed(early[:-1].reshape((CACHE, -1) + tail.shape[1:]), held).reshape(tail[:-1].shape)
        marks = jnp.pad(pushed(early[-1, :CACHE], held), ((0, tail.shape[1] - CACHE), (0, 0)))
        tail = tail + jnp.concatenate([body, marks[None]], axis=0)
        step *= 2
    return tail


def silu(half):
    return half + half * jnp.tanh(half)


def lane_mask():
    return lax.broadcasted_iota(jnp.int32, (1, 1, 1, LANES), 3) < LANES // 2


def gains(gain_ref):
    low, high = 0.5 * gain_ref[:, :LANES], 0.5 * gain_ref[:, LANES:]
    return low.reshape(1, 1, 1, LANES), jnp.concatenate([high, high], axis=-1).reshape(1, 1, 1, LANES)


def rolled(values):
    shape = values.shape
    return pltpu.roll(values.reshape(-1, LANES), LANES // 2, 1).reshape(shape)


def first_rows(left, right, gain_ref, channels):
    raw = jnp.concatenate([left.astype(jnp.float32), right.astype(jnp.float32)], axis=2)
    front, back, high = raw[..., :LANES], raw[..., LANES:2 * LANES], raw[..., 2 * LANES:]
    lower = lane_mask()
    squared = high * high

    def inverse(low, mask):
        total = jnp.sum(low * low + jnp.where(mask, squared, 0.0), axis=-1, keepdims=True)
        return lax.rsqrt(total * (1.0 / channels) + epsilon)

    scale_front, scale_back = inverse(front, lower), inverse(back, jnp.logical_not(lower))
    gain_low, gain_high = gains(gain_ref)
    front = silu(front * scale_front * gain_low)
    back = silu(back * scale_back * gain_low)
    high = silu(high * jnp.where(lower, scale_front, scale_back) * gain_high)
    turned = rolled(high)
    one = [front, jnp.where(lower, high, 0.0), jnp.where(lower, 0.0, turned)]
    two = [back, jnp.where(lower, turned, 0.0), jnp.where(lower, 0.0, high)]
    return [[part.astype(jnp.bfloat16) for part in row] for row in (one, two)]


def second_rows(hidden, flag, gain_ref, channels):
    gain = 0.5 * gain_ref[...].reshape(1, 1, 1, channels)
    total = jnp.sum(hidden * hidden, axis=-1, keepdims=True)
    inverse = lax.rsqrt(total * (1.0 / channels) + epsilon) * flag
    values = silu(hidden * inverse * gain)
    rest = jnp.zeros(values.shape[:-1] + (LANES // 2,), jnp.float32)
    high = jnp.concatenate([values[..., LANES:], rest], axis=-1)
    parts = [values[..., :LANES], high, rolled(high)]
    return jnp.stack([part.astype(jnp.bfloat16) for part in parts])


def convolved(operand, weights_ref, bias_ref, frame, frames, rows, then):
    products = -(-frames * rows * operand.shape[3] // PRODUCT)
    step = -(-frames // products)
    for start in range(0, frames, step):
        count = min(step, frames - start)
        then(start, count, convolved_part(operand, weights_ref, bias_ref, frame + start, count, rows))


def convolved_part(operand, weights_ref, bias_ref, frame, frames, rows):
    width = operand.shape[3]
    channels = weights_ref.shape[-1]
    taps = [(a, i) for a in range(TAPS) for i in range(TAPS)]
    groups = [taps[start:start + 2] for start in range(0, len(taps), 2)]

    def window(tap, part):
        a, i = tap
        value = operand[part, frame + a:frame + a + frames, i:i + rows]
        return value.reshape(frames * rows * width, LANES)

    def operands(groups):
        pieces = []
        for group in groups:
            pieces += [window(tap, 0) for tap in group]
            high = window(group[0], 1)
            pieces.append(high + window(group[1], 2) if len(group) > 1 else high)
        return jnp.concatenate(pieces, axis=-1)

    def weights(groups, j, depth):
        rights = []
        for group in groups:
            held = [weights_ref[a, i, j] for a, i in group]
            rights += [weight[:LANES] for weight in held] + [weight[LANES:] for weight in held]
        rest = depth - sum(right.shape[0] for right in rights)
        if rest:
            rights.append(jnp.zeros((rest, channels), jnp.bfloat16))
        return jnp.concatenate(rights, axis=0)

    half = len(groups) // 2
    parts = [(part, operands(part)) for part in (groups[:half], groups[half:])]
    products = []
    for j in range(TAPS):
        total = None
        for part, left in parts if j % 2 == 0 else parts[::-1]:
            product = jnp.dot(left, weights(part, j, left.shape[1]), preferred_element_type=jnp.float32)
            total = product if total is None else total + product
        products.append(total.reshape(frames * rows, width, channels))
    column = lax.broadcasted_iota(jnp.int32, (1, width, 1), 1)
    before = jnp.where(column == 0, 0.0, pltpu.roll(products[0], 1, 1))
    after = jnp.where(column == width - 1, 0.0, pltpu.roll(products[2], width - 1, 1))
    result = products[1] + before + after + bias_ref[...].reshape(1, 1, channels)
    return result.reshape(frames, rows, width, channels)


def halves(core, mine, other):
    return jnp.where(core == 0, mine, other), jnp.where(core == 0, other, mine)


def frame_flags(marks, frames):
    values = marks.astype(jnp.float32)
    return [values[k:k + 1, 0:1].reshape(1, 1, 1, 1) for k in frames]


def fill_rows(operand, frame, row, mine, other, gain_ref):
    left, right = halves(lax.axis_index("wa"), mine, other)
    frames, pairs = mine.shape[:2]
    upper, lower = first_rows(left, right, gain_ref, gain_ref.shape[-1])
    for part in range(len(upper)):
        for pair in range(pairs):
            operand[part, frame:frame + frames, pl.ds(row + 2 * pair, 1)] = upper[part][:, pair:pair + 1]
            operand[part, frame:frame + frames, pl.ds(row + 2 * pair + 1, 1)] = lower[part][:, pair:pair + 1]


def border_kernel(tail_ref, mine_ref, other_ref, tail_edge_ref, own_edge_ref):
    frames, held = mine_ref.shape[:2]
    pairs = tail_ref.shape[0] // CACHE
    core = lax.axis_index("wa")
    pair = core * (held - 1)
    for slot in range(CACHE):
        tail_edge_ref[slot] = tail_ref[slot * pairs + core * (pairs - 1)]
        tail_edge_ref[CACHE + slot] = other_ref[slot * held + pair]
    spare = tail_edge_ref.shape[0] - 2 * CACHE
    tail_edge_ref[2 * CACHE:] = jnp.zeros((spare,) + tail_edge_ref.shape[1:], tail_edge_ref.dtype)
    for frame in range(frames):
        own_edge_ref[0, frame] = mine_ref[frame, pair]
        own_edge_ref[1, frame] = other_ref[(CACHE + frame) * held + pair]


def finish(mine_ref, other_ref, live, first, pairs, value, targets):
    _, held, side, _ = mine_ref.shape
    frames, channels = value.shape[0], value.shape[-1]
    start, count = pairs
    near, far = halves(lax.axis_index("wa"), value[:, :, :side], value[:, :, side:])
    for mine, value, target in ((True, near, targets[0]), (False, far, targets[1])):
        for frame in range(frames):
            for k in range(count):
                if mine:
                    raw = mine_ref[first + frame, start + k]
                else:
                    raw = other_ref[(CACHE + first + frame) * held + start + k]
                raw = raw.astype(jnp.float32)
                high = raw[:, 2 * LANES:]
                for row, tail in ((0, high), (1, pltpu.roll(high, LANES // 2, 1))):
                    low = raw[:, row * LANES:(row + 1) * LANES]
                    features = jnp.concatenate([low, tail[:, :channels - LANES]], axis=-1)
                    summed = features + value[frame, 2 * k + row]
                    kept = jnp.where(live[first + frame].reshape(1, 1) > 0.5, summed, 0.0)
                    target(first + frame, 2 * k + row, kept.astype(jnp.bfloat16))


def hide(operand, weights_ref, bias_ref, gain_ref, first, count, rows, flags, store):
    channels = weights_ref.shape[-1]

    def then(begin, part, hidden):
        flag = jnp.concatenate(flags[begin:begin + part], axis=0)
        store(begin, begin + part, second_rows(hidden, flag, gain_ref, channels))

    convolved(operand, weights_ref, bias_ref, first, count, rows, then)


def inside_flags(rows):
    core, place = lax.axis_index("wa"), lax.axis_index("ha")
    inside = jnp.where(core == 0, place > 0, place < lax.axis_size("ha") - 1)
    row = lax.broadcasted_iota(jnp.int32, (1, rows, 1, 1), 1)
    return jnp.where((row == (rows - 1) * core) & jnp.logical_not(inside), 0.0, 1.0)


def other_rows_kernel(tail_ref, late_ref, rest_ref):
    pairs, held = tail_ref.shape[0] // CACHE, rest_ref.shape[0] // CACHE
    first = (1 - lax.axis_index("wa")) * (pairs - held)
    for slot in range(CACHE):
        rest_ref[slot * held:(slot + 1) * held] = tail_ref[pl.ds(slot * pairs + first, held)]


def own_kernel(
    marks_ref, mine_ref, other_ref, gain1_ref, w1_ref, bias1_ref, gain2_ref, first_ref, late_ref
):
    frames, pairs, side, packed = mine_ref.shape
    other = other_ref[CACHE * pairs:].reshape(frames, pairs, side, packed)
    fill_rows(first_ref, 0, 0, mine_ref[...], other, gain1_ref)
    live = frame_flags(marks_ref[...], range(2, frames))

    def store(begin, end, rows):
        late_ref[:, begin:end] = rows

    hide(first_ref, w1_ref, bias1_ref, gain2_ref, 0, frames - 2, 2 * pairs - 2, live, store)


def edge_kernel(
    marks_ref, mine_ref, other_ref, edge_ref, first_ref, late_ref,
    gain1_ref, w1_ref, bias1_ref, gain2_ref, w2_ref, bias2_ref,
    strip_ref, hidden_ref, keep_ref, send_ref, strip, operand,
):
    core = lax.axis_index("wa")
    frames, pairs = mine_ref.shape[:2]
    rows = 2 * pairs
    fill_rows(strip, 0, 2 * core, edge_ref[1][:, None], edge_ref[0][:, None], gain1_ref)
    strip[:, :, pl.ds(2 * (1 - core), 2)] = first_ref[:, :, pl.ds((rows - 2) * core, 2)]
    live = frame_flags(marks_ref[...], range(frames))
    inside = inside_flags(2)

    def store(begin, end, values):
        operand[:, begin:end, pl.ds((rows - 2) * core, 2)] = values

    hide(strip, w1_ref, bias1_ref, gain2_ref, 0, frames - 2, 2, [flag * inside for flag in live[2:]], store)
    operand[:, :, pl.ds(2 * (1 - core), rows - 2)] = late_ref[...]
    strip_ref[...] = strip[:, 0:2, pl.ds(2 * core, 2)]
    hidden_ref[...] = operand[:, 0:2]

    def put(ref):
        def store(frame, row, value):
            ref[frame - CACHE, row] = value
        return store

    def then(start, part, result):
        finish(
            mine_ref, other_ref, live, CACHE + start, (core, pairs - 1), result, (put(keep_ref), put(send_ref))
        )

    convolved(operand, w2_ref, bias2_ref, 0, frames - CACHE, rows - 2, then)


def early_kernel(
    marks_ref, tail_mine_ref, tail_other_ref, mine_ref, other_ref, edge_ref, first_ref, strip_ref, hidden_ref,
    late_keep_ref, late_send_ref, gain1_ref, w1_ref, bias1_ref, gain2_ref, w2_ref, bias2_ref,
    keep_ref, send_ref, plane, operand,
):
    core = lax.axis_index("wa")
    held = mine_ref.shape[1]
    rows = 2 * held
    pairs = tail_mine_ref.shape[0] // CACHE
    live = frame_flags(marks_ref[...], range(CACHE))
    inside = inside_flags(rows)
    earlier = lax.axis_index("tchunk") > 0
    middle, border = 2 * (1 - core), rows * core

    def unpacked(ref, stride, first):
        return jnp.stack([ref[pl.ds(slot * stride + first, held)] for slot in range(CACHE)])

    plane[:, CACHE:, pl.ds(middle, rows)] = first_ref[:, 0:2]
    plane[:, CACHE:, pl.ds(border, 2)] = strip_ref[...]
    operand[:, CACHE:] = hidden_ref[...]

    def fill(first, flags):
        def store(begin, end, values):
            operand[:, first + begin:first + end] = values

        flags = [flag * inside for flag in flags]
        hide(plane, w1_ref, bias1_ref, gain2_ref, first, CACHE - first, rows, flags, store)

    @pl.when(earlier)
    def _():
        mine = unpacked(tail_mine_ref, pairs, core * (pairs - held))
        fill_rows(plane, 0, middle, mine, unpacked(tail_other_ref, held, 0), gain1_ref)
        mine, other = edge_ref[CACHE:2 * CACHE], edge_ref[0:CACHE]
        fill_rows(plane, 0, border, mine[:, None], other[:, None], gain1_ref)
        fill(0, frame_flags(tail_mine_ref[CACHE * pairs], range(CACHE - 2, CACHE)) + live[0:2])

    @pl.when(jnp.logical_not(earlier))
    def _():
        plane[:, 0:CACHE] = jnp.zeros(plane.shape[:1] + (CACHE,) + plane.shape[2:], plane.dtype)
        operand[:, 0:2] = jnp.zeros(operand.shape[:1] + (2,) + operand.shape[2:], operand.dtype)
        fill(2, live[0:2])

    def put(ref):
        def store(frame, row, value):
            ref[frame, row] = value
        return store

    def then(start, part, result):
        finish(mine_ref, other_ref, live, start, (core, held - 1), result, (put(keep_ref), put(send_ref)))

    convolved(operand, w2_ref, bias2_ref, 0, CACHE, rows - 2, then)
    keep_ref[CACHE:] = late_keep_ref[...]
    send_ref[CACHE:] = late_send_ref[...]


def place_kernel(keep_ref, got_ref, result_ref, arrived):
    core, half = lax.axis_index("wa"), keep_ref.shape[1]
    copies = [
        pltpu.make_async_copy(keep_ref, result_ref.at[:, pl.ds(half * core, half)], arrived.at[0]),
        pltpu.make_async_copy(got_ref, result_ref.at[:, pl.ds(half * (1 - core), half)], arrived.at[1]),
    ]
    for copy in copies:
        copy.start()
    for copy in copies:
        copy.wait()


def shards(features, frame_counts, gain_first, conv_first, bias_first, gain_second, conv_second, bias_second):
    frames, rows, side, channels = features.shape
    pairs, half = rows // 2, rows // 2
    held = half // 2 + 1
    tall, cores, blocks = lax.axis_size("ha"), lax.axis_size("wa"), lax.axis_size("tchunk")
    packed, width, tiles = 3 * LANES, 2 * side, CACHE * held
    bf16 = jnp.bfloat16
    vmem = pl.BlockSpec(memory_space=pltpu.VMEM)
    limit = pltpu.CompilerParams(vmem_limit_bytes=20 * 2**20)
    work = 2 * TAPS**3 * channels * channels * width

    def shape(*extent):
        return jax.ShapeDtypeStruct(extent, bf16)

    def cost(flops, fetched):
        return pl.CostEstimate(flops=flops, bytes_accessed=fetched, transcendentals=0)

    slots = pl.pallas_call(
        slots_kernel,
        out_shape=jax.ShapeDtypeStruct((side, packed), jnp.int32),
        out_specs=vmem,
        compiler_params=limit,
        cost_estimate=cost(2**34, 2**20),
    )()
    slots, frame_counts = lax.optimization_barrier((slots, frame_counts))
    tail, mine, theirs, marks = pl.pallas_call(
        prepare_kernel,
        out_shape=(
            shape(CACHE * pairs + 1, side, packed), shape(frames, held, side, packed),
            shape((CACHE + frames) * held, side, packed), shape(side, packed),
        ),
        in_specs=[pl.BlockSpec(memory_space=pltpu.SMEM), vmem, vmem],
        out_specs=(vmem,) * 4,
        scratch_shapes=[pltpu.VMEM((frames, pairs, side, packed), bf16)],
        compiler_params=limit,
    )(frame_counts, slots, features)

    if blocks > 2:
        tail = joined_tail(tail)
        rest = lax.dynamic_slice_in_dim(
            tail[:-1].reshape(CACHE, pairs, side, packed), (1 - lax.axis_index("wa")) * (pairs - held), held, 1
        )
        theirs = jnp.concatenate([rest.reshape(tiles, side, packed), theirs[tiles:]], axis=0)
    straight, diagonal, across = [], [], []

    def index(block, h, core):
        return (block * tall + h) * cores + core

    for k in range(blocks - 1):
        for h in range(tall):
            for core in range(cores):
                straight.append((index(k, h, core), index(k + 1, h, core)))
    for h in range(tall - 1):
        for k in range(blocks):
            lower, upper = index(k, h, 1), index(k, h + 1, 0)
            across += [(lower, upper), (upper, lower)]
            if k + 1 < blocks:
                lower_next, upper_next = index(k + 1, h, 1), index(k + 1, h + 1, 0)
                diagonal += [(lower, upper_next), (upper, lower_next)]
    axes = ("tchunk", "ha", "wa")
    swap = [(0, 1), (1, 0)]
    tail_mine = lax.ppermute(tail, axes, straight)
    other = lax.ppermute(theirs, "wa", swap)
    tail_edge, own_edge = pl.pallas_call(
        border_kernel,
        out_shape=(shape(tiles + 1, side, packed), shape(2, frames, side, packed)),
        in_specs=[vmem] * 3,
        out_specs=(vmem, vmem),
        compiler_params=limit,
        cost_estimate=cost(2**34, 2**20),
    )(tail, mine, other)
    own_edge = lax.ppermute(own_edge, axes, across)
    tail_edge = lax.ppermute(tail_edge, axes, diagonal)

    weights = (
        gain_first.reshape(1, channels), conv_first, bias_first.reshape(1, channels),
        gain_second.reshape(1, channels), conv_second, bias_second.reshape(1, channels),
    )
    first, late = pl.pallas_call(
        own_kernel,
        out_shape=(shape(3, frames, half + 2, width, LANES), shape(3, frames - 2, half, width, LANES)),
        in_specs=[vmem] * 7,
        out_specs=(vmem,) * 2,
        compiler_params=limit,
        cost_estimate=cost(work * (frames - 2) * half, 4 * 2**20),
    )(marks, mine, other, *weights[:4])
    rest = pl.pallas_call(
        other_rows_kernel,
        out_shape=shape(tiles, side, packed),
        in_specs=[vmem, pl.BlockSpec(memory_space=pl.ANY)],
        out_specs=vmem,
        compiler_params=limit,
        cost_estimate=cost(1, 1),
    )(tail_mine, late)
    tail_other = lax.ppermute(rest, "wa", swap)
    strip, hidden, keep, send = pl.pallas_call(
        edge_kernel,
        out_shape=(
            shape(3, 2, 2, width, LANES), shape(3, 2, half + 2, width, LANES),
            shape(frames - CACHE, half, side, channels), shape(frames - CACHE, half, side, channels),
        ),
        in_specs=[vmem] * 12,
        out_specs=(vmem,) * 4,
        scratch_shapes=[
            pltpu.VMEM((3, frames, 4, width, LANES), bf16),
            pltpu.VMEM((3, frames - 2, half + 2, width, LANES), bf16),
        ],
        compiler_params=limit,
        cost_estimate=cost(2**20, 2**20),
    )(marks, mine, other, own_edge, first, late, *weights)
    keep, send = pl.pallas_call(
        early_kernel,
        out_shape=(shape(frames, half, side, channels), shape(frames, half, side, channels)),
        in_specs=[vmem] * 17,
        out_specs=(vmem, vmem),
        scratch_shapes=[
            pltpu.VMEM((3, CACHE + 2, half + 4, width, LANES), bf16),
            pltpu.VMEM((3, CACHE + 2, half + 2, width, LANES), bf16),
        ],
        compiler_params=limit,
        cost_estimate=cost(work * CACHE * (2 * half + 2), 8 * 2**20),
    )(marks, tail_mine, tail_other, mine, other, tail_edge, first, strip, hidden, keep, send, *weights)
    got = lax.ppermute(send, "wa", swap)
    return pl.pallas_call(
        place_kernel,
        out_shape=shape(*features.shape),
        in_specs=[vmem, vmem],
        out_specs=pl.BlockSpec(memory_space=pltpu.HBM),
        scratch_shapes=[pltpu.SemaphoreType.DMA((2,))],
        compiler_params=limit,
    )(keep, got)


def solution(mesh):
    return jax.shard_map(
        shards,
        mesh=mesh,
        in_specs=(
            P(("grp", "tchunk"), "ha", "wa", None),
            P(("grp", "tchunk")),
            P(), P(), P(), P(), P(), P(),
        ),
        out_specs=P(("grp", "tchunk"), "ha", "wa", None),
        check_vma=False,
    )
```

profile of v0, /device:TPU:0, one launch (start us, length us, event | category | flops | bytes accessed | tf_op | source)
XLA Modules:
  0.0 19.9 jit_solution(10458879647739421560)
XLA Ops:
  0.0 0.0 copy-start.2
  0.7 0.3 %copy-done.2 = bf16[8,8,8,192]{3,2,1,0:T(8,128)(2,1)S(1)} copy-done((bf16[8,8,8,192]{3,2,1,0:T(8,128)(2,1)S(1)}, bf16[8,8,8,192]{3,2,1,0:T(8,128)(2,1)}, u32[]{:S(2)}) %copy-start.2) | copy-done | bytes 196632
  1.0 0.1 shard_map.83
  1.1 0.5 %collective-permute-start.1 = (bf16[36,8,384]{2,1,0:T(8,128)(2,1)S(1)}, bf16[36,8,384]{2,1,0:T(8,128)(2,1)S(1)}, u32[]{:S(2)}, u32[]{:S(2)}) collective-permute-start(bf16[36,8,384]{2,1,0:T(8,128)(2,1)S(1)} %get-tuple-element.26), channel_id=1, source_target_pairs={{0,1},{1,0},{2,3},{3,2},{4,5},{5,4},{6,7},{7,6},{8,9},{9,8},{10,11... | collective-permute-start | bytes 663560 | tf_op jit(solution)/shard_map/ppermute | solution.py:427
  1.6 4.4 %collective-permute-start = (bf16[17,8,384]{2,1,0:T(8,128)(2,1)S(1)}, bf16[17,8,384]{2,1,0:T(8,128)(2,1)S(1)}, u32[]{:S(2)}, u32[]{:S(2)}) collective-permute-start(bf16[17,8,384]{2,1,0:T(8,128)(2,1)S(1)} %get-tuple-element.24.tail_ref), channel_id=1, source_target_pairs={{0,8},{1,9},{2,10},{3,11},{4,12},{5,13},{6,14},{7,15},{16,24},{17,... | collective-permute-start | bytes 313352 | tf_op jit(solution)/shard_map/ppermute | solution.py:426
  6.1 0.0 collective-permute-done.1.other_ref
  6.1 0.0 copy-start
  6.1 0.0 copy-start.3
  6.1 0.0 copy-start.4
  6.1 0.0 copy-start.5
  6.1 0.0 copy-start.1
  6.2 0.0 copy-start.6
  6.2 0.8 %collective-permute-start.4 = (bf16[2,8,8,384]{3,2,1,0:T(8,128)(2,1)S(1)}, bf16[2,8,8,384]{3,2,1,0:T(8,128)(2,1)S(1)}, u32[]{:S(2)}, u32[]{:S(2)}) collective-permute-start(bf16[2,8,8,384]{3,2,1,0:T(8,128)(2,1)S(1)} %get-tuple-element.30), channel_id=1, source_target_pairs={{1,2},{2,1},{9,10},{10,9},{3,4},{4,3},{11,12},{12,11},{5,6},{6,5},... | collective-permute-start | bytes 294920 | tf_op jit(solution)/shard_map/ppermute | solution.py:436
  7.0 0.8 %collective-permute-start.3 = (bf16[13,8,384]{2,1,0:T(8,128)(2,1)S(1)}, bf16[13,8,384]{2,1,0:T(8,128)(2,1)S(1)}, u32[]{:S(2)}, u32[]{:S(2)}) collective-permute-start(bf16[13,8,384]{2,1,0:T(8,128)(2,1)S(1)} %get-tuple-element.28), channel_id=1, source_target_pairs={{1,10},{2,9},{3,12},{4,11},{5,14},{6,13},{17,26},{18,25},{19,28},{... | collective-permute-start | bytes 239624 | tf_op jit(solution)/shard_map/ppermute | solution.py:437
  7.8 0.0 copy-done
  7.8 0.0 copy-done.3
  7.8 0.0 copy-done.4
  7.8 0.0 copy-done.5
  7.8 1.8 %shard_map.84 = (bf16[3,8,6,16,128]{4,3,2,1,0:T(8,128)(2,1)S(1)}, bf16[3,6,4,16,128]{4,3,2,1,0:T(8,128)(2,1)S(1)}) custom-call(bf16[8,384]{1,0:T(8,128)(2,1)S(1)} %get-tuple-element.23.marks_ref, bf16[8,3,8,384]{3,2,1,0:T(8,128)(2,1)S(1)} %get-tuple-element.25.mine_ref, bf16[36,8,384]{2,1,0:T(8,128)(2,1)S(1)} %collective-permute-done.1.other_ref, ...), custom_call_target="tpu_custom_call" | custom-call | flops 764411904 | bytes 4194304 | tf_op jit(solution)/shard_map/pallas_call | solution.py:443
  9.7 0.0 collective-permute-done.tail_ref.tail_mine_ref
  9.7 3.6 %collective-permute-start.2 = (bf16[12,8,384]{2,1,0:T(8,128)(2,1)S(1)}, bf16[12,8,384]{2,1,0:T(8,128)(2,1)S(1)}, u32[]{:S(2)}, u32[]{:S(2)}) collective-permute-start(bf16[12,8,384]{2,1,0:T(8,128)(2,1)S(1)} %shard_map.85), channel_id=1, source_target_pairs={{0,1},{1,0},{2,3},{3,2},{4,5},{5,4},{6,7},{7,6},{8,9},{9,8},{10,11... | collective-permute-start | bytes 221192 | tf_op jit(solution)/shard_map/ppermute | solution.py:459
  13.3 0.0 collective-permute-done.4.edge_ref
  13.3 0.0 copy-done.1
  13.3 0.0 copy-done.6
  13.3 2.4 %shard_map.87 = (bf16[3,2,2,16,128]{4,3,2,1,0:T(8,128)(2,1)S(1)}, bf16[3,2,6,16,128]{4,3,2,1,0:T(8,128)(2,1)S(1)}, bf16[4,4,8,192]{3,2,1,0:T(8,128)(2,1)S(1)}, bf16[4,4,8,192]{3,2,1,0:T(8,128)(2,1)S(1)}) custom-call(bf16[8,384]{1,0:T(8,128)(2,1)S(1)} %get-tuple-element.23.marks_ref, bf16[8,3,8,384]{3,2,1,0:T(8,128)(2,1)S(1)} %get-tuple-element.25.mine_ref, ...), custom_call_target="tpu_custom_call" | custom-call | flops 1048576 | bytes 1048576 | tf_op jit(solution)/shard_map/pallas_call | solution.py:460
  15.8 0.0 collective-permute-done.2.tail_other_ref
  15.8 0.0 collective-permute-done.3.edge_ref
  15.8 1.9 %shard_map.88 = (bf16[8,4,8,192]{3,2,1,0:T(8,128)(2,1)S(1)}, bf16[8,4,8,192]{3,2,1,0:T(8,128)(2,1)S(1)}) custom-call(bf16[8,384]{1,0:T(8,128)(2,1)S(1)} %get-tuple-element.23.marks_ref, bf16[17,8,384]{2,1,0:T(8,128)(2,1)S(1)} %collective-permute-done.tail_ref.tail_mine_ref, bf16[12,8,384]{2,1,0:T(8,128)(2,1)S(1)} %collective-permute-done.2.tail_other_ref, ...), custom_call_target="tpu_custom_call" | custom-call | flops 1274019840 | bytes 8388608 | tf_op jit(solution)/shard_map/pallas_call | solution.py:475
  17.7 0.1 collective-permute-start.5
  17.8 1.3 %collective-permute-done.5.got_ref = bf16[8,4,8,192]{3,2,1,0:T(8,128)(2,1)S(1)} collective-permute-done((bf16[8,4,8,192]{3,2,1,0:T(8,128)(2,1)S(1)}, bf16[8,4,8,192]{3,2,1,0:T(8,128)(2,1)S(1)}, u32[]{:S(2)}, u32[]{:S(2)}) %collective-permute-start.5) | collective-permute-done | bytes 98336 | tf_op jit(solution)/shard_map/ppermute | solution.py:487
  19.1 0.7 %shard_map.89 = bf16[8,8,8,192]{3,2,1,0:T(8,128)(2,1)} custom-call(bf16[8,4,8,192]{3,2,1,0:T(8,128)(2,1)S(1)} %get-tuple-element.35.keep_ref, bf16[8,4,8,192]{3,2,1,0:T(8,128)(2,1)S(1)} %collective-permute-done.5.got_ref), custom_call_target="tpu_custom_call" | custom-call | tf_op jit(solution)/shard_map/pallas_call | solution.py:488
  (3 shorter events, 0.0 us)
Async XLA Ops:
  0.0 1.0 %copy-start.2 = (bf16[8,8,8,192]{3,2,1,0:T(8,128)(2,1)S(1)}, bf16[8,8,8,192]{3,2,1,0:T(8,128)(2,1)}, u32[]{:S(2)}) copy-start(bf16[8,8,8,192]{3,2,1,0:T(8,128)(2,1)} %raw.1) | copy-start | bytes 589828
  1.1 4.9 %collective-permute-start.1 = (bf16[36,8,384]{2,1,0:T(8,128)(2,1)S(1)}, bf16[36,8,384]{2,1,0:T(8,128)(2,1)S(1)}, u32[]{:S(2)}, u32[]{:S(2)}) collective-permute-start(bf16[36,8,384]{2,1,0:T(8,128)(2,1)S(1)} %get-tuple-element.26), channel_id=1, source_target_pairs={{0,1},{1,0},{2,3},{3,2},{4,5},{5,4},{6,7},{7,6},{8,9},{9,8},{10,11... | collective-permute-start | bytes 663560 | tf_op jit(solution)/shard_map/ppermute | solution.py:427
  1.6 8.0 %collective-permute-start = (bf16[17,8,384]{2,1,0:T(8,128)(2,1)S(1)}, bf16[17,8,384]{2,1,0:T(8,128)(2,1)S(1)}, u32[]{:S(2)}, u32[]{:S(2)}) collective-permute-start(bf16[17,8,384]{2,1,0:T(8,128)(2,1)S(1)} %get-tuple-element.24.tail_ref), channel_id=1, source_target_pairs={{0,8},{1,9},{2,10},{3,11},{4,12},{5,13},{6,14},{7,15},{16,24},{17,... | collective-permute-start | bytes 313352 | tf_op jit(solution)/shard_map/ppermute | solution.py:426
  6.1 1.8 %copy-start = (bf16[3,3,3,192,192]{4,3,2,1,0:T(8,128)(2,1)S(1)}, bf16[3,3,3,192,192]{4,3,2,1,0:T(8,128)(2,1)}, u32[]{:S(2)}) copy-start(bf16[3,3,3,192,192]{4,3,2,1,0:T(8,128)(2,1)} %w1_ref.5) | copy-start | bytes 5971972
  6.1 1.7 %copy-start.3 = (f32[192]{0:T(256)S(1)}, f32[192]{0:T(256)}, u32[]{:S(2)}) copy-start(f32[192]{0:T(256)} %param.10) | copy-start | bytes 2308
  6.1 1.7 %copy-start.4 = (f32[192]{0:T(256)S(1)}, f32[192]{0:T(256)}, u32[]{:S(2)}) copy-start(f32[192]{0:T(256)} %param.12) | copy-start | bytes 2308
  6.1 1.7 %copy-start.5 = (f32[192]{0:T(256)S(1)}, f32[192]{0:T(256)}, u32[]{:S(2)}) copy-start(f32[192]{0:T(256)} %param.13) | copy-start | bytes 2308
  6.1 7.2 %copy-start.1 = (bf16[3,3,3,192,192]{4,3,2,1,0:T(8,128)(2,1)S(1)}, bf16[3,3,3,192,192]{4,3,2,1,0:T(8,128)(2,1)}, u32[]{:S(2)}) copy-start(bf16[3,3,3,192,192]{4,3,2,1,0:T(8,128)(2,1)} %w2_ref.3) | copy-start | bytes 5971972
  6.2 7.2 %copy-start.6 = (f32[192]{0:T(256)S(1)}, f32[192]{0:T(256)}, u32[]{:S(2)}) copy-start(f32[192]{0:T(256)} %param.15) | copy-start | bytes 2308
  6.2 7.1 %collective-permute-start.4 = (bf16[2,8,8,384]{3,2,1,0:T(8,128)(2,1)S(1)}, bf16[2,8,8,384]{3,2,1,0:T(8,128)(2,1)S(1)}, u32[]{:S(2)}, u32[]{:S(2)}) collective-permute-start(bf16[2,8,8,384]{3,2,1,0:T(8,128)(2,1)S(1)} %get-tuple-element.30), channel_id=1, source_target_pairs={{1,2},{2,1},{9,10},{10,9},{3,4},{4,3},{11,12},{12,11},{5,6},{6,5},... | collective-permute-start | bytes 294920 | tf_op jit(solution)/shard_map/ppermute | solution.py:436
  7.0 8.8 %collective-permute-start.3 = (bf16[13,8,384]{2,1,0:T(8,128)(2,1)S(1)}, bf16[13,8,384]{2,1,0:T(8,128)(2,1)S(1)}, u32[]{:S(2)}, u32[]{:S(2)}) collective-permute-start(bf16[13,8,384]{2,1,0:T(8,128)(2,1)S(1)} %get-tuple-element.28), channel_id=1, source_target_pairs={{1,10},{2,9},{3,12},{4,11},{5,14},{6,13},{17,26},{18,25},{19,28},{... | collective-permute-start | bytes 239624 | tf_op jit(solution)/shard_map/ppermute | solution.py:437
  9.7 6.1 %collective-permute-start.2 = (bf16[12,8,384]{2,1,0:T(8,128)(2,1)S(1)}, bf16[12,8,384]{2,1,0:T(8,128)(2,1)S(1)}, u32[]{:S(2)}, u32[]{:S(2)}) collective-permute-start(bf16[12,8,384]{2,1,0:T(8,128)(2,1)S(1)} %shard_map.85), channel_id=1, source_target_pairs={{0,1},{1,0},{2,3},{3,2},{4,5},{5,4},{6,7},{7,6},{8,9},{9,8},{10,11... | collective-permute-start | bytes 221192 | tf_op jit(solution)/shard_map/ppermute | solution.py:459
  17.7 1.4 %collective-permute-start.5 = (bf16[8,4,8,192]{3,2,1,0:T(8,128)(2,1)S(1)}, bf16[8,4,8,192]{3,2,1,0:T(8,128)(2,1)S(1)}, u32[]{:S(2)}, u32[]{:S(2)}) collective-permute-start(bf16[8,4,8,192]{3,2,1,0:T(8,128)(2,1)S(1)} %get-tuple-element.36), channel_id=1, source_target_pairs={{0,1},{1,0},{2,3},{3,2},{4,5},{5,4},{6,7},{7,6},{8,9},{9,8},{10,11... | collective-permute-start | bytes 294920 | tf_op jit(solution)/shard_map/ppermute | solution.py:487
where the time goes:
time: 20 us; the launch traced here: 19.9 us
  starting transfers between devices  10.2 us (51%)
  Pallas kernels  7.1 us (36%)
  waiting for transfers between devices  1.32 us (7%)
  between operations  0.84 us (4%)
  local copies, waits for them, and re-layouts  0.34 us (2%)
    ppermute x1, starting transfers between devices, shards(): tail_mine = lax.ppermute(tail, axes, straight)  4.41 us
    ppermute x1, starting transfers between devices, shards(): tail_other = lax.ppermute(rest, 'wa', swap)  3.62 us
    pallas_call x1, Pallas kernels, shards(): pl.pallas_call(edge_kernel, out_shape=(shape(3, 2, 2, width, LANES), shap...  2.44 us
    pallas_call x1, Pallas kernels, shards(): pl.pallas_call(early_kernel, out_shape=(shape(frames, half, side, channel...  1.93 us
    pallas_call x1, Pallas kernels, shards(): pl.pallas_call(own_kernel, out_shape=(shape(3, frames, half + 2, width, L...  1.82 us
    ppermute x1, waiting for transfers between devices, shards(): got = lax.ppermute(send, 'wa', swap)  1.31 us
    ppermute x1, starting transfers between devices, shards(): own_edge = lax.ppermute(own_edge, axes, across)  0.8 us
    ppermute x1, starting transfers between devices, shards(): tail_edge = lax.ppermute(tail_edge, axes, diagonal)  0.8 us
  transfers between devices with their start and end apart: 6, of which 1 were waited for; matrix products, arithmetic and copies ran while one was open for 0% of the time, Pallas kernels for 22%

commit v1 on v0

--- a/solution.py
+++ b/solution.py
@@ -114,17 +114,17 @@
     return jnp.stack([part.astype(jnp.bfloat16) for part in parts])
 
 
-def convolved(operand, weights_ref, bias_ref, frame, frames, rows, then):
+def convolved(operand, refs, bias_ref, frame, frames, rows, then):
     products = -(-frames * rows * operand.shape[3] // PRODUCT)
     step = -(-frames // products)
     for start in range(0, frames, step):
         count = min(step, frames - start)
-        then(start, count, convolved_part(operand, weights_ref, bias_ref, frame + start, count, rows))
-
-
-def convolved_part(operand, weights_ref, bias_ref, frame, frames, rows):
+        then(start, count, convolved_part(operand, refs, bias_ref, frame + start, count, rows))
+
+
+def convolved_part(operand, refs, bias_ref, frame, frames, rows):
     width = operand.shape[3]
-    channels = weights_ref.shape[-1]
+    channels = bias_ref.shape[-1]
     taps = [(a, i) for a in range(TAPS) for i in range(TAPS)]
     groups = [taps[start:start + 2] for start in range(0, len(taps), 2)]
 
@@ -142,14 +142,17 @@
         return jnp.concatenate(pieces, axis=-1)
 
     def weights(groups, j, depth):
-        rights = []
-        for group in groups:
-            held = [weights_ref[a, i, j] for a, i in group]
-            rights += [weight[:LANES] for weight in held] + [weight[LANES:] for weight in held]
-        rest = depth - sum(right.shape[0] for right in rights)
-        if rest:
-            rights.append(jnp.zeros((rest, channels), jnp.bfloat16))
-        return jnp.concatenate(rights, axis=0)
+        sides = []
+        for ref in refs:
+            rights = []
+            for group in groups:
+                held = [ref[a, i, j] for a, i in group]
+                rights += [weight[:LANES] for weight in held] + [weight[LANES:] for weight in held]
+            rest = depth - sum(right.shape[0] for right in rights)
+            if rest:
+                rights.append(jnp.zeros((rest, ref.shape[-1]), jnp.bfloat16))
+            sides.append(jnp.concatenate(rights, axis=0))
+        return sides[0] if len(sides) == 1 else jnp.concatenate(sides, axis=1)
 
     half = len(groups) // 2
     parts = [(part, operands(part)) for part in (groups[:half], groups[half:])]
@@ -223,14 +226,14 @@
                     target(first + frame, 2 * k + row, kept.astype(jnp.bfloat16))
 
 
-def hide(operand, weights_ref, bias_ref, gain_ref, first, count, rows, flags, store):
-    channels = weights_ref.shape[-1]
+def hide(operand, refs, bias_ref, gain_ref, first, count, rows, flags, store):
+    channels = bias_ref.shape[-1]
 
     def then(begin, part, hidden):
         flag = jnp.concatenate(flags[begin:begin + part], axis=0)
         store(begin, begin + part, second_rows(hidden, flag, gain_ref, channels))
 
-    convolved(operand, weights_ref, bias_ref, first, count, rows, then)
+    convolved(operand, refs, bias_ref, first, count, rows, then)
 
 
 def inside_flags(rows):
@@ -248,8 +251,17 @@
 
 
 def own_kernel(
-    marks_ref, mine_ref, other_ref, gain1_ref, w1_ref, bias1_ref, gain2_ref, first_ref, late_ref
+    marks_ref, mine_ref, other_ref, gain1_ref, w1_ref, bias1_ref, gain2_ref, w2_hbm,
+    first_ref, late_ref, low1_ref, high1_ref, low2_ref, high2_ref, arrived,
 ):
+    fetches = []
+    for source, low, high in ((w2_hbm, low2_ref, high2_ref), (w1_ref, low1_ref, high1_ref)):
+        for target, lanes in ((low, pl.ds(0, LANES)), (high, pl.ds(LANES, source.shape[-1] - LANES))):
+            fetches.append(
+                pltpu.make_async_copy(source.at[:, :, :, :, lanes], target, arrived.at[len(fetches)])
+            )
+    for fetch in fetches:
+        fetch.start()
     frames, pairs, side, packed = mine_ref.shape
     other = other_ref[CACHE * pairs:].reshape(frames, pairs, side, packed)
     fill_rows(first_ref, 0, 0, mine_ref[...], other, gain1_ref)
@@ -258,12 +270,14 @@
     def store(begin, end, rows):
         late_ref[:, begin:end] = rows
 
-    hide(first_ref, w1_ref, bias1_ref, gain2_ref, 0, frames - 2, 2 * pairs - 2, live, store)
+    hide(first_ref, [w1_ref], bias1_ref, gain2_ref, 0, frames - 2, 2 * pairs - 2, live, store)
+    for fetch in fetches:
+        fetch.wait()
 
 
 def edge_kernel(
     marks_ref, mine_ref, other_ref, edge_ref, first_ref, late_ref,
-    gain1_ref, w1_ref, bias1_ref, gain2_ref, w2_ref, bias2_ref,
+    low1_ref, high1_ref, low2_ref, high2_ref, gain1_ref, bias1_ref, gain2_ref, bias2_ref,
     strip_ref, hidden_ref, keep_ref, send_ref, strip, operand,
 ):
     core = lax.axis_index("wa")
@@ -277,7 +291,7 @@
     def store(begin, end, values):
         operand[:, begin:end, pl.ds((rows - 2) * core, 2)] = values
 
-    hide(strip, w1_ref, bias1_ref, gain2_ref, 0, frames - 2, 2, [flag * inside for flag in live[2:]], store)
+    hide(strip, [low1_ref, high1_ref], bias1_ref, gain2_ref, 0, frames - 2, 2, [flag * inside for flag in live[2:]], store)
     operand[:, :, pl.ds(2 * (1 - core), rows - 2)] = late_ref[...]
     strip_ref[...] = strip[:, 0:2, pl.ds(2 * core, 2)]
     hidden_ref[...] = operand[:, 0:2]
@@ -292,12 +306,13 @@
             mine_ref, other_ref, live, CACHE + start, (core, pairs - 1), result, (put(keep_ref), put(send_ref))
         )
 
-    convolved(operand, w2_ref, bias2_ref, 0, frames - CACHE, rows - 2, then)
+    convolved(operand, [low2_ref, high2_ref], bias2_ref, 0, frames - CACHE, rows - 2, then)
 
 
 def early_kernel(
     marks_ref, tail_mine_ref, tail_other_ref, mine_ref, other_ref, edge_ref, first_ref, strip_ref, hidden_ref,
-    late_keep_ref, late_send_ref, gain1_ref, w1_ref, bias1_ref, gain2_ref, w2_ref, bias2_ref,
+    late_keep_ref, late_send_ref,
+    low1_ref, high1_ref, low2_ref, high2_ref, gain1_ref, bias1_ref, gain2_ref, bias2_ref,
     keep_ref, send_ref, plane, operand,
 ):
     core = lax.axis_index("wa")
@@ -321,7 +336,7 @@
             operand[:, first + begin:first + end] = values
 
         flags = [flag * inside for flag in flags]
-        hide(plane, w1_ref, bias1_ref, gain2_ref, first, CACHE - first, rows, flags, store)
+        hide(plane, [low1_ref, high1_ref], bias1_ref, gain2_ref, first, CACHE - first, rows, flags, store)
 
     @pl.when(earlier)
     def _():
@@ -345,7 +360,7 @@
     def then(start, part, result):
         finish(mine_ref, other_ref, live, start, (core, held - 1), result, (put(keep_ref), put(send_ref)))
 
-    convolved(operand, w2_ref, bias2_ref, 0, CACHE, rows - 2, then)
+    convolved(operand, [low2_ref, high2_ref], bias2_ref, 0, CACHE, rows - 2, then)
     keep_ref[CACHE:] = late_keep_ref[...]
     send_ref[CACHE:] = late_send_ref[...]
 
@@ -436,18 +451,24 @@
     own_edge = lax.ppermute(own_edge, axes, across)
     tail_edge = lax.ppermute(tail_edge, axes, diagonal)
 
-    weights = (
-        gain_first.reshape(1, channels), conv_first, bias_first.reshape(1, channels),
-        gain_second.reshape(1, channels), conv_second, bias_second.reshape(1, channels),
+    gain1, gain2 = gain_first.reshape(1, channels), gain_second.reshape(1, channels)
+    bias1, bias2 = bias_first.reshape(1, channels), bias_second.reshape(1, channels)
+    low, high = shape(*conv_first.shape[:-1], LANES), shape(*conv_first.shape[:-1], channels - LANES)
+    first, late, *cut = pl.pallas_call(
+        own_kernel,
+        out_shape=(
+            shape(3, frames, half + 2, width, LANES), shape(3, frames - 2, half, width, LANES), low, high, low, high
+        ),
+        in_specs=[vmem] * 7 + [pl.BlockSpec(memory_space=pltpu.HBM)],
+        out_specs=(vmem,) * 6,
+        scratch_shapes=[pltpu.SemaphoreType.DMA((4,))],
+        compiler_params=limit,
+        cost_estimate=cost(work * (frames - 2) * half, 4 * 2**20),
+    )(
+        marks, mine, other, gain1, conv_first, bias1, gain2,
+        pltpu.with_memory_space_constraint(conv_second, pltpu.HBM),
     )
-    first, late = pl.pallas_call(
-        own_kernel,
-        out_shape=(shape(3, frames, half + 2, width, LANES), shape(3, frames - 2, half, width, LANES)),
-        in_specs=[vmem] * 7,
-        out_specs=(vmem,) * 2,
-        compiler_params=limit,
-        cost_estimate=cost(work * (frames - 2) * half, 4 * 2**20),
-    )(marks, mine, other, *weights[:4])
+    weights = (*cut, gain1, bias1, gain2, bias2)
     rest = pl.pallas_call(
         other_rows_kernel,
         out_shape=shape(tiles, side, packed),
@@ -463,7 +484,7 @@
             shape(3, 2, 2, width, LANES), shape(3, 2, half + 2, width, LANES),
             shape(frames - CACHE, half, side, channels), shape(frames - CACHE, half, side, channels),
         ),
-        in_specs=[vmem] * 12,
+        in_specs=[vmem] * 14,
         out_specs=(vmem,) * 4,
         scratch_shapes=[
             pltpu.VMEM((3, frames, 4, width, LANES), bf16),
@@ -475,7 +496,7 @@
     keep, send = pl.pallas_call(
         early_kernel,
         out_shape=(shape(frames, half, side, channels), shape(frames, half, side, channels)),
-        in_specs=[vmem] * 17,
+        in_specs=[vmem] * 19,
         out_specs=(vmem, vmem),
         scratch_shapes=[
             pltpu.VMEM((3, CACHE + 2, half + 4, width, LANES), bf16),

time: 20 us -> 20.5 us (1.025)
  Pallas kernels: 7.1 us -> 7.7 us
  starting transfers between devices: 10.2 us -> 9.97 us
    pallas_call x1, Pallas kernels: 1.82 us -> 2.32 us  [shards(): pl.pallas_call(own_kernel, out_shape=(shape(3, frames, half + 2, width, L...]
    unnamed x14 -> x12, local copies, waits for them, and re-layouts: 0.34 us -> 0.49 us
  transfers between devices with their start and end apart: 6 -> 6, of which waited for: 1 -> 1; matrix products, arithmetic and copies ran while one was open for 0% -> 0% of each run, Pallas kernels for 22% -> 24%
where the time goes in v1:
time: 20.5 us; the launch traced here: 20.3 us
  starting transfers between devices  9.97 us (49%)
  Pallas kernels  7.7 us (38%)
  waiting for transfers between devices  1.32 us (6%)
  between operations  0.84 us (4%)
  local copies, waits for them, and re-layouts  0.49 us (2%)
    ppermute x1, starting transfers between devices, shards(): tail_mine = lax.ppermute(tail, axes, straight)  4.41 us
    ppermute x1, starting transfers between devices, shards(): tail_other = lax.ppermute(rest, 'wa', swap)  3.47 us
    pallas_call x1, Pallas kernels, shards(): pl.pallas_call(edge_kernel, out_shape=(shape(3, 2, 2, width, LANES), shap...  2.47 us
    pallas_call x1, Pallas kernels, shards(): pl.pallas_call(own_kernel, out_shape=(shape(3, frames, half + 2, width, L...  2.32 us
    pallas_call x1, Pallas kernels, shards(): pl.pallas_call(early_kernel, out_shape=(shape(frames, half, side, channel...  2 us
    ppermute x1, waiting for transfers between devices, shards(): got = lax.ppermute(send, 'wa', swap)  1.31 us
    ppermute x1, starting transfers between devices, shards(): own_edge = lax.ppermute(own_edge, axes, across)  0.8 us
    pallas_call x1, Pallas kernels, shards(): pl.pallas_call(place_kernel, out_shape=shape(*features.shape), in_specs=[...  0.71 us
  transfers between devices with their start and end apart: 6, of which 1 were waited for; matrix products, arithmetic and copies ran while one was open for 0% of the time, Pallas kernels for 24%

profile of v1, /device:TPU:0, one launch (start us, length us, event | category | flops | bytes accessed | tf_op | source)
XLA Modules:
  0.0 20.3 jit_solution(17307443094745148650)
XLA Ops:
  0.0 0.0 copy-start.1
  0.7 0.3 %copy-done.1 = bf16[8,8,8,192]{3,2,1,0:T(8,128)(2,1)S(1)} copy-done((bf16[8,8,8,192]{3,2,1,0:T(8,128)(2,1)S(1)}, bf16[8,8,8,192]{3,2,1,0:T(8,128)(2,1)}, u32[]{:S(2)}) %copy-start.1) | copy-done | bytes 196632
  1.0 0.1 shard_map.83
  1.1 0.5 %collective-permute-start.1 = (bf16[36,8,384]{2,1,0:T(8,128)(2,1)S(1)}, bf16[36,8,384]{2,1,0:T(8,128)(2,1)S(1)}, u32[]{:S(2)}, u32[]{:S(2)}) collective-permute-start(bf16[36,8,384]{2,1,0:T(8,128)(2,1)S(1)} %get-tuple-element.30), channel_id=1, source_target_pairs={{0,1},{1,0},{2,3},{3,2},{4,5},{5,4},{6,7},{7,6},{8,9},{9,8},{10,11... | collective-permute-start | bytes 663560 | tf_op jit(solution)/shard_map/ppermute | solution.py:442
  1.6 4.4 %collective-permute-start = (bf16[17,8,384]{2,1,0:T(8,128)(2,1)S(1)}, bf16[17,8,384]{2,1,0:T(8,128)(2,1)S(1)}, u32[]{:S(2)}, u32[]{:S(2)}) collective-permute-start(bf16[17,8,384]{2,1,0:T(8,128)(2,1)S(1)} %get-tuple-element.28.tail_ref), channel_id=1, source_target_pairs={{0,8},{1,9},{2,10},{3,11},{4,12},{5,13},{6,14},{7,15},{16,24},{17,... | collective-permute-start | bytes 313352 | tf_op jit(solution)/shard_map/ppermute | solution.py:441
  6.1 0.0 collective-permute-done.1.other_ref
  6.1 0.0 copy-start
  6.1 0.0 copy-start.2
  6.1 0.0 copy-start.3
  6.1 0.0 copy-start.4
  6.1 0.8 %collective-permute-start.4 = (bf16[2,8,8,384]{3,2,1,0:T(8,128)(2,1)S(1)}, bf16[2,8,8,384]{3,2,1,0:T(8,128)(2,1)S(1)}, u32[]{:S(2)}, u32[]{:S(2)}) collective-permute-start(bf16[2,8,8,384]{3,2,1,0:T(8,128)(2,1)S(1)} %get-tuple-element.34), channel_id=1, source_target_pairs={{1,2},{2,1},{9,10},{10,9},{3,4},{4,3},{11,12},{12,11},{5,6},{6,5},... | collective-permute-start | bytes 294920 | tf_op jit(solution)/shard_map/ppermute | solution.py:451
  7.0 0.7 %collective-permute-start.3 = (bf16[13,8,384]{2,1,0:T(8,128)(2,1)S(1)}, bf16[13,8,384]{2,1,0:T(8,128)(2,1)S(1)}, u32[]{:S(2)}, u32[]{:S(2)}) collective-permute-start(bf16[13,8,384]{2,1,0:T(8,128)(2,1)S(1)} %get-tuple-element.32), channel_id=1, source_target_pairs={{1,10},{2,9},{3,12},{4,11},{5,14},{6,13},{17,26},{18,25},{19,28},{... | collective-permute-start | bytes 239624 | tf_op jit(solution)/shard_map/ppermute | solution.py:452
  7.6 0.2 copy-done
  7.8 0.0 copy-done.2
  7.8 0.0 copy-done.3
  7.8 0.0 copy-done.4
  7.8 0.0 copy-start.5
  7.8 2.3 %shard_map.84 = (bf16[3,8,6,16,128]{4,3,2,1,0:T(8,128)(2,1)S(1)}, bf16[3,6,4,16,128]{4,3,2,1,0:T(8,128)(2,1)S(1)}, bf16[3,3,3,192,128]{4,3,2,1,0:T(8,128)(2,1)S(...) custom-call(bf16[8,384]{1,0:T(8,128)(2,1)S(1)} %get-tuple-element.27, ...), custom_call_target="tpu_custom_call" | custom-call | flops 764411904 | bytes 4194304 | tf_op jit(solution)/shard_map/pallas_call | solution.py:457
  10.2 0.0 collective-permute-done.tail_ref.tail_mine_ref
  10.2 3.5 %collective-permute-start.2 = (bf16[12,8,384]{2,1,0:T(8,128)(2,1)S(1)}, bf16[12,8,384]{2,1,0:T(8,128)(2,1)S(1)}, u32[]{:S(2)}, u32[]{:S(2)}) collective-permute-start(bf16[12,8,384]{2,1,0:T(8,128)(2,1)S(1)} %shard_map.85), channel_id=1, source_target_pairs={{0,1},{1,0},{2,3},{3,2},{4,5},{5,4},{6,7},{7,6},{8,9},{9,8},{10,11... | collective-permute-start | bytes 221192 | tf_op jit(solution)/shard_map/ppermute | solution.py:480
  13.7 0.0 collective-permute-done.4.edge_ref
  13.7 0.0 copy-done.5
  13.7 2.5 %shard_map.87 = (bf16[3,2,2,16,128]{4,3,2,1,0:T(8,128)(2,1)S(1)}, bf16[3,2,6,16,128]{4,3,2,1,0:T(8,128)(2,1)S(1)}, bf16[4,4,8,192]{3,2,1,0:T(8,128)(2,1)S(1)}, bf16[4,4,8,192]{3,2,1,0:T(8,128)(2,1)S(1)}) custom-call(bf16[8,384]{1,0:T(8,128)(2,1)S(1)} %get-tuple-element.27.marks_ref, bf16[8,3,8,384]{3,2,1,0:T(8,128)(2,1)S(1)} %get-tuple-element.29.mine_ref, ...), custom_call_target="tpu_custom_call" | custom-call | flops 1048576 | bytes 1048576 | tf_op jit(solution)/shard_map/pallas_call | solution.py:481
  16.2 0.0 collective-permute-done.2.tail_other_ref
  16.2 0.0 collective-permute-done.3.edge_ref
  16.2 2.0 %shard_map.88 = (bf16[8,4,8,192]{3,2,1,0:T(8,128)(2,1)S(1)}, bf16[8,4,8,192]{3,2,1,0:T(8,128)(2,1)S(1)}) custom-call(bf16[8,384]{1,0:T(8,128)(2,1)S(1)} %get-tuple-element.27.marks_ref, bf16[17,8,384]{2,1,0:T(8,128)(2,1)S(1)} %collective-permute-done.tail_ref.tail_mine_ref, bf16[12,8,384]{2,1,0:T(8,128)(2,1)S(1)} %collective-permute-done.2.tail_other_ref, ...), custom_call_target="tpu_custom_call" | custom-call | flops 1274019840 | bytes 8388608 | tf_op jit(solution)/shard_map/pallas_call | solution.py:496
  18.2 0.1 collective-permute-start.5
  18.3 1.3 %collective-permute-done.5.got_ref = bf16[8,4,8,192]{3,2,1,0:T(8,128)(2,1)S(1)} collective-permute-done((bf16[8,4,8,192]{3,2,1,0:T(8,128)(2,1)S(1)}, bf16[8,4,8,192]{3,2,1,0:T(8,128)(2,1)S(1)}, u32[]{:S(2)}, u32[]{:S(2)}) %collective-permute-start.5) | collective-permute-done | bytes 98336 | tf_op jit(solution)/shard_map/ppermute | solution.py:508
  19.6 0.7 %shard_map.89 = bf16[8,8,8,192]{3,2,1,0:T(8,128)(2,1)} custom-call(bf16[8,4,8,192]{3,2,1,0:T(8,128)(2,1)S(1)} %get-tuple-element.43.keep_ref, bf16[8,4,8,192]{3,2,1,0:T(8,128)(2,1)S(1)} %collective-permute-done.5.got_ref), custom_call_target="tpu_custom_call" | custom-call | tf_op jit(solution)/shard_map/pallas_call | solution.py:509
  (3 shorter events, 0.0 us)
Async XLA Ops:
  0.0 1.0 %copy-start.1 = (bf16[8,8,8,192]{3,2,1,0:T(8,128)(2,1)S(1)}, bf16[8,8,8,192]{3,2,1,0:T(8,128)(2,1)}, u32[]{:S(2)}) copy-start(bf16[8,8,8,192]{3,2,1,0:T(8,128)(2,1)} %raw.1) | copy-start | bytes 589828
  1.1 4.9 %collective-permute-start.1 = (bf16[36,8,384]{2,1,0:T(8,128)(2,1)S(1)}, bf16[36,8,384]{2,1,0:T(8,128)(2,1)S(1)}, u32[]{:S(2)}, u32[]{:S(2)}) collective-permute-start(bf16[36,8,384]{2,1,0:T(8,128)(2,1)S(1)} %get-tuple-element.30), channel_id=1, source_target_pairs={{0,1},{1,0},{2,3},{3,2},{4,5},{5,4},{6,7},{7,6},{8,9},{9,8},{10,11... | collective-permute-start | bytes 663560 | tf_op jit(solution)/shard_map/ppermute | solution.py:442
  1.6 8.5 %collective-permute-start = (bf16[17,8,384]{2,1,0:T(8,128)(2,1)S(1)}, bf16[17,8,384]{2,1,0:T(8,128)(2,1)S(1)}, u32[]{:S(2)}, u32[]{:S(2)}) collective-permute-start(bf16[17,8,384]{2,1,0:T(8,128)(2,1)S(1)} %get-tuple-element.28.tail_ref), channel_id=1, source_target_pairs={{0,8},{1,9},{2,10},{3,11},{4,12},{5,13},{6,14},{7,15},{16,24},{17,... | collective-permute-start | bytes 313352 | tf_op jit(solution)/shard_map/ppermute | solution.py:441
  6.1 1.8 %copy-start = (bf16[3,3,3,192,192]{4,3,2,1,0:T(8,128)(2,1)S(1)}, bf16[3,3,3,192,192]{4,3,2,1,0:T(8,128)(2,1)}, u32[]{:S(2)}) copy-start(bf16[3,3,3,192,192]{4,3,2,1,0:T(8,128)(2,1)} %w1_ref.1) | copy-start | bytes 5971972
  6.1 1.7 %copy-start.2 = (f32[192]{0:T(256)S(1)}, f32[192]{0:T(256)}, u32[]{:S(2)}) copy-start(f32[192]{0:T(256)} %param.10) | copy-start | bytes 2308
  6.1 1.7 %copy-start.3 = (f32[192]{0:T(256)S(1)}, f32[192]{0:T(256)}, u32[]{:S(2)}) copy-start(f32[192]{0:T(256)} %param.12) | copy-start | bytes 2308
  6.1 1.7 %copy-start.4 = (f32[192]{0:T(256)S(1)}, f32[192]{0:T(256)}, u32[]{:S(2)}) copy-start(f32[192]{0:T(256)} %param.13) | copy-start | bytes 2308
  6.1 7.5 %collective-permute-start.4 = (bf16[2,8,8,384]{3,2,1,0:T(8,128)(2,1)S(1)}, bf16[2,8,8,384]{3,2,1,0:T(8,128)(2,1)S(1)}, u32[]{:S(2)}, u32[]{:S(2)}) collective-permute-start(bf16[2,8,8,384]{3,2,1,0:T(8,128)(2,1)S(1)} %get-tuple-element.34), channel_id=1, source_target_pairs={{1,2},{2,1},{9,10},{10,9},{3,4},{4,3},{11,12},{12,11},{5,6},{6,5},... | collective-permute-start | bytes 294920 | tf_op jit(solution)/shard_map/ppermute | solution.py:451
  7.0 9.2 %collective-permute-start.3 = (bf16[13,8,384]{2,1,0:T(8,128)(2,1)S(1)}, bf16[13,8,384]{2,1,0:T(8,128)(2,1)S(1)}, u32[]{:S(2)}, u32[]{:S(2)}) collective-permute-start(bf16[13,8,384]{2,1,0:T(8,128)(2,1)S(1)} %get-tuple-element.32), channel_id=1, source_target_pairs={{1,10},{2,9},{3,12},{4,11},{5,14},{6,13},{17,26},{18,25},{19,28},{... | collective-permute-start | bytes 239624 | tf_op jit(solution)/shard_map/ppermute | solution.py:452
  7.8 5.8 %copy-start.5 = (f32[192]{0:T(256)S(1)}, f32[192]{0:T(256)}, u32[]{:S(2)}) copy-start(f32[192]{0:T(256)} %param.15) | copy-start | bytes 2308
  10.2 6.0 %collective-permute-start.2 = (bf16[12,8,384]{2,1,0:T(8,128)(2,1)S(1)}, bf16[12,8,384]{2,1,0:T(8,128)(2,1)S(1)}, u32[]{:S(2)}, u32[]{:S(2)}) collective-permute-start(bf16[12,8,384]{2,1,0:T(8,128)(2,1)S(1)} %shard_map.85), channel_id=1, source_target_pairs={{0,1},{1,0},{2,3},{3,2},{4,5},{5,4},{6,7},{7,6},{8,9},{9,8},{10,11... | collective-permute-start | bytes 221192 | tf_op jit(solution)/shard_map/ppermute | solution.py:480
  18.2 1.4 %collective-permute-start.5 = (bf16[8,4,8,192]{3,2,1,0:T(8,128)(2,1)S(1)}, bf16[8,4,8,192]{3,2,1,0:T(8,128)(2,1)S(1)}, u32[]{:S(2)}, u32[]{:S(2)}) collective-permute-start(bf16[8,4,8,192]{3,2,1,0:T(8,128)(2,1)S(1)} %get-tuple-element.44), channel_id=1, source_target_pairs={{0,1},{1,0},{2,3},{3,2},{4,5},{5,4},{6,7},{7,6},{8,9},{9,8},{10,11... | collective-permute-start | bytes 294920 | tf_op jit(solution)/shard_map/ppermute | solution.py:508

commit v2 on v0

--- a/solution.py
+++ b/solution.py
@@ -114,12 +114,28 @@
     return jnp.stack([part.astype(jnp.bfloat16) for part in parts])
 
 
+def in_turn(steps):
+    waiting = None
+    for product, then in steps:
+        result = product()
+        if waiting:
+            waiting[1](waiting[0])
+        waiting = (result, then)
+    waiting[1](waiting[0])
+
+
 def convolved(operand, weights_ref, bias_ref, frame, frames, rows, then):
     products = -(-frames * rows * operand.shape[3] // PRODUCT)
     step = -(-frames // products)
-    for start in range(0, frames, step):
+
+    def part(start):
         count = min(step, frames - start)
-        then(start, count, convolved_part(operand, weights_ref, bias_ref, frame + start, count, rows))
+        return (
+            lambda: convolved_part(operand, weights_ref, bias_ref, frame + start, count, rows),
+            lambda result: then(start, count, result),
+        )
+
+    return [part(start) for start in range(0, frames, step)]
 
 
 def convolved_part(operand, weights_ref, bias_ref, frame, frames, rows):
@@ -230,7 +246,7 @@
         flag = jnp.concatenate(flags[begin:begin + part], axis=0)
         store(begin, begin + part, second_rows(hidden, flag, gain_ref, channels))
 
-    convolved(operand, weights_ref, bias_ref, first, count, rows, then)
+    return convolved(operand, weights_ref, bias_ref, first, count, rows, then)
 
 
 def inside_flags(rows):
@@ -251,14 +267,22 @@
     marks_ref, mine_ref, other_ref, gain1_ref, w1_ref, bias1_ref, gain2_ref, first_ref, late_ref
 ):
     frames, pairs, side, packed = mine_ref.shape
-    other = other_ref[CACHE * pairs:].reshape(frames, pairs, side, packed)
-    fill_rows(first_ref, 0, 0, mine_ref[...], other, gain1_ref)
     live = frame_flags(marks_ref[...], range(2, frames))
+
+    def fill(start, end):
+        other = other_ref[(CACHE + start) * pairs:(CACHE + end) * pairs].reshape(end - start, pairs, side, packed)
+        fill_rows(first_ref, start, 0, mine_ref[start:end], other, gain1_ref)
 
     def store(begin, end, rows):
         late_ref[:, begin:end] = rows
 
-    hide(first_ref, w1_ref, bias1_ref, gain2_ref, 0, frames - 2, 2 * pairs - 2, live, store)
+    steps = hide(first_ref, w1_ref, bias1_ref, gain2_ref, 0, frames - 2, 2 * pairs - 2, live, store)
+    half = -(-(frames - 2) // len(steps)) + 2
+    fill(0, half)
+    product, then = steps[0]
+    held = product()
+    fill(half, frames)
+    in_turn([(lambda: held, then)] + steps[1:])
 
 
 def edge_kernel(
@@ -269,30 +293,39 @@
     core = lax.axis_index("wa")
     frames, pairs = mine_ref.shape[:2]
     rows = 2 * pairs
+    late = frames - CACHE
+    outward, inward = pl.ds(2 * core, 2), pl.ds(2 * (1 - core), 2)
     fill_rows(strip, 0, 2 * core, edge_ref[1][:, None], edge_ref[0][:, None], gain1_ref)
-    strip[:, :, pl.ds(2 * (1 - core), 2)] = first_ref[:, :, pl.ds((rows - 2) * core, 2)]
+    strip[:, :, inward] = first_ref[:, :, pl.ds((rows - 2) * core, 2)]
+    operand[:, :, inward] = late_ref[:, :, pl.ds((rows - 4) * core, 2)]
     live = frame_flags(marks_ref[...], range(frames))
     inside = inside_flags(2)
 
     def store(begin, end, values):
-        operand[:, begin:end, pl.ds((rows - 2) * core, 2)] = values
-
-    hide(strip, w1_ref, bias1_ref, gain2_ref, 0, frames - 2, 2, [flag * inside for flag in live[2:]], store)
-    operand[:, :, pl.ds(2 * (1 - core), rows - 2)] = late_ref[...]
-    strip_ref[...] = strip[:, 0:2, pl.ds(2 * core, 2)]
-    hidden_ref[...] = operand[:, 0:2]
-
-    def put(ref):
-        def store(frame, row, value):
-            ref[frame - CACHE, row] = value
-        return store
-
-    def then(start, part, result):
-        finish(
-            mine_ref, other_ref, live, CACHE + start, (core, pairs - 1), result, (put(keep_ref), put(send_ref))
-        )
-
-    convolved(operand, w2_ref, bias2_ref, 0, frames - CACHE, rows - 2, then)
+        operand[:, begin:end, outward] = values
+
+    def finished(start_row, pair, count):
+        def put(ref):
+            def store(frame, row, value):
+                ref[frame - CACHE, start_row + row] = value
+            return store
+
+        def then(start, part, result):
+            targets = (put(keep_ref), put(send_ref))
+            finish(mine_ref, other_ref, live, CACHE + start, (pair, count), result, targets)
+
+        return then
+
+    flags = [flag * inside for flag in live[2:]]
+    middle, border = finished(2 * (1 - core), 1, pairs - 2), finished((rows - 4) * core, (pairs - 1) * core, 1)
+    in_turn(
+        hide(strip, w1_ref, bias1_ref, gain2_ref, 0, frames - 2, 2, flags, store)
+        + convolved(late_ref, w2_ref, bias2_ref, 0, late, rows - 4, middle)
+        + convolved(operand, w2_ref, bias2_ref, 0, late, 2, border)
+    )
+    strip_ref[...] = strip[:, 0:2, outward]
+    hidden_ref[:, :, pl.ds(2 * (1 - core), rows - 2)] = late_ref[:, 0:2]
+    hidden_ref[:, :, pl.ds((rows - 2) * core, 2)] = operand[:, 0:2, outward]
 
 
 def early_kernel(
@@ -321,7 +354,7 @@
             operand[:, first + begin:first + end] = values
 
         flags = [flag * inside for flag in flags]
-        hide(plane, w1_ref, bias1_ref, gain2_ref, first, CACHE - first, rows, flags, store)
+        in_turn(hide(plane, w1_ref, bias1_ref, gain2_ref, first, CACHE - first, rows, flags, store))
 
     @pl.when(earlier)
     def _():
@@ -345,7 +378,7 @@
     def then(start, part, result):
         finish(mine_ref, other_ref, live, start, (core, held - 1), result, (put(keep_ref), put(send_ref)))
 
-    convolved(operand, w2_ref, bias2_ref, 0, CACHE, rows - 2, then)
+    in_turn(convolved(operand, w2_ref, bias2_ref, 0, CACHE, rows - 2, then))
     keep_ref[CACHE:] = late_keep_ref[...]
     send_ref[CACHE:] = late_send_ref[...]
 
@@ -467,7 +500,7 @@
         out_specs=(vmem,) * 4,
         scratch_shapes=[
             pltpu.VMEM((3, frames, 4, width, LANES), bf16),
-            pltpu.VMEM((3, frames - 2, half + 2, width, LANES), bf16),
+            pltpu.VMEM((3, frames - 2, 4, width, LANES), bf16),
         ],
         compiler_params=limit,
         cost_estimate=cost(2**20, 2**20),

time: 20 us -> 19.6 us (0.980)
  Pallas kernels: 7.1 us -> 6.68 us
    pallas_call x1, Pallas kernels: 2.44 us -> 2 us  [shards(): pl.pallas_call(edge_kernel, out_shape=(shape(3, 2, 2, width, LANES), shap...]
  transfers between devices with their start and end apart: 6 -> 6, of which waited for: 1 -> 1; matrix products, arithmetic and copies ran while one was open for 0% -> 0% of each run, Pallas kernels for 22% -> 20%
where the time goes in v2:
time: 19.6 us; the launch traced here: 19.4 us
  starting transfers between devices  10.3 us (53%)
  Pallas kernels  6.68 us (34%)
  waiting for transfers between devices  1.32 us (7%)
  between operations  0.84 us (4%)
  local copies, waits for them, and re-layouts  0.34 us (2%)
    ppermute x1, starting transfers between devices, shards(): tail_mine = lax.ppermute(tail, axes, straight)  4.41 us
    ppermute x1, starting transfers between devices, shards(): tail_other = lax.ppermute(rest, 'wa', swap)  3.62 us
    pallas_call x1, Pallas kernels, shards(): pl.pallas_call(edge_kernel, out_shape=(shape(3, 2, 2, width, LANES), shap...  2 us
    pallas_call x1, Pallas kernels, shards(): pl.pallas_call(early_kernel, out_shape=(shape(frames, half, side, channel...  1.93 us
    pallas_call x1, Pallas kernels, shards(): pl.pallas_call(own_kernel, out_shape=(shape(3, frames, half + 2, width, L...  1.84 us
    ppermute x1, waiting for transfers between devices, shards(): got = lax.ppermute(send, 'wa', swap)  1.3 us
    ppermute x1, starting transfers between devices, shards(): own_edge = lax.ppermute(own_edge, axes, across)  0.8 us
    ppermute x1, starting transfers between devices, shards(): tail_edge = lax.ppermute(tail_edge, axes, diagonal)  0.8 us
  transfers between devices with their start and end apart: 6, of which 1 were waited for; matrix products, arithmetic and copies ran while one was open for 0% of the time, Pallas kernels for 20%

profile of v2, /device:TPU:0, one launch (start us, length us, event | category | flops | bytes accessed | tf_op | source)
XLA Modules:
  0.0 19.4 jit_solution(7268852423992875713)
XLA Ops:
  0.0 0.0 copy-start.2
  0.7 0.3 %copy-done.2 = bf16[8,8,8,192]{3,2,1,0:T(8,128)(2,1)S(1)} copy-done((bf16[8,8,8,192]{3,2,1,0:T(8,128)(2,1)S(1)}, bf16[8,8,8,192]{3,2,1,0:T(8,128)(2,1)}, u32[]{:S(2)}) %copy-start.2) | copy-done | bytes 196632
  1.0 0.1 shard_map.83
  1.1 0.5 %collective-permute-start.1 = (bf16[36,8,384]{2,1,0:T(8,128)(2,1)S(1)}, bf16[36,8,384]{2,1,0:T(8,128)(2,1)S(1)}, u32[]{:S(2)}, u32[]{:S(2)}) collective-permute-start(bf16[36,8,384]{2,1,0:T(8,128)(2,1)S(1)} %get-tuple-element.26), channel_id=1, source_target_pairs={{0,1},{1,0},{2,3},{3,2},{4,5},{5,4},{6,7},{7,6},{8,9},{9,8},{10,11... | collective-permute-start | bytes 663560 | tf_op jit(solution)/shard_map/ppermute | solution.py:460
  1.6 4.4 %collective-permute-start = (bf16[17,8,384]{2,1,0:T(8,128)(2,1)S(1)}, bf16[17,8,384]{2,1,0:T(8,128)(2,1)S(1)}, u32[]{:S(2)}, u32[]{:S(2)}) collective-permute-start(bf16[17,8,384]{2,1,0:T(8,128)(2,1)S(1)} %get-tuple-element.24.tail_ref), channel_id=1, source_target_pairs={{0,8},{1,9},{2,10},{3,11},{4,12},{5,13},{6,14},{7,15},{16,24},{17,... | collective-permute-start | bytes 313352 | tf_op jit(solution)/shard_map/ppermute | solution.py:459
  6.1 0.0 collective-permute-done.1.other_ref
  6.1 0.0 copy-start
  6.1 0.0 copy-start.3
  6.1 0.0 copy-start.4
  6.1 0.0 copy-start.5
  6.1 0.0 copy-start.1
  6.2 0.0 copy-start.6
  6.2 0.8 %collective-permute-start.4 = (bf16[2,8,8,384]{3,2,1,0:T(8,128)(2,1)S(1)}, bf16[2,8,8,384]{3,2,1,0:T(8,128)(2,1)S(1)}, u32[]{:S(2)}, u32[]{:S(2)}) collective-permute-start(bf16[2,8,8,384]{3,2,1,0:T(8,128)(2,1)S(1)} %get-tuple-element.30), channel_id=1, source_target_pairs={{1,2},{2,1},{9,10},{10,9},{3,4},{4,3},{11,12},{12,11},{5,6},{6,5},... | collective-permute-start | bytes 294920 | tf_op jit(solution)/shard_map/ppermute | solution.py:469
  7.0 0.8 %collective-permute-start.3 = (bf16[13,8,384]{2,1,0:T(8,128)(2,1)S(1)}, bf16[13,8,384]{2,1,0:T(8,128)(2,1)S(1)}, u32[]{:S(2)}, u32[]{:S(2)}) collective-permute-start(bf16[13,8,384]{2,1,0:T(8,128)(2,1)S(1)} %get-tuple-element.28), channel_id=1, source_target_pairs={{1,10},{2,9},{3,12},{4,11},{5,14},{6,13},{17,26},{18,25},{19,28},{... | collective-permute-start | bytes 239624 | tf_op jit(solution)/shard_map/ppermute | solution.py:470
  7.8 0.0 copy-done
  7.8 0.0 copy-done.3
  7.8 0.0 copy-done.4
  7.8 0.0 copy-done.5
  7.8 1.8 %shard_map.84 = (bf16[3,8,6,16,128]{4,3,2,1,0:T(8,128)(2,1)S(1)}, bf16[3,6,4,16,128]{4,3,2,1,0:T(8,128)(2,1)S(1)}) custom-call(bf16[8,384]{1,0:T(8,128)(2,1)S(1)} %get-tuple-element.23.marks_ref, bf16[8,3,8,384]{3,2,1,0:T(8,128)(2,1)S(1)} %get-tuple-element.25.mine_ref, bf16[36,8,384]{2,1,0:T(8,128)(2,1)S(1)} %collective-permute-done.1.other_ref, ...), custom_call_target="tpu_custom_call" | custom-call | flops 764411904 | bytes 4194304 | tf_op jit(solution)/shard_map/pallas_call | solution.py:476
  9.7 0.0 collective-permute-done.tail_ref.tail_mine_ref
  9.7 3.6 %collective-permute-start.2 = (bf16[12,8,384]{2,1,0:T(8,128)(2,1)S(1)}, bf16[12,8,384]{2,1,0:T(8,128)(2,1)S(1)}, u32[]{:S(2)}, u32[]{:S(2)}) collective-permute-start(bf16[12,8,384]{2,1,0:T(8,128)(2,1)S(1)} %shard_map.85), channel_id=1, source_target_pairs={{0,1},{1,0},{2,3},{3,2},{4,5},{5,4},{6,7},{7,6},{8,9},{9,8},{10,11... | collective-permute-start | bytes 221192 | tf_op jit(solution)/shard_map/ppermute | solution.py:492
  13.3 0.0 collective-permute-done.4.edge_ref
  13.3 0.0 copy-done.1
  13.3 0.0 copy-done.6
  13.3 2.0 %shard_map.87 = (bf16[3,2,2,16,128]{4,3,2,1,0:T(8,128)(2,1)S(1)}, bf16[3,2,6,16,128]{4,3,2,1,0:T(8,128)(2,1)S(1)}, bf16[4,4,8,192]{3,2,1,0:T(8,128)(2,1)S(1)}, bf16[4,4,8,192]{3,2,1,0:T(8,128)(2,1)S(1)}) custom-call(bf16[8,384]{1,0:T(8,128)(2,1)S(1)} %get-tuple-element.23.marks_ref, bf16[8,3,8,384]{3,2,1,0:T(8,128)(2,1)S(1)} %get-tuple-element.25.mine_ref, ...), custom_call_target="tpu_custom_call" | custom-call | flops 1048576 | bytes 1048576 | tf_op jit(solution)/shard_map/pallas_call | solution.py:493
  15.3 0.0 collective-permute-done.2.tail_other_ref
  15.3 0.0 collective-permute-done.3.edge_ref
  15.4 1.9 %shard_map.88 = (bf16[8,4,8,192]{3,2,1,0:T(8,128)(2,1)S(1)}, bf16[8,4,8,192]{3,2,1,0:T(8,128)(2,1)S(1)}) custom-call(bf16[8,384]{1,0:T(8,128)(2,1)S(1)} %get-tuple-element.23.marks_ref, bf16[17,8,384]{2,1,0:T(8,128)(2,1)S(1)} %collective-permute-done.tail_ref.tail_mine_ref, bf16[12,8,384]{2,1,0:T(8,128)(2,1)S(1)} %collective-permute-done.2.tail_other_ref, ...), custom_call_target="tpu_custom_call" | custom-call | flops 1274019840 | bytes 8388608 | tf_op jit(solution)/shard_map/pallas_call | solution.py:508
  17.3 0.1 collective-permute-start.5
  17.4 1.3 %collective-permute-done.5.got_ref = bf16[8,4,8,192]{3,2,1,0:T(8,128)(2,1)S(1)} collective-permute-done((bf16[8,4,8,192]{3,2,1,0:T(8,128)(2,1)S(1)}, bf16[8,4,8,192]{3,2,1,0:T(8,128)(2,1)S(1)}, u32[]{:S(2)}, u32[]{:S(2)}) %collective-permute-start.5) | collective-permute-done | bytes 98336 | tf_op jit(solution)/shard_map/ppermute | solution.py:520
  18.7 0.7 %shard_map.89 = bf16[8,8,8,192]{3,2,1,0:T(8,128)(2,1)} custom-call(bf16[8,4,8,192]{3,2,1,0:T(8,128)(2,1)S(1)} %get-tuple-element.35.keep_ref, bf16[8,4,8,192]{3,2,1,0:T(8,128)(2,1)S(1)} %collective-permute-done.5.got_ref), custom_call_target="tpu_custom_call" | custom-call | tf_op jit(solution)/shard_map/pallas_call | solution.py:521
  (3 shorter events, 0.0 us)
Async XLA Ops:
  0.0 1.0 %copy-start.2 = (bf16[8,8,8,192]{3,2,1,0:T(8,128)(2,1)S(1)}, bf16[8,8,8,192]{3,2,1,0:T(8,128)(2,1)}, u32[]{:S(2)}) copy-start(bf16[8,8,8,192]{3,2,1,0:T(8,128)(2,1)} %raw.1) | copy-start | bytes 589828
  1.1 4.9 %collective-permute-start.1 = (bf16[36,8,384]{2,1,0:T(8,128)(2,1)S(1)}, bf16[36,8,384]{2,1,0:T(8,128)(2,1)S(1)}, u32[]{:S(2)}, u32[]{:S(2)}) collective-permute-start(bf16[36,8,384]{2,1,0:T(8,128)(2,1)S(1)} %get-tuple-element.26), channel_id=1, source_target_pairs={{0,1},{1,0},{2,3},{3,2},{4,5},{5,4},{6,7},{7,6},{8,9},{9,8},{10,11... | collective-permute-start | bytes 663560 | tf_op jit(solution)/shard_map/ppermute | solution.py:460
  1.6 8.0 %collective-permute-start = (bf16[17,8,384]{2,1,0:T(8,128)(2,1)S(1)}, bf16[17,8,384]{2,1,0:T(8,128)(2,1)S(1)}, u32[]{:S(2)}, u32[]{:S(2)}) collective-permute-start(bf16[17,8,384]{2,1,0:T(8,128)(2,1)S(1)} %get-tuple-element.24.tail_ref), channel_id=1, source_target_pairs={{0,8},{1,9},{2,10},{3,11},{4,12},{5,13},{6,14},{7,15},{16,24},{17,... | collective-permute-start | bytes 313352 | tf_op jit(solution)/shard_map/ppermute | solution.py:459
  6.1 1.8 %copy-start = (bf16[3,3,3,192,192]{4,3,2,1,0:T(8,128)(2,1)S(1)}, bf16[3,3,3,192,192]{4,3,2,1,0:T(8,128)(2,1)}, u32[]{:S(2)}) copy-start(bf16[3,3,3,192,192]{4,3,2,1,0:T(8,128)(2,1)} %w1_ref.5) | copy-start | bytes 5971972
  6.1 1.7 %copy-start.3 = (f32[192]{0:T(256)S(1)}, f32[192]{0:T(256)}, u32[]{:S(2)}) copy-start(f32[192]{0:T(256)} %param.10) | copy-start | bytes 2308
  6.1 1.7 %copy-start.4 = (f32[192]{0:T(256)S(1)}, f32[192]{0:T(256)}, u32[]{:S(2)}) copy-start(f32[192]{0:T(256)} %param.12) | copy-start | bytes 2308
  6.1 1.7 %copy-start.5 = (f32[192]{0:T(256)S(1)}, f32[192]{0:T(256)}, u32[]{:S(2)}) copy-start(f32[192]{0:T(256)} %param.13) | copy-start | bytes 2308
  6.1 7.2 %copy-start.1 = (bf16[3,3,3,192,192]{4,3,2,1,0:T(8,128)(2,1)S(1)}, bf16[3,3,3,192,192]{4,3,2,1,0:T(8,128)(2,1)}, u32[]{:S(2)}) copy-start(bf16[3,3,3,192,192]{4,3,2,1,0:T(8,128)(2,1)} %w2_ref.3) | copy-start | bytes 5971972
  6.2 7.2 %copy-start.6 = (f32[192]{0:T(256)S(1)}, f32[192]{0:T(256)}, u32[]{:S(2)}) copy-start(f32[192]{0:T(256)} %param.15) | copy-start | bytes 2308
  6.2 7.1 %collective-permute-start.4 = (bf16[2,8,8,384]{3,2,1,0:T(8,128)(2,1)S(1)}, bf16[2,8,8,384]{3,2,1,0:T(8,128)(2,1)S(1)}, u32[]{:S(2)}, u32[]{:S(2)}) collective-permute-start(bf16[2,8,8,384]{3,2,1,0:T(8,128)(2,1)S(1)} %get-tuple-element.30), channel_id=1, source_target_pairs={{1,2},{2,1},{9,10},{10,9},{3,4},{4,3},{11,12},{12,11},{5,6},{6,5},... | collective-permute-start | bytes 294920 | tf_op jit(solution)/shard_map/ppermute | solution.py:469
  7.0 8.4 %collective-permute-start.3 = (bf16[13,8,384]{2,1,0:T(8,128)(2,1)S(1)}, bf16[13,8,384]{2,1,0:T(8,128)(2,1)S(1)}, u32[]{:S(2)}, u32[]{:S(2)}) collective-permute-start(bf16[13,8,384]{2,1,0:T(8,128)(2,1)S(1)} %get-tuple-element.28), channel_id=1, source_target_pairs={{1,10},{2,9},{3,12},{4,11},{5,14},{6,13},{17,26},{18,25},{19,28},{... | collective-permute-start | bytes 239624 | tf_op jit(solution)/shard_map/ppermute | solution.py:470
  9.7 5.6 %collective-permute-start.2 = (bf16[12,8,384]{2,1,0:T(8,128)(2,1)S(1)}, bf16[12,8,384]{2,1,0:T(8,128)(2,1)S(1)}, u32[]{:S(2)}, u32[]{:S(2)}) collective-permute-start(bf16[12,8,384]{2,1,0:T(8,128)(2,1)S(1)} %shard_map.85), channel_id=1, source_target_pairs={{0,1},{1,0},{2,3},{3,2},{4,5},{5,4},{6,7},{7,6},{8,9},{9,8},{10,11... | collective-permute-start | bytes 221192 | tf_op jit(solution)/shard_map/ppermute | solution.py:492
  17.3 1.4 %collective-permute-start.5 = (bf16[8,4,8,192]{3,2,1,0:T(8,128)(2,1)S(1)}, bf16[8,4,8,192]{3,2,1,0:T(8,128)(2,1)S(1)}, u32[]{:S(2)}, u32[]{:S(2)}) collective-permute-start(bf16[8,4,8,192]{3,2,1,0:T(8,128)(2,1)S(1)} %get-tuple-element.36), channel_id=1, source_target_pairs={{0,1},{1,0},{2,3},{3,2},{4,5},{5,4},{6,7},{7,6},{8,9},{9,8},{10,11... | collective-permute-start | bytes 294920 | tf_op jit(solution)/shard_map/ppermute | solution.py:520

commit v3 on v2

--- a/solution.py
+++ b/solution.py
@@ -16,10 +16,14 @@
     slots_ref[...] = lax.broadcasted_iota(jnp.int32, slots_ref.shape, 0)
 
 
+def lower_part():
+    return 1 - lax.axis_index("wa")
+
+
 def prepare_kernel(total_ref, slots_ref, raw, tail_ref, mine_ref, theirs_ref, marks_ref, pack):
     frames, rows = raw.shape[:2]
     pairs, held = rows // 2, mine_ref.shape[1]
-    core = lax.axis_index("wa")
+    core = lower_part()
     total = total_ref[0]
     for frame in range(frames):
         for pair in range(pairs):
@@ -124,8 +128,8 @@
     waiting[1](waiting[0])
 
 
-def convolved(operand, weights_ref, bias_ref, frame, frames, rows, then):
-    products = -(-frames * rows * operand.shape[3] // PRODUCT)
+def convolved(operand, weights_ref, bias_ref, frame, frames, rows, then, most=PRODUCT):
+    products = -(-frames * rows * operand.shape[3] // most)
     step = -(-frames // products)
 
     def part(start):
@@ -205,7 +209,7 @@
 def border_kernel(tail_ref, mine_ref, other_ref, tail_edge_ref, own_edge_ref):
     frames, held = mine_ref.shape[:2]
     pairs = tail_ref.shape[0] // CACHE
-    core = lax.axis_index("wa")
+    core = lower_part()
     pair = core * (held - 1)
     for slot in range(CACHE):
         tail_edge_ref[slot] = tail_ref[slot * pairs + core * (pairs - 1)]
@@ -239,18 +243,18 @@
                     target(first + frame, 2 * k + row, kept.astype(jnp.bfloat16))
 
 
-def hide(operand, weights_ref, bias_ref, gain_ref, first, count, rows, flags, store):
+def hide(operand, weights_ref, bias_ref, gain_ref, first, count, rows, flags, store, most=PRODUCT):
     channels = weights_ref.shape[-1]
 
     def then(begin, part, hidden):
         flag = jnp.concatenate(flags[begin:begin + part], axis=0)
         store(begin, begin + part, second_rows(hidden, flag, gain_ref, channels))
 
-    return convolved(operand, weights_ref, bias_ref, first, count, rows, then)
+    return convolved(operand, weights_ref, bias_ref, first, count, rows, then, most)
 
 
 def inside_flags(rows):
-    core, place = lax.axis_index("wa"), lax.axis_index("ha")
+    core, place = lower_part(), lax.axis_index("ha")
     inside = jnp.where(core == 0, place > 0, place < lax.axis_size("ha") - 1)
     row = lax.broadcasted_iota(jnp.int32, (1, rows, 1, 1), 1)
     return jnp.where((row == (rows - 1) * core) & jnp.logical_not(inside), 0.0, 1.0)
@@ -258,7 +262,7 @@
 
 def other_rows_kernel(tail_ref, late_ref, rest_ref):
     pairs, held = tail_ref.shape[0] // CACHE, rest_ref.shape[0] // CACHE
-    first = (1 - lax.axis_index("wa")) * (pairs - held)
+    first = (1 - lower_part()) * (pairs - held)
     for slot in range(CACHE):
         rest_ref[slot * held:(slot + 1) * held] = tail_ref[pl.ds(slot * pairs + first, held)]
 
@@ -276,13 +280,16 @@
     def store(begin, end, rows):
         late_ref[:, begin:end] = rows
 
-    steps = hide(first_ref, w1_ref, bias1_ref, gain2_ref, 0, frames - 2, 2 * pairs - 2, live, store)
-    half = -(-(frames - 2) // len(steps)) + 2
-    fill(0, half)
-    product, then = steps[0]
-    held = product()
-    fill(half, frames)
-    in_turn([(lambda: held, then)] + steps[1:])
+    steps = hide(first_ref, w1_ref, bias1_ref, gain2_ref, 0, frames - 2, 2 * pairs - 2, live, store, 2 * PRODUCT // 3)
+    each = -(-(frames - 2) // len(steps))
+
+    def filled(k, product):
+        def run():
+            fill(min(frames, each * k + (2 if k else 0)), min(frames, each * (k + 1) + 2))
+            return product()
+        return run
+
+    in_turn([(filled(k, product), then) for k, (product, then) in enumerate(steps)])
 
 
 def edge_kernel(
@@ -290,7 +297,7 @@
     gain1_ref, w1_ref, bias1_ref, gain2_ref, w2_ref, bias2_ref,
     strip_ref, hidden_ref, keep_ref, send_ref, strip, operand,
 ):
-    core = lax.axis_index("wa")
+    core = lower_part()
     frames, pairs = mine_ref.shape[:2]
     rows = 2 * pairs
     late = frames - CACHE
@@ -333,7 +340,7 @@
     late_keep_ref, late_send_ref, gain1_ref, w1_ref, bias1_ref, gain2_ref, w2_ref, bias2_ref,
     keep_ref, send_ref, plane, operand,
 ):
-    core = lax.axis_index("wa")
+    core = lower_part()
     held = mine_ref.shape[1]
     rows = 2 * held
     pairs = tail_mine_ref.shape[0] // CACHE
@@ -384,7 +391,7 @@
 
 
 def place_kernel(keep_ref, got_ref, result_ref, arrived):
-    core, half = lax.axis_index("wa"), keep_ref.shape[1]
+    core, half = lower_part(), keep_ref.shape[1]
     copies = [
         pltpu.make_async_copy(keep_ref, result_ref.at[:, pl.ds(half * core, half)], arrived.at[0]),
         pltpu.make_async_copy(got_ref, result_ref.at[:, pl.ds(half * (1 - core), half)], arrived.at[1]),
@@ -435,7 +442,7 @@
     if blocks > 2:
         tail = joined_tail(tail)
         rest = lax.dynamic_slice_in_dim(
-            tail[:-1].reshape(CACHE, pairs, side, packed), (1 - lax.axis_index("wa")) * (pairs - held), held, 1
+            tail[:-1].reshape(CACHE, pairs, side, packed), (1 - lower_part()) * (pairs - held), held, 1
         )
         theirs = jnp.concatenate([rest.reshape(tiles, side, packed), theirs[tiles:]], axis=0)
     straight, diagonal, across = [], [], []
@@ -449,10 +456,10 @@
                 straight.append((index(k, h, core), index(k + 1, h, core)))
     for h in range(tall - 1):
         for k in range(blocks):
-            lower, upper = index(k, h, 1), index(k, h + 1, 0)
+            lower, upper = index(k, h, 0), index(k, h + 1, 1)
             across += [(lower, upper), (upper, lower)]
             if k + 1 < blocks:
-                lower_next, upper_next = index(k + 1, h, 1), index(k + 1, h + 1, 0)
+                lower_next, upper_next = index(k + 1, h, 0), index(k + 1, h + 1, 1)
                 diagonal += [(lower, upper_next), (upper, lower_next)]
     axes = ("tchunk", "ha", "wa")
     swap = [(0, 1), (1, 0)]

time: 19.6 us -> 19.4 us (0.990)
  waiting for transfers between devices: 1.32 us -> 1 us
    ppermute x1, starting transfers between devices: 3.62 us -> 0.07 us  [shards(): tail_other = lax.ppermute(rest, 'wa', swap)]
    ppermute x1, starting transfers between devices: 0.8 us -> 3.56 us  [shards(): own_edge = lax.ppermute(own_edge, axes, across)]
    ppermute x1, starting transfers between devices: 0.8 us -> 1.29 us  [shards(): tail_edge = lax.ppermute(tail_edge, axes, diagonal)]
    ppermute x1, starting transfers between devices: 0.11 us -> 0.54 us  [shards(): got = lax.ppermute(send, 'wa', swap)]
    ppermute x1, waiting for transfers between devices: 1.3 us -> 0.99 us  [shards(): got = lax.ppermute(send, 'wa', swap)]
where the time goes in v3:
time: 19.4 us; the launch traced here: 19.2 us
  starting transfers between devices  10.4 us (54%)
  Pallas kernels  6.64 us (34%)
  waiting for transfers between devices  1 us (5%)
  between operations  0.91 us (5%)
  local copies, waits for them, and re-layouts  0.31 us (2%)
    ppermute x1, starting transfers between devices, shards(): tail_mine = lax.ppermute(tail, axes, straight)  4.41 us
    ppermute x1, starting transfers between devices, shards(): own_edge = lax.ppermute(own_edge, axes, across)  3.56 us
    pallas_call x1, Pallas kernels, shards(): pl.pallas_call(edge_kernel, out_shape=(shape(3, 2, 2, width, LANES), shap...  1.99 us
    pallas_call x1, Pallas kernels, shards(): pl.pallas_call(early_kernel, out_shape=(shape(frames, half, side, channel...  1.91 us
    pallas_call x1, Pallas kernels, shards(): pl.pallas_call(own_kernel, out_shape=(shape(3, frames, half + 2, width, L...  1.83 us
    ppermute x1, starting transfers between devices, shards(): tail_edge = lax.ppermute(tail_edge, axes, diagonal)  1.29 us
    ppermute x1, waiting for transfers between devices, shards(): got = lax.ppermute(send, 'wa', swap)  0.99 us
    pallas_call x1, Pallas kernels, shards(): pl.pallas_call(place_kernel, out_shape=shape(*features.shape), in_specs=[...  0.71 us
  transfers between devices with their start and end apart: 6, of which 1 were waited for; matrix products, arithmetic and copies ran while one was open for 0% of the time, Pallas kernels for 20%

profile of v3, /device:TPU:0, one launch (start us, length us, event | category | flops | bytes accessed | tf_op | source)
XLA Modules:
  0.0 19.2 jit_solution(6332262167231703542)
XLA Ops:
  0.0 0.0 copy-start.2
  0.7 0.3 %copy-done.2 = bf16[8,8,8,192]{3,2,1,0:T(8,128)(2,1)S(1)} copy-done((bf16[8,8,8,192]{3,2,1,0:T(8,128)(2,1)S(1)}, bf16[8,8,8,192]{3,2,1,0:T(8,128)(2,1)}, u32[]{:S(2)}) %copy-start.2) | copy-done | bytes 196632
  1.0 0.1 shard_map.83
  1.1 0.5 %collective-permute-start.1 = (bf16[36,8,384]{2,1,0:T(8,128)(2,1)S(1)}, bf16[36,8,384]{2,1,0:T(8,128)(2,1)S(1)}, u32[]{:S(2)}, u32[]{:S(2)}) collective-permute-start(bf16[36,8,384]{2,1,0:T(8,128)(2,1)S(1)} %get-tuple-element.26), channel_id=1, source_target_pairs={{0,1},{1,0},{2,3},{3,2},{4,5},{5,4},{6,7},{7,6},{8,9},{9,8},{10,11... | collective-permute-start | bytes 663560 | tf_op jit(solution)/shard_map/ppermute | solution.py:467
  1.6 4.4 %collective-permute-start = (bf16[17,8,384]{2,1,0:T(8,128)(2,1)S(1)}, bf16[17,8,384]{2,1,0:T(8,128)(2,1)S(1)}, u32[]{:S(2)}, u32[]{:S(2)}) collective-permute-start(bf16[17,8,384]{2,1,0:T(8,128)(2,1)S(1)} %get-tuple-element.24.tail_ref), channel_id=1, source_target_pairs={{0,8},{1,9},{2,10},{3,11},{4,12},{5,13},{6,14},{7,15},{16,24},{17,... | collective-permute-start | bytes 313352 | tf_op jit(solution)/shard_map/ppermute | solution.py:466
  6.1 0.0 collective-permute-done.1.other_ref
  6.1 0.0 copy-start
  6.1 0.0 copy-start.3
  6.1 0.0 copy-start.4
  6.1 0.0 copy-start.5
  6.2 0.0 copy-start.1
  6.2 0.0 copy-start.6
  6.2 3.6 %collective-permute-start.4 = (bf16[2,8,8,384]{3,2,1,0:T(8,128)(2,1)S(1)}, bf16[2,8,8,384]{3,2,1,0:T(8,128)(2,1)S(1)}, u32[]{:S(2)}, u32[]{:S(2)}) collective-permute-start(bf16[2,8,8,384]{3,2,1,0:T(8,128)(2,1)S(1)} %get-tuple-element.30), channel_id=1, source_target_pairs={{0,3},{3,0},{8,11},{11,8},{2,5},{5,2},{10,13},{13,10},{4,7},{7,4},... | collective-permute-start | bytes 294920 | tf_op jit(solution)/shard_map/ppermute | solution.py:476
  9.7 1.3 %collective-permute-start.3 = (bf16[13,8,384]{2,1,0:T(8,128)(2,1)S(1)}, bf16[13,8,384]{2,1,0:T(8,128)(2,1)S(1)}, u32[]{:S(2)}, u32[]{:S(2)}) collective-permute-start(bf16[13,8,384]{2,1,0:T(8,128)(2,1)S(1)} %get-tuple-element.28), channel_id=1, source_target_pairs={{0,11},{3,8},{2,13},{5,10},{4,15},{7,12},{16,27},{19,24},{18,29},{... | collective-permute-start | bytes 239624 | tf_op jit(solution)/shard_map/ppermute | solution.py:477
  11.0 0.0 copy-done
  11.1 0.0 copy-done.3
  11.1 0.0 copy-done.4
  11.1 0.0 copy-done.5
  11.1 1.8 %shard_map.84 = (bf16[3,8,6,16,128]{4,3,2,1,0:T(8,128)(2,1)S(1)}, bf16[3,6,4,16,128]{4,3,2,1,0:T(8,128)(2,1)S(1)}) custom-call(bf16[8,384]{1,0:T(8,128)(2,1)S(1)} %get-tuple-element.23.marks_ref, bf16[8,3,8,384]{3,2,1,0:T(8,128)(2,1)S(1)} %get-tuple-element.25.mine_ref, bf16[36,8,384]{2,1,0:T(8,128)(2,1)S(1)} %collective-permute-done.1.other_ref, ...), custom_call_target="tpu_custom_call" | custom-call | flops 764411904 | bytes 4194304 | tf_op jit(solution)/shard_map/pallas_call | solution.py:483
  12.9 0.0 collective-permute-done.tail_ref.tail_mine_ref
  13.0 0.1 collective-permute-start.2
  13.0 0.0 collective-permute-done.4.edge_ref
  13.0 0.0 copy-done.1
  13.1 0.0 copy-done.6
  13.1 2.0 %shard_map.87 = (bf16[3,2,2,16,128]{4,3,2,1,0:T(8,128)(2,1)S(1)}, bf16[3,2,6,16,128]{4,3,2,1,0:T(8,128)(2,1)S(1)}, bf16[4,4,8,192]{3,2,1,0:T(8,128)(2,1)S(1)}, bf16[4,4,8,192]{3,2,1,0:T(8,128)(2,1)S(1)}) custom-call(bf16[8,384]{1,0:T(8,128)(2,1)S(1)} %get-tuple-element.23.marks_ref, bf16[8,3,8,384]{3,2,1,0:T(8,128)(2,1)S(1)} %get-tuple-element.25.mine_ref, ...), custom_call_target="tpu_custom_call" | custom-call | flops 1048576 | bytes 1048576 | tf_op jit(solution)/shard_map/pallas_call | solution.py:500
  15.1 0.0 collective-permute-done.2.tail_other_ref
  15.1 0.0 collective-permute-done.3.edge_ref
  15.1 1.9 %shard_map.88 = (bf16[8,4,8,192]{3,2,1,0:T(8,128)(2,1)S(1)}, bf16[8,4,8,192]{3,2,1,0:T(8,128)(2,1)S(1)}) custom-call(bf16[8,384]{1,0:T(8,128)(2,1)S(1)} %get-tuple-element.23.marks_ref, bf16[17,8,384]{2,1,0:T(8,128)(2,1)S(1)} %collective-permute-done.tail_ref.tail_mine_ref, bf16[12,8,384]{2,1,0:T(8,128)(2,1)S(1)} %collective-permute-done.2.tail_other_ref, ...), custom_call_target="tpu_custom_call" | custom-call | flops 1274019840 | bytes 8388608 | tf_op jit(solution)/shard_map/pallas_call | solution.py:515
  17.0 0.5 %collective-permute-start.5 = (bf16[8,4,8,192]{3,2,1,0:T(8,128)(2,1)S(1)}, bf16[8,4,8,192]{3,2,1,0:T(8,128)(2,1)S(1)}, u32[]{:S(2)}, u32[]{:S(2)}) collective-permute-start(bf16[8,4,8,192]{3,2,1,0:T(8,128)(2,1)S(1)} %get-tuple-element.36), channel_id=1, source_target_pairs={{0,1},{1,0},{2,3},{3,2},{4,5},{5,4},{6,7},{7,6},{8,9},{9,8},{10,11... | collective-permute-start | bytes 294920 | tf_op jit(solution)/shard_map/ppermute | solution.py:527
  17.5 1.0 %collective-permute-done.5.got_ref = bf16[8,4,8,192]{3,2,1,0:T(8,128)(2,1)S(1)} collective-permute-done((bf16[8,4,8,192]{3,2,1,0:T(8,128)(2,1)S(1)}, bf16[8,4,8,192]{3,2,1,0:T(8,128)(2,1)S(1)}, u32[]{:S(2)}, u32[]{:S(2)}) %collective-permute-start.5) | collective-permute-done | bytes 98336 | tf_op jit(solution)/shard_map/ppermute | solution.py:527
  18.5 0.7 %shard_map.89 = bf16[8,8,8,192]{3,2,1,0:T(8,128)(2,1)} custom-call(bf16[8,4,8,192]{3,2,1,0:T(8,128)(2,1)S(1)} %get-tuple-element.35.keep_ref, bf16[8,4,8,192]{3,2,1,0:T(8,128)(2,1)S(1)} %collective-permute-done.5.got_ref), custom_call_target="tpu_custom_call" | custom-call | tf_op jit(solution)/shard_map/pallas_call | solution.py:528
  (3 shorter events, 0.0 us)
Async XLA Ops:
  0.0 1.0 %copy-start.2 = (bf16[8,8,8,192]{3,2,1,0:T(8,128)(2,1)S(1)}, bf16[8,8,8,192]{3,2,1,0:T(8,128)(2,1)}, u32[]{:S(2)}) copy-start(bf16[8,8,8,192]{3,2,1,0:T(8,128)(2,1)} %raw.1) | copy-start | bytes 589828
  1.1 4.9 %collective-permute-start.1 = (bf16[36,8,384]{2,1,0:T(8,128)(2,1)S(1)}, bf16[36,8,384]{2,1,0:T(8,128)(2,1)S(1)}, u32[]{:S(2)}, u32[]{:S(2)}) collective-permute-start(bf16[36,8,384]{2,1,0:T(8,128)(2,1)S(1)} %get-tuple-element.26), channel_id=1, source_target_pairs={{0,1},{1,0},{2,3},{3,2},{4,5},{5,4},{6,7},{7,6},{8,9},{9,8},{10,11... | collective-permute-start | bytes 663560 | tf_op jit(solution)/shard_map/ppermute | solution.py:467
  1.6 11.3 %collective-permute-start = (bf16[17,8,384]{2,1,0:T(8,128)(2,1)S(1)}, bf16[17,8,384]{2,1,0:T(8,128)(2,1)S(1)}, u32[]{:S(2)}, u32[]{:S(2)}) collective-permute-start(bf16[17,8,384]{2,1,0:T(8,128)(2,1)S(1)} %get-tuple-element.24.tail_ref), channel_id=1, source_target_pairs={{0,8},{1,9},{2,10},{3,11},{4,12},{5,13},{6,14},{7,15},{16,24},{17,... | collective-permute-start | bytes 313352 | tf_op jit(solution)/shard_map/ppermute | solution.py:466
  6.1 5.0 %copy-start = (bf16[3,3,3,192,192]{4,3,2,1,0:T(8,128)(2,1)S(1)}, bf16[3,3,3,192,192]{4,3,2,1,0:T(8,128)(2,1)}, u32[]{:S(2)}) copy-start(bf16[3,3,3,192,192]{4,3,2,1,0:T(8,128)(2,1)} %w1_ref.5) | copy-start | bytes 5971972
  6.1 5.0 %copy-start.3 = (f32[192]{0:T(256)S(1)}, f32[192]{0:T(256)}, u32[]{:S(2)}) copy-start(f32[192]{0:T(256)} %param.10) | copy-start | bytes 2308
  6.1 5.0 %copy-start.4 = (f32[192]{0:T(256)S(1)}, f32[192]{0:T(256)}, u32[]{:S(2)}) copy-start(f32[192]{0:T(256)} %param.12) | copy-start | bytes 2308
  6.1 5.0 %copy-start.5 = (f32[192]{0:T(256)S(1)}, f32[192]{0:T(256)}, u32[]{:S(2)}) copy-start(f32[192]{0:T(256)} %param.13) | copy-start | bytes 2308
  6.2 6.9 %copy-start.1 = (bf16[3,3,3,192,192]{4,3,2,1,0:T(8,128)(2,1)S(1)}, bf16[3,3,3,192,192]{4,3,2,1,0:T(8,128)(2,1)}, u32[]{:S(2)}) copy-start(bf16[3,3,3,192,192]{4,3,2,1,0:T(8,128)(2,1)} %w2_ref.3) | copy-start | bytes 5971972
  6.2 6.9 %copy-start.6 = (f32[192]{0:T(256)S(1)}, f32[192]{0:T(256)}, u32[]{:S(2)}) copy-start(f32[192]{0:T(256)} %param.15) | copy-start | bytes 2308
  6.2 6.9 %collective-permute-start.4 = (bf16[2,8,8,384]{3,2,1,0:T(8,128)(2,1)S(1)}, bf16[2,8,8,384]{3,2,1,0:T(8,128)(2,1)S(1)}, u32[]{:S(2)}, u32[]{:S(2)}) collective-permute-start(bf16[2,8,8,384]{3,2,1,0:T(8,128)(2,1)S(1)} %get-tuple-element.30), channel_id=1, source_target_pairs={{0,3},{3,0},{8,11},{11,8},{2,5},{5,2},{10,13},{13,10},{4,7},{7,4},... | collective-permute-start | bytes 294920 | tf_op jit(solution)/shard_map/ppermute | solution.py:476
  9.7 5.3 %collective-permute-start.3 = (bf16[13,8,384]{2,1,0:T(8,128)(2,1)S(1)}, bf16[13,8,384]{2,1,0:T(8,128)(2,1)S(1)}, u32[]{:S(2)}, u32[]{:S(2)}) collective-permute-start(bf16[13,8,384]{2,1,0:T(8,128)(2,1)S(1)} %get-tuple-element.28), channel_id=1, source_target_pairs={{0,11},{3,8},{2,13},{5,10},{4,15},{7,12},{16,27},{19,24},{18,29},{... | collective-permute-start | bytes 239624 | tf_op jit(solution)/shard_map/ppermute | solution.py:477
  13.0 2.1 %collective-permute-start.2 = (bf16[12,8,384]{2,1,0:T(8,128)(2,1)S(1)}, bf16[12,8,384]{2,1,0:T(8,128)(2,1)S(1)}, u32[]{:S(2)}, u32[]{:S(2)}) collective-permute-start(bf16[12,8,384]{2,1,0:T(8,128)(2,1)S(1)} %shard_map.85), channel_id=1, source_target_pairs={{0,1},{1,0},{2,3},{3,2},{4,5},{5,4},{6,7},{7,6},{8,9},{9,8},{10,11... | collective-permute-start | bytes 221192 | tf_op jit(solution)/shard_map/ppermute | solution.py:499
  17.0 1.5 %collective-permute-start.5 = (bf16[8,4,8,192]{3,2,1,0:T(8,128)(2,1)S(1)}, bf16[8,4,8,192]{3,2,1,0:T(8,128)(2,1)S(1)}, u32[]{:S(2)}, u32[]{:S(2)}) collective-permute-start(bf16[8,4,8,192]{3,2,1,0:T(8,128)(2,1)S(1)} %get-tuple-element.36), channel_id=1, source_target_pairs={{0,1},{1,0},{2,3},{3,2},{4,5},{5,4},{6,7},{7,6},{8,9},{9,8},{10,11... | collective-permute-start | bytes 294920 | tf_op jit(solution)/shard_map/ppermute | solution.py:527

commit v4 on v3

--- a/solution.py
+++ b/solution.py
@@ -86,8 +86,7 @@
     return pltpu.roll(values.reshape(-1, LANES), LANES // 2, 1).reshape(shape)
 
 
-def first_rows(left, right, gain_ref, channels):
-    raw = jnp.concatenate([left.astype(jnp.float32), right.astype(jnp.float32)], axis=2)
+def first_active(raw, gain_ref, channels):
     front, back, high = raw[..., :LANES], raw[..., LANES:2 * LANES], raw[..., 2 * LANES:]
     lower = lane_mask()
     squared = high * high
@@ -101,6 +100,11 @@
     front = silu(front * scale_front * gain_low)
     back = silu(back * scale_back * gain_low)
     high = silu(high * jnp.where(lower, scale_front, scale_back) * gain_high)
+    return front, back, high
+
+
+def first_rows(front, back, high):
+    lower = lane_mask()
     turned = rolled(high)
     one = [front, jnp.where(lower, high, 0.0), jnp.where(lower, 0.0, turned)]
     two = [back, jnp.where(lower, turned, 0.0), jnp.where(lower, 0.0, high)]
@@ -198,8 +202,13 @@
 
 def fill_rows(operand, frame, row, mine, other, gain_ref):
     left, right = halves(lax.axis_index("wa"), mine, other)
+    raw = jnp.concatenate([left.astype(jnp.float32), right.astype(jnp.float32)], axis=2)
     frames, pairs = mine.shape[:2]
-    upper, lower = first_rows(left, right, gain_ref, gain_ref.shape[-1])
+    if gain_ref is None:
+        active = raw[..., :LANES], raw[..., LANES:2 * LANES], raw[..., 2 * LANES:]
+    else:
+        active = first_active(raw, gain_ref, gain_ref.shape[-1])
+    upper, lower = first_rows(*active)
     for part in range(len(upper)):
         for pair in range(pairs):
             operand[part, frame:frame + frames, pl.ds(row + 2 * pair, 1)] = upper[part][:, pair:pair + 1]
@@ -260,11 +269,24 @@
     return jnp.where((row == (rows - 1) * core) & jnp.logical_not(inside), 0.0, 1.0)
 
 
-def other_rows_kernel(tail_ref, late_ref, rest_ref):
+def tail_kernel(tail_ref, gain_ref, late_ref, mine_ref, rest_ref, active):
     pairs, held = tail_ref.shape[0] // CACHE, rest_ref.shape[0] // CACHE
-    first = (1 - lower_part()) * (pairs - held)
-    for slot in range(CACHE):
-        rest_ref[slot * held:(slot + 1) * held] = tail_ref[pl.ds(slot * pairs + first, held)]
+    place = lower_part() * (pairs - held)
+    earlier = lax.axis_index("tchunk") > 0
+
+    @pl.when(earlier)
+    def _():
+        raw = tail_ref[0:CACHE * pairs].astype(jnp.float32)[None]
+        parts = first_active(raw, gain_ref, gain_ref.shape[-1])
+        active[...] = jnp.concatenate([part[0].astype(jnp.bfloat16) for part in parts], axis=-1)
+        for slot in range(CACHE):
+            for ref, first in ((mine_ref, place), (rest_ref, pairs - held - place)):
+                ref[slot * held:(slot + 1) * held] = active[pl.ds(slot * pairs + first, held)]
+
+    @pl.when(jnp.logical_not(earlier))
+    def _():
+        for ref in (mine_ref, rest_ref):
+            ref[...] = jnp.zeros(ref.shape, ref.dtype)
 
 
 def own_kernel(
@@ -336,7 +358,7 @@
 
 
 def early_kernel(
-    marks_ref, tail_mine_ref, tail_other_ref, mine_ref, other_ref, edge_ref, first_ref, strip_ref, hidden_ref,
+    marks_ref, tail_mine_ref, tail_rows_ref, tail_other_ref, mine_ref, other_ref, edge_ref, first_ref, strip_ref, hidden_ref,
     late_keep_ref, late_send_ref, gain1_ref, w1_ref, bias1_ref, gain2_ref, w2_ref, bias2_ref,
     keep_ref, send_ref, plane, operand,
 ):
@@ -349,8 +371,8 @@
     earlier = lax.axis_index("tchunk") > 0
     middle, border = 2 * (1 - core), rows * core
 
-    def unpacked(ref, stride, first):
-        return jnp.stack([ref[pl.ds(slot * stride + first, held)] for slot in range(CACHE)])
+    def unpacked(ref):
+        return ref[...].reshape((CACHE, held) + ref.shape[1:])
 
     plane[:, CACHE:, pl.ds(middle, rows)] = first_ref[:, 0:2]
     plane[:, CACHE:, pl.ds(border, 2)] = strip_ref[...]
@@ -365,8 +387,7 @@
 
     @pl.when(earlier)
     def _():
-        mine = unpacked(tail_mine_ref, pairs, core * (pairs - held))
-        fill_rows(plane, 0, middle, mine, unpacked(tail_other_ref, held, 0), gain1_ref)
+        fill_rows(plane, 0, middle, unpacked(tail_rows_ref), unpacked(tail_other_ref), None)
         mine, other = edge_ref[CACHE:2 * CACHE], edge_ref[0:CACHE]
         fill_rows(plane, 0, border, mine[:, None], other[:, None], gain1_ref)
         fill(0, frame_flags(tail_mine_ref[CACHE * pairs], range(CACHE - 2, CACHE)) + live[0:2])
@@ -391,11 +412,16 @@
 
 
 def place_kernel(keep_ref, got_ref, result_ref, arrived):
-    core, half = lower_part(), keep_ref.shape[1]
-    copies = [
-        pltpu.make_async_copy(keep_ref, result_ref.at[:, pl.ds(half * core, half)], arrived.at[0]),
-        pltpu.make_async_copy(got_ref, result_ref.at[:, pl.ds(half * (1 - core), half)], arrived.at[1]),
-    ]
+    core = lower_part()
+    frames, half = keep_ref.shape[:2]
+    step = max(1, frames // 4)
+    copies = []
+    for source, place in ((keep_ref, core), (got_ref, 1 - core)):
+        for frame in range(0, frames, step):
+            chosen = pl.ds(frame, min(step, frames - frame))
+            copies.append(pltpu.make_async_copy(
+                source.at[chosen], result_ref.at[chosen, pl.ds(half * place, half)], arrived.at[len(copies)]
+            ))
     for copy in copies:
         copy.start()
     for copy in copies:
@@ -488,14 +514,15 @@
         compiler_params=limit,
         cost_estimate=cost(work * (frames - 2) * half, 4 * 2**20),
     )(marks, mine, other, *weights[:4])
-    rest = pl.pallas_call(
-        other_rows_kernel,
-        out_shape=shape(tiles, side, packed),
-        in_specs=[vmem, pl.BlockSpec(memory_space=pl.ANY)],
-        out_specs=vmem,
+    tail_rows, rest = pl.pallas_call(
+        tail_kernel,
+        out_shape=(shape(tiles, side, packed), shape(tiles, side, packed)),
+        in_specs=[vmem, vmem, pl.BlockSpec(memory_space=pl.ANY)],
+        out_specs=(vmem, vmem),
+        scratch_shapes=[pltpu.VMEM((CACHE * pairs, side, packed), bf16)],
         compiler_params=limit,
         cost_estimate=cost(1, 1),
-    )(tail_mine, late)
+    )(tail_mine, weights[0], late)
     tail_other = lax.ppermute(rest, "wa", swap)
     strip, hidden, keep, send = pl.pallas_call(
         edge_kernel,
@@ -515,7 +542,7 @@
     keep, send = pl.pallas_call(
         early_kernel,
         out_shape=(shape(frames, half, side, channels), shape(frames, half, side, channels)),
-        in_specs=[vmem] * 17,
+        in_specs=[vmem] * 18,
         out_specs=(vmem, vmem),
         scratch_shapes=[
             pltpu.VMEM((3, CACHE + 2, half + 4, width, LANES), bf16),
@@ -523,14 +550,14 @@
         ],
         compiler_params=limit,
         cost_estimate=cost(work * CACHE * (2 * half + 2), 8 * 2**20),
-    )(marks, tail_mine, tail_other, mine, other, tail_edge, first, strip, hidden, keep, send, *weights)
+    )(marks, tail_mine, tail_rows, tail_other, mine, other, tail_edge, first, strip, hidden, keep, send, *weights)
     got = lax.ppermute(send, "wa", swap)
     return pl.pallas_call(
         place_kernel,
         out_shape=shape(*features.shape),
         in_specs=[vmem, vmem],
         out_specs=pl.BlockSpec(memory_space=pltpu.HBM),
-        scratch_shapes=[pltpu.SemaphoreType.DMA((2,))],
+        scratch_shapes=[pltpu.SemaphoreType.DMA((2 * frames,))],
         compiler_params=limit,
     )(keep, got)
 

time: 19.4 us -> 19.8 us (1.021)
  Pallas kernels: 6.64 us -> 6.97 us
where the time goes in v4:
time: 19.8 us; the launch traced here: 19.6 us
  starting transfers between devices  10.4 us (53%)
  Pallas kernels  6.97 us (35%)
  waiting for transfers between devices  1 us (5%)
  between operations  0.91 us (5%)
  local copies, waits for them, and re-layouts  0.31 us (2%)
    ppermute x1, starting transfers between devices, shards(): tail_mine = lax.ppermute(tail, axes, straight)  4.41 us
    ppermute x1, starting transfers between devices, shards(): own_edge = lax.ppermute(own_edge, axes, across)  3.56 us
    pallas_call x1, Pallas kernels, shards(): pl.pallas_call(edge_kernel, out_shape=(shape(3, 2, 2, width, LANES), shap...  2.06 us
    pallas_call x1, Pallas kernels, shards(): pl.pallas_call(early_kernel, out_shape=(shape(frames, half, side, channel...  1.99 us
    pallas_call x1, Pallas kernels, shards(): pl.pallas_call(own_kernel, out_shape=(shape(3, frames, half + 2, width, L...  1.88 us
    ppermute x1, starting transfers between devices, shards(): tail_edge = lax.ppermute(tail_edge, axes, diagonal)  1.29 us
    ppermute x1, waiting for transfers between devices, shards(): got = lax.ppermute(send, 'wa', swap)  0.99 us
    pallas_call x1, Pallas kernels, shards(): pl.pallas_call(place_kernel, out_shape=shape(*features.shape), in_specs=[...  0.83 us
  transfers between devices with their start and end apart: 6, of which 1 were waited for; matrix products, arithmetic and copies ran while one was open for 0% of the time, Pallas kernels for 20%

profile of v4, /device:TPU:0, one launch (start us, length us, event | category | flops | bytes accessed | tf_op | source)
XLA Modules:
  0.0 19.6 jit_solution(2965232095430723144)
XLA Ops:
  0.0 0.0 copy-start.2
  0.7 0.3 %copy-done.2 = bf16[8,8,8,192]{3,2,1,0:T(8,128)(2,1)S(1)} copy-done((bf16[8,8,8,192]{3,2,1,0:T(8,128)(2,1)S(1)}, bf16[8,8,8,192]{3,2,1,0:T(8,128)(2,1)}, u32[]{:S(2)}) %copy-start.2) | copy-done | bytes 196632
  1.0 0.1 shard_map.83
  1.1 0.5 %collective-permute-start.1 = (bf16[36,8,384]{2,1,0:T(8,128)(2,1)S(1)}, bf16[36,8,384]{2,1,0:T(8,128)(2,1)S(1)}, u32[]{:S(2)}, u32[]{:S(2)}) collective-permute-start(bf16[36,8,384]{2,1,0:T(8,128)(2,1)S(1)} %get-tuple-element.28), channel_id=1, source_target_pairs={{0,1},{1,0},{2,3},{3,2},{4,5},{5,4},{6,7},{7,6},{8,9},{9,8},{10,11... | collective-permute-start | bytes 663560 | tf_op jit(solution)/shard_map/ppermute | solution.py:493
  1.6 4.4 %collective-permute-start = (bf16[17,8,384]{2,1,0:T(8,128)(2,1)S(1)}, bf16[17,8,384]{2,1,0:T(8,128)(2,1)S(1)}, u32[]{:S(2)}, u32[]{:S(2)}) collective-permute-start(bf16[17,8,384]{2,1,0:T(8,128)(2,1)S(1)} %get-tuple-element.26.tail_ref), channel_id=1, source_target_pairs={{0,8},{1,9},{2,10},{3,11},{4,12},{5,13},{6,14},{7,15},{16,24},{17,... | collective-permute-start | bytes 313352 | tf_op jit(solution)/shard_map/ppermute | solution.py:492
  6.1 0.0 collective-permute-done.1.other_ref
  6.1 0.0 copy-start
  6.1 0.0 copy-start.3
  6.1 0.0 copy-start.4
  6.1 0.0 copy-start.5
  6.2 0.0 copy-start.1
  6.2 0.0 copy-start.6
  6.2 3.6 %collective-permute-start.4 = (bf16[2,8,8,384]{3,2,1,0:T(8,128)(2,1)S(1)}, bf16[2,8,8,384]{3,2,1,0:T(8,128)(2,1)S(1)}, u32[]{:S(2)}, u32[]{:S(2)}) collective-permute-start(bf16[2,8,8,384]{3,2,1,0:T(8,128)(2,1)S(1)} %get-tuple-element.34), channel_id=1, source_target_pairs={{0,3},{3,0},{8,11},{11,8},{2,5},{5,2},{10,13},{13,10},{4,7},{7,4},... | collective-permute-start | bytes 294920 | tf_op jit(solution)/shard_map/ppermute | solution.py:502
  9.7 1.3 %collective-permute-start.3 = (bf16[13,8,384]{2,1,0:T(8,128)(2,1)S(1)}, bf16[13,8,384]{2,1,0:T(8,128)(2,1)S(1)}, u32[]{:S(2)}, u32[]{:S(2)}) collective-permute-start(bf16[13,8,384]{2,1,0:T(8,128)(2,1)S(1)} %get-tuple-element.32), channel_id=1, source_target_pairs={{0,11},{3,8},{2,13},{5,10},{4,15},{7,12},{16,27},{19,24},{18,29},{... | collective-permute-start | bytes 239624 | tf_op jit(solution)/shard_map/ppermute | solution.py:503
  11.0 0.0 copy-done
  11.1 0.0 copy-done.3
  11.1 0.0 copy-done.4
  11.1 0.0 copy-done.5
  11.1 1.9 %shard_map.84 = (bf16[3,8,6,16,128]{4,3,2,1,0:T(8,128)(2,1)S(1)}, bf16[3,6,4,16,128]{4,3,2,1,0:T(8,128)(2,1)S(1)}) custom-call(bf16[8,384]{1,0:T(8,128)(2,1)S(1)} %get-tuple-element.25.marks_ref, bf16[8,3,8,384]{3,2,1,0:T(8,128)(2,1)S(1)} %get-tuple-element.27.mine_ref, bf16[36,8,384]{2,1,0:T(8,128)(2,1)S(1)} %collective-permute-done.1.other_ref, ...), custom_call_target="tpu_custom_call" | custom-call | flops 764411904 | bytes 4194304 | tf_op jit(solution)/shard_map/pallas_call | solution.py:509
  13.0 0.0 collective-permute-done.tail_ref.tail_mine_ref
  13.0 0.1 collective-permute-start.2
  13.1 0.0 collective-permute-done.4.edge_ref
  13.1 0.0 copy-done.1
  13.1 0.0 copy-done.6
  13.1 2.1 %shard_map.87 = (bf16[3,2,2,16,128]{4,3,2,1,0:T(8,128)(2,1)S(1)}, bf16[3,2,6,16,128]{4,3,2,1,0:T(8,128)(2,1)S(1)}, bf16[4,4,8,192]{3,2,1,0:T(8,128)(2,1)S(1)}, bf16[4,4,8,192]{3,2,1,0:T(8,128)(2,1)S(1)}) custom-call(bf16[8,384]{1,0:T(8,128)(2,1)S(1)} %get-tuple-element.25.marks_ref, bf16[8,3,8,384]{3,2,1,0:T(8,128)(2,1)S(1)} %get-tuple-element.27.mine_ref, ...), custom_call_target="tpu_custom_call" | custom-call | flops 1048576 | bytes 1048576 | tf_op jit(solution)/shard_map/pallas_call | solution.py:527
  15.2 0.0 collective-permute-done.2.tail_other_ref
  15.2 0.0 collective-permute-done.3.edge_ref
  15.2 2.0 %shard_map.88 = (bf16[8,4,8,192]{3,2,1,0:T(8,128)(2,1)S(1)}, bf16[8,4,8,192]{3,2,1,0:T(8,128)(2,1)S(1)}) custom-call(bf16[8,384]{1,0:T(8,128)(2,1)S(1)} %get-tuple-element.25.marks_ref, bf16[17,8,384]{2,1,0:T(8,128)(2,1)S(1)} %collective-permute-done.tail_ref.tail_mine_ref, bf16[12,8,384]{2,1,0:T(8,128)(2,1)S(1)} %get-tuple-element.30.tail_rows_ref, ...), custom_call_target="tpu_custom_call" | custom-call | flops 1274019840 | bytes 8388608 | tf_op jit(solution)/shard_map/pallas_call | solution.py:542
  17.2 0.5 %collective-permute-start.5 = (bf16[8,4,8,192]{3,2,1,0:T(8,128)(2,1)S(1)}, bf16[8,4,8,192]{3,2,1,0:T(8,128)(2,1)S(1)}, u32[]{:S(2)}, u32[]{:S(2)}) collective-permute-start(bf16[8,4,8,192]{3,2,1,0:T(8,128)(2,1)S(1)} %get-tuple-element.40), channel_id=1, source_target_pairs={{0,1},{1,0},{2,3},{3,2},{4,5},{5,4},{6,7},{7,6},{8,9},{9,8},{10,11... | collective-permute-start | bytes 294920 | tf_op jit(solution)/shard_map/ppermute | solution.py:554
  17.8 1.0 %collective-permute-done.5.got_ref = bf16[8,4,8,192]{3,2,1,0:T(8,128)(2,1)S(1)} collective-permute-done((bf16[8,4,8,192]{3,2,1,0:T(8,128)(2,1)S(1)}, bf16[8,4,8,192]{3,2,1,0:T(8,128)(2,1)S(1)}, u32[]{:S(2)}, u32[]{:S(2)}) %collective-permute-start.5) | collective-permute-done | bytes 98336 | tf_op jit(solution)/shard_map/ppermute | solution.py:554
  18.7 0.8 %shard_map.89 = bf16[8,8,8,192]{3,2,1,0:T(8,128)(2,1)} custom-call(bf16[8,4,8,192]{3,2,1,0:T(8,128)(2,1)S(1)} %get-tuple-element.39.keep_ref, bf16[8,4,8,192]{3,2,1,0:T(8,128)(2,1)S(1)} %collective-permute-done.5.got_ref), custom_call_target="tpu_custom_call" | custom-call | tf_op jit(solution)/shard_map/pallas_call | solution.py:555
  (3 shorter events, 0.1 us)
Async XLA Ops:
  0.0 1.0 %copy-start.2 = (bf16[8,8,8,192]{3,2,1,0:T(8,128)(2,1)S(1)}, bf16[8,8,8,192]{3,2,1,0:T(8,128)(2,1)}, u32[]{:S(2)}) copy-start(bf16[8,8,8,192]{3,2,1,0:T(8,128)(2,1)} %raw.1) | copy-start | bytes 589828
  1.1 4.9 %collective-permute-start.1 = (bf16[36,8,384]{2,1,0:T(8,128)(2,1)S(1)}, bf16[36,8,384]{2,1,0:T(8,128)(2,1)S(1)}, u32[]{:S(2)}, u32[]{:S(2)}) collective-permute-start(bf16[36,8,384]{2,1,0:T(8,128)(2,1)S(1)} %get-tuple-element.28), channel_id=1, source_target_pairs={{0,1},{1,0},{2,3},{3,2},{4,5},{5,4},{6,7},{7,6},{8,9},{9,8},{10,11... | collective-permute-start | bytes 663560 | tf_op jit(solution)/shard_map/ppermute | solution.py:493
  1.6 11.3 %collective-permute-start = (bf16[17,8,384]{2,1,0:T(8,128)(2,1)S(1)}, bf16[17,8,384]{2,1,0:T(8,128)(2,1)S(1)}, u32[]{:S(2)}, u32[]{:S(2)}) collective-permute-start(bf16[17,8,384]{2,1,0:T(8,128)(2,1)S(1)} %get-tuple-element.26.tail_ref), channel_id=1, source_target_pairs={{0,8},{1,9},{2,10},{3,11},{4,12},{5,13},{6,14},{7,15},{16,24},{17,... | collective-permute-start | bytes 313352 | tf_op jit(solution)/shard_map/ppermute | solution.py:492
  6.1 5.0 %copy-start = (bf16[3,3,3,192,192]{4,3,2,1,0:T(8,128)(2,1)S(1)}, bf16[3,3,3,192,192]{4,3,2,1,0:T(8,128)(2,1)}, u32[]{:S(2)}) copy-start(bf16[3,3,3,192,192]{4,3,2,1,0:T(8,128)(2,1)} %w1_ref.5) | copy-start | bytes 5971972
  6.1 5.0 %copy-start.3 = (f32[192]{0:T(256)S(1)}, f32[192]{0:T(256)}, u32[]{:S(2)}) copy-start(f32[192]{0:T(256)} %param.10) | copy-start | bytes 2308
  6.1 5.0 %copy-start.4 = (f32[192]{0:T(256)S(1)}, f32[192]{0:T(256)}, u32[]{:S(2)}) copy-start(f32[192]{0:T(256)} %param.12) | copy-start | bytes 2308
  6.1 5.0 %copy-start.5 = (f32[192]{0:T(256)S(1)}, f32[192]{0:T(256)}, u32[]{:S(2)}) copy-start(f32[192]{0:T(256)} %param.13) | copy-start | bytes 2308
  6.2 7.0 %copy-start.1 = (bf16[3,3,3,192,192]{4,3,2,1,0:T(8,128)(2,1)S(1)}, bf16[3,3,3,192,192]{4,3,2,1,0:T(8,128)(2,1)}, u32[]{:S(2)}) copy-start(bf16[3,3,3,192,192]{4,3,2,1,0:T(8,128)(2,1)} %w2_ref.3) | copy-start | bytes 5971972
  6.2 7.0 %copy-start.6 = (f32[192]{0:T(256)S(1)}, f32[192]{0:T(256)}, u32[]{:S(2)}) copy-start(f32[192]{0:T(256)} %param.15) | copy-start | bytes 2308
  6.2 6.9 %collective-permute-start.4 = (bf16[2,8,8,384]{3,2,1,0:T(8,128)(2,1)S(1)}, bf16[2,8,8,384]{3,2,1,0:T(8,128)(2,1)S(1)}, u32[]{:S(2)}, u32[]{:S(2)}) collective-permute-start(bf16[2,8,8,384]{3,2,1,0:T(8,128)(2,1)S(1)} %get-tuple-element.34), channel_id=1, source_target_pairs={{0,3},{3,0},{8,11},{11,8},{2,5},{5,2},{10,13},{13,10},{4,7},{7,4},... | collective-permute-start | bytes 294920 | tf_op jit(solution)/shard_map/ppermute | solution.py:502
  9.7 5.5 %collective-permute-start.3 = (bf16[13,8,384]{2,1,0:T(8,128)(2,1)S(1)}, bf16[13,8,384]{2,1,0:T(8,128)(2,1)S(1)}, u32[]{:S(2)}, u32[]{:S(2)}) collective-permute-start(bf16[13,8,384]{2,1,0:T(8,128)(2,1)S(1)} %get-tuple-element.32), channel_id=1, source_target_pairs={{0,11},{3,8},{2,13},{5,10},{4,15},{7,12},{16,27},{19,24},{18,29},{... | collective-permute-start | bytes 239624 | tf_op jit(solution)/shard_map/ppermute | solution.py:503
  13.0 2.2 %collective-permute-start.2 = (bf16[12,8,384]{2,1,0:T(8,128)(2,1)S(1)}, bf16[12,8,384]{2,1,0:T(8,128)(2,1)S(1)}, u32[]{:S(2)}, u32[]{:S(2)}) collective-permute-start(bf16[12,8,384]{2,1,0:T(8,128)(2,1)S(1)} %get-tuple-element.31), channel_id=1, source_target_pairs={{0,1},{1,0},{2,3},{3,2},{4,5},{5,4},{6,7},{7,6},{8,9},{9,8},{10,11... | collective-permute-start | bytes 221192 | tf_op jit(solution)/shard_map/ppermute | solution.py:526
  17.2 1.5 %collective-permute-start.5 = (bf16[8,4,8,192]{3,2,1,0:T(8,128)(2,1)S(1)}, bf16[8,4,8,192]{3,2,1,0:T(8,128)(2,1)S(1)}, u32[]{:S(2)}, u32[]{:S(2)}) collective-permute-start(bf16[8,4,8,192]{3,2,1,0:T(8,128)(2,1)S(1)} %get-tuple-element.40), channel_id=1, source_target_pairs={{0,1},{1,0},{2,3},{3,2},{4,5},{5,4},{6,7},{7,6},{8,9},{9,8},{10,11... | collective-permute-start | bytes 294920 | tf_op jit(solution)/shard_map/ppermute | solution.py:554

commit v5 on v3

--- a/solution.py
+++ b/solution.py
@@ -128,23 +128,42 @@
     waiting[1](waiting[0])
 
 
-def convolved(operand, weights_ref, bias_ref, frame, frames, rows, then, most=PRODUCT):
+def convolved(operand, weights, bias_ref, frame, frames, rows, then, most=PRODUCT):
     products = -(-frames * rows * operand.shape[3] // most)
     step = -(-frames // products)
 
     def part(start):
         count = min(step, frames - start)
         return (
-            lambda: convolved_part(operand, weights_ref, bias_ref, frame + start, count, rows),
+            lambda: convolved_part(operand, weights, bias_ref, frame + start, count, rows),
             lambda result: then(start, count, result),
         )
 
     return [part(start) for start in range(0, frames, step)]
 
 
-def convolved_part(operand, weights_ref, bias_ref, frame, frames, rows):
+def operand_of(weights_ref):
+    made = {}
+
+    def weights(groups, j, depth):
+        key = (groups[0][0], j)
+        if key not in made:
+            rights = []
+            for group in groups:
+                held = [weights_ref[a, i, j] for a, i in group]
+                rights += [weight[:LANES] for weight in held] + [weight[LANES:] for weight in held]
+            rest = depth - sum(right.shape[0] for right in rights)
+            if rest:
+                rights.append(jnp.zeros((rest, weights_ref.shape[-1]), jnp.bfloat16))
+            made[key] = jnp.concatenate(rights, axis=0)
+        return made[key]
+
+    return weights
+
+
+def convolved_part(operand, weights, bias_ref, frame, frames, rows):
     width = operand.shape[3]
-    channels = weights_ref.shape[-1]
+    channels = bias_ref.shape[-1]
     taps = [(a, i) for a in range(TAPS) for i in range(TAPS)]
     groups = [taps[start:start + 2] for start in range(0, len(taps), 2)]
 
@@ -160,16 +179,6 @@
             high = window(group[0], 1)
             pieces.append(high + window(group[1], 2) if len(group) > 1 else high)
         return jnp.concatenate(pieces, axis=-1)
-
-    def weights(groups, j, depth):
-        rights = []
-        for group in groups:
-            held = [weights_ref[a, i, j] for a, i in group]
-            rights += [weight[:LANES] for weight in held] + [weight[LANES:] for weight in held]
-        rest = depth - sum(right.shape[0] for right in rights)
-        if rest:
-            rights.append(jnp.zeros((rest, channels), jnp.bfloat16))
-        return jnp.concatenate(rights, axis=0)
 
     half = len(groups) // 2
     parts = [(part, operands(part)) for part in (groups[:half], groups[half:])]
@@ -243,14 +252,14 @@
                     target(first + frame, 2 * k + row, kept.astype(jnp.bfloat16))
 
 
-def hide(operand, weights_ref, bias_ref, gain_ref, first, count, rows, flags, store, most=PRODUCT):
-    channels = weights_ref.shape[-1]
+def hide(operand, weights, bias_ref, gain_ref, first, count, rows, flags, store, most=PRODUCT):
+    channels = bias_ref.shape[-1]
 
     def then(begin, part, hidden):
         flag = jnp.concatenate(flags[begin:begin + part], axis=0)
         store(begin, begin + part, second_rows(hidden, flag, gain_ref, channels))
 
-    return convolved(operand, weights_ref, bias_ref, first, count, rows, then, most)
+    return convolved(operand, weights, bias_ref, first, count, rows, then, most)
 
 
 def inside_flags(rows):
@@ -280,7 +289,7 @@
     def store(begin, end, rows):
         late_ref[:, begin:end] = rows
 
-    steps = hide(first_ref, w1_ref, bias1_ref, gain2_ref, 0, frames - 2, 2 * pairs - 2, live, store, 2 * PRODUCT // 3)
+    steps = hide(first_ref, operand_of(w1_ref), bias1_ref, gain2_ref, 0, frames - 2, 2 * pairs - 2, live, store, 2 * PRODUCT // 3)
     each = -(-(frames - 2) // len(steps))
 
     def filled(k, product):
@@ -325,10 +334,11 @@
 
     flags = [flag * inside for flag in live[2:]]
     middle, border = finished(2 * (1 - core), 1, pairs - 2), finished((rows - 4) * core, (pairs - 1) * core, 1)
+    second = operand_of(w2_ref)
     in_turn(
-        hide(strip, w1_ref, bias1_ref, gain2_ref, 0, frames - 2, 2, flags, store)
-        + convolved(late_ref, w2_ref, bias2_ref, 0, late, rows - 4, middle)
-        + convolved(operand, w2_ref, bias2_ref, 0, late, 2, border)
+        hide(strip, operand_of(w1_ref), bias1_ref, gain2_ref, 0, frames - 2, 2, flags, store)
+        + convolved(late_ref, second, bias2_ref, 0, late, rows - 4, middle)
+        + convolved(operand, second, bias2_ref, 0, late, 2, border)
     )
     strip_ref[...] = strip[:, 0:2, outward]
     hidden_ref[:, :, pl.ds(2 * (1 - core), rows - 2)] = late_ref[:, 0:2]
@@ -361,7 +371,7 @@
             operand[:, first + begin:first + end] = values
 
         flags = [flag * inside for flag in flags]
-        in_turn(hide(plane, w1_ref, bias1_ref, gain2_ref, first, CACHE - first, rows, flags, store))
+        in_turn(hide(plane, operand_of(w1_ref), bias1_ref, gain2_ref, first, CACHE - first, rows, flags, store))
 
     @pl.when(earlier)
     def _():
@@ -385,7 +395,7 @@
     def then(start, part, result):
         finish(mine_ref, other_ref, live, start, (core, held - 1), result, (put(keep_ref), put(send_ref)))
 
-    in_turn(convolved(operand, w2_ref, bias2_ref, 0, CACHE, rows - 2, then))
+    in_turn(convolved(operand, operand_of(w2_ref), bias2_ref, 0, CACHE, rows - 2, then))
     keep_ref[CACHE:] = late_keep_ref[...]
     send_ref[CACHE:] = late_send_ref[...]
 

time: 19.4 us -> 19.4 us (level)
  no operation moved by 1% of the time
where the time goes in v5:
time: 19.4 us; the launch traced here: 19.2 us
  starting transfers between devices  10.4 us (54%)
  Pallas kernels  6.61 us (34%)
  waiting for transfers between devices  1 us (5%)
  between operations  0.91 us (5%)
  local copies, waits for them, and re-layouts  0.31 us (2%)
    ppermute x1, starting transfers between devices, shards(): tail_mine = lax.ppermute(tail, axes, straight)  4.41 us
    ppermute x1, starting transfers between devices, shards(): own_edge = lax.ppermute(own_edge, axes, across)  3.56 us
    pallas_call x1, Pallas kernels, shards(): pl.pallas_call(edge_kernel, out_shape=(shape(3, 2, 2, width, LANES), shap...  1.97 us
    pallas_call x1, Pallas kernels, shards(): pl.pallas_call(early_kernel, out_shape=(shape(frames, half, side, channel...  1.91 us
    pallas_call x1, Pallas kernels, shards(): pl.pallas_call(own_kernel, out_shape=(shape(3, frames, half + 2, width, L...  1.82 us
    ppermute x1, starting transfers between devices, shards(): tail_edge = lax.ppermute(tail_edge, axes, diagonal)  1.29 us
    ppermute x1, waiting for transfers between devices, shards(): got = lax.ppermute(send, 'wa', swap)  0.99 us
    pallas_call x1, Pallas kernels, shards(): pl.pallas_call(place_kernel, out_shape=shape(*features.shape), in_specs=[...  0.71 us
  transfers between devices with their start and end apart: 6, of which 1 were waited for; matrix products, arithmetic and copies ran while one was open for 0% of the time, Pallas kernels for 20%

profile of v5, /device:TPU:0, one launch (start us, length us, event | category | flops | bytes accessed | tf_op | source)
XLA Modules:
  0.0 19.2 jit_solution(6180095252611126673)
XLA Ops:
  0.0 0.0 copy-start.2
  0.7 0.3 %copy-done.2 = bf16[8,8,8,192]{3,2,1,0:T(8,128)(2,1)S(1)} copy-done((bf16[8,8,8,192]{3,2,1,0:T(8,128)(2,1)S(1)}, bf16[8,8,8,192]{3,2,1,0:T(8,128)(2,1)}, u32[]{:S(2)}) %copy-start.2) | copy-done | bytes 196632
  1.0 0.1 shard_map.83
  1.1 0.5 %collective-permute-start.1 = (bf16[36,8,384]{2,1,0:T(8,128)(2,1)S(1)}, bf16[36,8,384]{2,1,0:T(8,128)(2,1)S(1)}, u32[]{:S(2)}, u32[]{:S(2)}) collective-permute-start(bf16[36,8,384]{2,1,0:T(8,128)(2,1)S(1)} %get-tuple-element.26), channel_id=1, source_target_pairs={{0,1},{1,0},{2,3},{3,2},{4,5},{5,4},{6,7},{7,6},{8,9},{9,8},{10,11... | collective-permute-start | bytes 663560 | tf_op jit(solution)/shard_map/ppermute | solution.py:477
  1.6 4.4 %collective-permute-start = (bf16[17,8,384]{2,1,0:T(8,128)(2,1)S(1)}, bf16[17,8,384]{2,1,0:T(8,128)(2,1)S(1)}, u32[]{:S(2)}, u32[]{:S(2)}) collective-permute-start(bf16[17,8,384]{2,1,0:T(8,128)(2,1)S(1)} %get-tuple-element.24.tail_ref), channel_id=1, source_target_pairs={{0,8},{1,9},{2,10},{3,11},{4,12},{5,13},{6,14},{7,15},{16,24},{17,... | collective-permute-start | bytes 313352 | tf_op jit(solution)/shard_map/ppermute | solution.py:476
  6.1 0.0 collective-permute-done.1.other_ref
  6.1 0.0 copy-start
  6.1 0.0 copy-start.3
  6.1 0.0 copy-start.4
  6.1 0.0 copy-start.5
  6.2 0.0 copy-start.1
  6.2 0.0 copy-start.6
  6.2 3.6 %collective-permute-start.4 = (bf16[2,8,8,384]{3,2,1,0:T(8,128)(2,1)S(1)}, bf16[2,8,8,384]{3,2,1,0:T(8,128)(2,1)S(1)}, u32[]{:S(2)}, u32[]{:S(2)}) collective-permute-start(bf16[2,8,8,384]{3,2,1,0:T(8,128)(2,1)S(1)} %get-tuple-element.30), channel_id=1, source_target_pairs={{0,3},{3,0},{8,11},{11,8},{2,5},{5,2},{10,13},{13,10},{4,7},{7,4},... | collective-permute-start | bytes 294920 | tf_op jit(solution)/shard_map/ppermute | solution.py:486
  9.7 1.3 %collective-permute-start.3 = (bf16[13,8,384]{2,1,0:T(8,128)(2,1)S(1)}, bf16[13,8,384]{2,1,0:T(8,128)(2,1)S(1)}, u32[]{:S(2)}, u32[]{:S(2)}) collective-permute-start(bf16[13,8,384]{2,1,0:T(8,128)(2,1)S(1)} %get-tuple-element.28), channel_id=1, source_target_pairs={{0,11},{3,8},{2,13},{5,10},{4,15},{7,12},{16,27},{19,24},{18,29},{... | collective-permute-start | bytes 239624 | tf_op jit(solution)/shard_map/ppermute | solution.py:487
  11.0 0.0 copy-done
  11.1 0.0 copy-done.3
  11.1 0.0 copy-done.4
  11.1 0.0 copy-done.5
  11.1 1.8 %shard_map.84 = (bf16[3,8,6,16,128]{4,3,2,1,0:T(8,128)(2,1)S(1)}, bf16[3,6,4,16,128]{4,3,2,1,0:T(8,128)(2,1)S(1)}) custom-call(bf16[8,384]{1,0:T(8,128)(2,1)S(1)} %get-tuple-element.23.marks_ref, bf16[8,3,8,384]{3,2,1,0:T(8,128)(2,1)S(1)} %get-tuple-element.25.mine_ref, bf16[36,8,384]{2,1,0:T(8,128)(2,1)S(1)} %collective-permute-done.1.other_ref, ...), custom_call_target="tpu_custom_call" | custom-call | flops 764411904 | bytes 4194304 | tf_op jit(solution)/shard_map/pallas_call | solution.py:493
  12.9 0.0 collective-permute-done.tail_ref.tail_mine_ref
  12.9 0.1 collective-permute-start.2
  13.0 0.0 collective-permute-done.4.edge_ref
  13.0 0.0 copy-done.1
  13.0 0.0 copy-done.6
  13.1 2.0 %shard_map.87 = (bf16[3,2,2,16,128]{4,3,2,1,0:T(8,128)(2,1)S(1)}, bf16[3,2,6,16,128]{4,3,2,1,0:T(8,128)(2,1)S(1)}, bf16[4,4,8,192]{3,2,1,0:T(8,128)(2,1)S(1)}, bf16[4,4,8,192]{3,2,1,0:T(8,128)(2,1)S(1)}) custom-call(bf16[8,384]{1,0:T(8,128)(2,1)S(1)} %get-tuple-element.23.marks_ref, bf16[8,3,8,384]{3,2,1,0:T(8,128)(2,1)S(1)} %get-tuple-element.25.mine_ref, ...), custom_call_target="tpu_custom_call" | custom-call | flops 1048576 | bytes 1048576 | tf_op jit(solution)/shard_map/pallas_call | solution.py:510
  15.0 0.0 collective-permute-done.2.tail_other_ref
  15.0 0.0 collective-permute-done.3.edge_ref
  15.1 1.9 %shard_map.88 = (bf16[8,4,8,192]{3,2,1,0:T(8,128)(2,1)S(1)}, bf16[8,4,8,192]{3,2,1,0:T(8,128)(2,1)S(1)}) custom-call(bf16[8,384]{1,0:T(8,128)(2,1)S(1)} %get-tuple-element.23.marks_ref, bf16[17,8,384]{2,1,0:T(8,128)(2,1)S(1)} %collective-permute-done.tail_ref.tail_mine_ref, bf16[12,8,384]{2,1,0:T(8,128)(2,1)S(1)} %collective-permute-done.2.tail_other_ref, ...), custom_call_target="tpu_custom_call" | custom-call | flops 1274019840 | bytes 8388608 | tf_op jit(solution)/shard_map/pallas_call | solution.py:525
  17.0 0.5 %collective-permute-start.5 = (bf16[8,4,8,192]{3,2,1,0:T(8,128)(2,1)S(1)}, bf16[8,4,8,192]{3,2,1,0:T(8,128)(2,1)S(1)}, u32[]{:S(2)}, u32[]{:S(2)}) collective-permute-start(bf16[8,4,8,192]{3,2,1,0:T(8,128)(2,1)S(1)} %get-tuple-element.36), channel_id=1, source_target_pairs={{0,1},{1,0},{2,3},{3,2},{4,5},{5,4},{6,7},{7,6},{8,9},{9,8},{10,11... | collective-permute-start | bytes 294920 | tf_op jit(solution)/shard_map/ppermute | solution.py:537
  17.5 1.0 %collective-permute-done.5.got_ref = bf16[8,4,8,192]{3,2,1,0:T(8,128)(2,1)S(1)} collective-permute-done((bf16[8,4,8,192]{3,2,1,0:T(8,128)(2,1)S(1)}, bf16[8,4,8,192]{3,2,1,0:T(8,128)(2,1)S(1)}, u32[]{:S(2)}, u32[]{:S(2)}) %collective-permute-start.5) | collective-permute-done | bytes 98336 | tf_op jit(solution)/shard_map/ppermute | solution.py:537
  18.5 0.7 %shard_map.89 = bf16[8,8,8,192]{3,2,1,0:T(8,128)(2,1)} custom-call(bf16[8,4,8,192]{3,2,1,0:T(8,128)(2,1)S(1)} %get-tuple-element.35.keep_ref, bf16[8,4,8,192]{3,2,1,0:T(8,128)(2,1)S(1)} %collective-permute-done.5.got_ref), custom_call_target="tpu_custom_call" | custom-call | tf_op jit(solution)/shard_map/pallas_call | solution.py:538
  (3 shorter events, 0.0 us)
Async XLA Ops:
  0.0 1.0 %copy-start.2 = (bf16[8,8,8,192]{3,2,1,0:T(8,128)(2,1)S(1)}, bf16[8,8,8,192]{3,2,1,0:T(8,128)(2,1)}, u32[]{:S(2)}) copy-start(bf16[8,8,8,192]{3,2,1,0:T(8,128)(2,1)} %raw.1) | copy-start | bytes 589828
  1.1 4.9 %collective-permute-start.1 = (bf16[36,8,384]{2,1,0:T(8,128)(2,1)S(1)}, bf16[36,8,384]{2,1,0:T(8,128)(2,1)S(1)}, u32[]{:S(2)}, u32[]{:S(2)}) collective-permute-start(bf16[36,8,384]{2,1,0:T(8,128)(2,1)S(1)} %get-tuple-element.26), channel_id=1, source_target_pairs={{0,1},{1,0},{2,3},{3,2},{4,5},{5,4},{6,7},{7,6},{8,9},{9,8},{10,11... | collective-permute-start | bytes 663560 | tf_op jit(solution)/shard_map/ppermute | solution.py:477
  1.6 11.3 %collective-permute-start = (bf16[17,8,384]{2,1,0:T(8,128)(2,1)S(1)}, bf16[17,8,384]{2,1,0:T(8,128)(2,1)S(1)}, u32[]{:S(2)}, u32[]{:S(2)}) collective-permute-start(bf16[17,8,384]{2,1,0:T(8,128)(2,1)S(1)} %get-tuple-element.24.tail_ref), channel_id=1, source_target_pairs={{0,8},{1,9},{2,10},{3,11},{4,12},{5,13},{6,14},{7,15},{16,24},{17,... | collective-permute-start | bytes 313352 | tf_op jit(solution)/shard_map/ppermute | solution.py:476
  6.1 5.0 %copy-start = (bf16[3,3,3,192,192]{4,3,2,1,0:T(8,128)(2,1)S(1)}, bf16[3,3,3,192,192]{4,3,2,1,0:T(8,128)(2,1)}, u32[]{:S(2)}) copy-start(bf16[3,3,3,192,192]{4,3,2,1,0:T(8,128)(2,1)} %w1_ref.5) | copy-start | bytes 5971972
  6.1 5.0 %copy-start.3 = (f32[192]{0:T(256)S(1)}, f32[192]{0:T(256)}, u32[]{:S(2)}) copy-start(f32[192]{0:T(256)} %param.10) | copy-start | bytes 2308
  6.1 5.0 %copy-start.4 = (f32[192]{0:T(256)S(1)}, f32[192]{0:T(256)}, u32[]{:S(2)}) copy-start(f32[192]{0:T(256)} %param.12) | copy-start | bytes 2308
  6.1 5.0 %copy-start.5 = (f32[192]{0:T(256)S(1)}, f32[192]{0:T(256)}, u32[]{:S(2)}) copy-start(f32[192]{0:T(256)} %param.13) | copy-start | bytes 2308
  6.2 6.9 %copy-start.1 = (bf16[3,3,3,192,192]{4,3,2,1,0:T(8,128)(2,1)S(1)}, bf16[3,3,3,192,192]{4,3,2,1,0:T(8,128)(2,1)}, u32[]{:S(2)}) copy-start(bf16[3,3,3,192,192]{4,3,2,1,0:T(8,128)(2,1)} %w2_ref.3) | copy-start | bytes 5971972
  6.2 6.9 %copy-start.6 = (f32[192]{0:T(256)S(1)}, f32[192]{0:T(256)}, u32[]{:S(2)}) copy-start(f32[192]{0:T(256)} %param.15) | copy-start | bytes 2308
  6.2 6.9 %collective-permute-start.4 = (bf16[2,8,8,384]{3,2,1,0:T(8,128)(2,1)S(1)}, bf16[2,8,8,384]{3,2,1,0:T(8,128)(2,1)S(1)}, u32[]{:S(2)}, u32[]{:S(2)}) collective-permute-start(bf16[2,8,8,384]{3,2,1,0:T(8,128)(2,1)S(1)} %get-tuple-element.30), channel_id=1, source_target_pairs={{0,3},{3,0},{8,11},{11,8},{2,5},{5,2},{10,13},{13,10},{4,7},{7,4},... | collective-permute-start | bytes 294920 | tf_op jit(solution)/shard_map/ppermute | solution.py:486
  9.7 5.3 %collective-permute-start.3 = (bf16[13,8,384]{2,1,0:T(8,128)(2,1)S(1)}, bf16[13,8,384]{2,1,0:T(8,128)(2,1)S(1)}, u32[]{:S(2)}, u32[]{:S(2)}) collective-permute-start(bf16[13,8,384]{2,1,0:T(8,128)(2,1)S(1)} %get-tuple-element.28), channel_id=1, source_target_pairs={{0,11},{3,8},{2,13},{5,10},{4,15},{7,12},{16,27},{19,24},{18,29},{... | collective-permute-start | bytes 239624 | tf_op jit(solution)/shard_map/ppermute | solution.py:487
  12.9 2.1 %collective-permute-start.2 = (bf16[12,8,384]{2,1,0:T(8,128)(2,1)S(1)}, bf16[12,8,384]{2,1,0:T(8,128)(2,1)S(1)}, u32[]{:S(2)}, u32[]{:S(2)}) collective-permute-start(bf16[12,8,384]{2,1,0:T(8,128)(2,1)S(1)} %shard_map.85), channel_id=1, source_target_pairs={{0,1},{1,0},{2,3},{3,2},{4,5},{5,4},{6,7},{7,6},{8,9},{9,8},{10,11... | collective-permute-start | bytes 221192 | tf_op jit(solution)/shard_map/ppermute | solution.py:509
  17.0 1.5 %collective-permute-start.5 = (bf16[8,4,8,192]{3,2,1,0:T(8,128)(2,1)S(1)}, bf16[8,4,8,192]{3,2,1,0:T(8,128)(2,1)S(1)}, u32[]{:S(2)}, u32[]{:S(2)}) collective-permute-start(bf16[8,4,8,192]{3,2,1,0:T(8,128)(2,1)S(1)} %get-tuple-element.36), channel_id=1, source_target_pairs={{0,1},{1,0},{2,3},{3,2},{4,5},{5,4},{6,7},{7,6},{8,9},{9,8},{10,11... | collective-permute-start | bytes 294920 | tf_op jit(solution)/shard_map/ppermute | solution.py:537

commit v6 on v3

--- a/solution.py
+++ b/solution.py
@@ -214,8 +214,6 @@
     for slot in range(CACHE):
         tail_edge_ref[slot] = tail_ref[slot * pairs + core * (pairs - 1)]
         tail_edge_ref[CACHE + slot] = other_ref[slot * held + pair]
-    spare = tail_edge_ref.shape[0] - 2 * CACHE
-    tail_edge_ref[2 * CACHE:] = jnp.zeros((spare,) + tail_edge_ref.shape[1:], tail_edge_ref.dtype)
     for frame in range(frames):
         own_edge_ref[0, frame] = mine_ref[frame, pair]
         own_edge_ref[1, frame] = other_ref[(CACHE + frame) * held + pair]
@@ -335,8 +333,20 @@
     hidden_ref[:, :, pl.ds((rows - 2) * core, 2)] = operand[:, 0:2, outward]
 
 
+def tail_edge_kernel(edge_ref, strip_ref, gain_ref, rows_ref):
+    rows_ref[:, CACHE:] = strip_ref[...]
+
+    @pl.when(lax.axis_index("tchunk") > 0)
+    def _():
+        fill_rows(rows_ref, 0, 0, edge_ref[CACHE:2 * CACHE][:, None], edge_ref[0:CACHE][:, None], gain_ref)
+
+    @pl.when(lax.axis_index("tchunk") == 0)
+    def _():
+        rows_ref[:, 0:CACHE] = jnp.zeros((rows_ref.shape[0], CACHE) + rows_ref.shape[2:], rows_ref.dtype)
+
+
 def early_kernel(
-    marks_ref, tail_mine_ref, tail_other_ref, mine_ref, other_ref, edge_ref, first_ref, strip_ref, hidden_ref,
+    marks_ref, tail_mine_ref, tail_other_ref, mine_ref, other_ref, edge_ref, first_ref, hidden_ref,
     late_keep_ref, late_send_ref, gain1_ref, w1_ref, bias1_ref, gain2_ref, w2_ref, bias2_ref,
     keep_ref, send_ref, plane, operand,
 ):
@@ -353,7 +363,7 @@
         return jnp.stack([ref[pl.ds(slot * stride + first, held)] for slot in range(CACHE)])
 
     plane[:, CACHE:, pl.ds(middle, rows)] = first_ref[:, 0:2]
-    plane[:, CACHE:, pl.ds(border, 2)] = strip_ref[...]
+    plane[:, :, pl.ds(border, 2)] = edge_ref[...]
     operand[:, CACHE:] = hidden_ref[...]
 
     def fill(first, flags):
@@ -367,13 +377,13 @@
     def _():
         mine = unpacked(tail_mine_ref, pairs, core * (pairs - held))
         fill_rows(plane, 0, middle, mine, unpacked(tail_other_ref, held, 0), gain1_ref)
-        mine, other = edge_ref[CACHE:2 * CACHE], edge_ref[0:CACHE]
-        fill_rows(plane, 0, border, mine[:, None], other[:, None], gain1_ref)
         fill(0, frame_flags(tail_mine_ref[CACHE * pairs], range(CACHE - 2, CACHE)) + live[0:2])
 
     @pl.when(jnp.logical_not(earlier))
     def _():
-        plane[:, 0:CACHE] = jnp.zeros(plane.shape[:1] + (CACHE,) + plane.shape[2:], plane.dtype)
+        plane[:, 0:CACHE, pl.ds(middle, rows)] = jnp.zeros(
+            plane.shape[:1] + (CACHE, rows) + plane.shape[3:], plane.dtype
+        )
         operand[:, 0:2] = jnp.zeros(operand.shape[:1] + (2,) + operand.shape[2:], operand.dtype)
         fill(2, live[0:2])
 
@@ -467,7 +477,7 @@
     other = lax.ppermute(theirs, "wa", swap)
     tail_edge, own_edge = pl.pallas_call(
         border_kernel,
-        out_shape=(shape(tiles + 1, side, packed), shape(2, frames, side, packed)),
+        out_shape=(shape(2 * CACHE, side, packed), shape(2, frames, side, packed)),
         in_specs=[vmem] * 3,
         out_specs=(vmem, vmem),
         compiler_params=limit,
@@ -512,10 +522,18 @@
         compiler_params=limit,
         cost_estimate=cost(2**20, 2**20),
     )(marks, mine, other, own_edge, first, late, *weights)
+    tail_edge = pl.pallas_call(
+        tail_edge_kernel,
+        out_shape=shape(3, CACHE + 2, 2, width, LANES),
+        in_specs=[vmem] * 3,
+        out_specs=vmem,
+        compiler_params=limit,
+        cost_estimate=cost(2**30, 2**18),
+    )(tail_edge, strip, weights[0])
     keep, send = pl.pallas_call(
         early_kernel,
         out_shape=(shape(frames, half, side, channels), shape(frames, half, side, channels)),
-        in_specs=[vmem] * 17,
+        in_specs=[vmem] * 16,
         out_specs=(vmem, vmem),
         scratch_shapes=[
             pltpu.VMEM((3, CACHE + 2, half + 4, width, LANES), bf16),
@@ -523,7 +541,7 @@
         ],
         compiler_params=limit,
         cost_estimate=cost(work * CACHE * (2 * half + 2), 8 * 2**20),
-    )(marks, tail_mine, tail_other, mine, other, tail_edge, first, strip, hidden, keep, send, *weights)
+    )(marks, tail_mine, tail_other, mine, other, tail_edge, first, hidden, keep, send, *weights)
     got = lax.ppermute(send, "wa", swap)
     return pl.pallas_call(
         place_kernel,

time: 19.4 us -> 19.5 us (level)
  no operation moved by 1% of the time
where the time goes in v6:
time: 19.5 us; the launch traced here: 19.3 us
  starting transfers between devices  10.4 us (53%)
  Pallas kernels  6.68 us (34%)
  waiting for transfers between devices  1 us (5%)
  between operations  0.91 us (5%)
  local copies, waits for them, and re-layouts  0.31 us (2%)
    ppermute x1, starting transfers between devices, shards(): tail_mine = lax.ppermute(tail, axes, straight)  4.41 us
    ppermute x1, starting transfers between devices, shards(): own_edge = lax.ppermute(own_edge, axes, across)  3.56 us
    pallas_call x1, Pallas kernels, shards(): pl.pallas_call(edge_kernel, out_shape=(shape(3, 2, 2, width, LANES), shap...  1.99 us
    pallas_call x1, Pallas kernels, shards(): pl.pallas_call(early_kernel, out_shape=(shape(frames, half, side, channel...  1.92 us
    pallas_call x1, Pallas kernels, shards(): pl.pallas_call(own_kernel, out_shape=(shape(3, frames, half + 2, width, L...  1.83 us
    ppermute x1, starting transfers between devices, shards(): tail_edge = lax.ppermute(tail_edge, axes, diagonal)  1.29 us
    ppermute x1, waiting for transfers between devices, shards(): got = lax.ppermute(send, 'wa', swap)  0.99 us
    pallas_call x1, Pallas kernels, shards(): pl.pallas_call(place_kernel, out_shape=shape(*features.shape), in_specs=[...  0.71 us
  transfers between devices with their start and end apart: 6, of which 1 were waited for; matrix products, arithmetic and copies ran while one was open for 0% of the time, Pallas kernels for 20%

profile of v6, /device:TPU:0, one launch (start us, length us, event | category | flops | bytes accessed | tf_op | source)
XLA Modules:
  0.0 19.3 jit_solution(1106088133481435502)
XLA Ops:
  0.0 0.0 copy-start.2
  0.7 0.3 %copy-done.2 = bf16[8,8,8,192]{3,2,1,0:T(8,128)(2,1)S(1)} copy-done((bf16[8,8,8,192]{3,2,1,0:T(8,128)(2,1)S(1)}, bf16[8,8,8,192]{3,2,1,0:T(8,128)(2,1)}, u32[]{:S(2)}) %copy-start.2) | copy-done | bytes 196632
  1.0 0.1 shard_map.83
  1.1 0.5 %collective-permute-start.1 = (bf16[36,8,384]{2,1,0:T(8,128)(2,1)S(1)}, bf16[36,8,384]{2,1,0:T(8,128)(2,1)S(1)}, u32[]{:S(2)}, u32[]{:S(2)}) collective-permute-start(bf16[36,8,384]{2,1,0:T(8,128)(2,1)S(1)} %get-tuple-element.26), channel_id=1, source_target_pairs={{0,1},{1,0},{2,3},{3,2},{4,5},{5,4},{6,7},{7,6},{8,9},{9,8},{10,11... | collective-permute-start | bytes 663560 | tf_op jit(solution)/shard_map/ppermute | solution.py:477
  1.6 4.4 %collective-permute-start = (bf16[17,8,384]{2,1,0:T(8,128)(2,1)S(1)}, bf16[17,8,384]{2,1,0:T(8,128)(2,1)S(1)}, u32[]{:S(2)}, u32[]{:S(2)}) collective-permute-start(bf16[17,8,384]{2,1,0:T(8,128)(2,1)S(1)} %get-tuple-element.24.tail_ref), channel_id=1, source_target_pairs={{0,8},{1,9},{2,10},{3,11},{4,12},{5,13},{6,14},{7,15},{16,24},{17,... | collective-permute-start | bytes 313352 | tf_op jit(solution)/shard_map/ppermute | solution.py:476
  6.1 0.0 collective-permute-done.1.other_ref
  6.1 0.0 copy-start
  6.1 0.0 copy-start.3
  6.1 0.0 copy-start.4
  6.1 0.0 copy-start.5
  6.2 0.0 copy-start.1
  6.2 0.0 copy-start.6
  6.2 3.6 %collective-permute-start.4 = (bf16[2,8,8,384]{3,2,1,0:T(8,128)(2,1)S(1)}, bf16[2,8,8,384]{3,2,1,0:T(8,128)(2,1)S(1)}, u32[]{:S(2)}, u32[]{:S(2)}) collective-permute-start(bf16[2,8,8,384]{3,2,1,0:T(8,128)(2,1)S(1)} %get-tuple-element.29), channel_id=1, source_target_pairs={{0,3},{3,0},{8,11},{11,8},{2,5},{5,2},{10,13},{13,10},{4,7},{7,4},... | collective-permute-start | bytes 294920 | tf_op jit(solution)/shard_map/ppermute | solution.py:486
  9.7 1.3 %collective-permute-start.3 = (bf16[8,8,384]{2,1,0:T(8,128)(2,1)S(1)}, bf16[8,8,384]{2,1,0:T(8,128)(2,1)S(1)}, u32[]{:S(2)}, u32[]{:S(2)}) collective-permute-start(bf16[8,8,384]{2,1,0:T(8,128)(2,1)S(1)} %get-tuple-element.28), channel_id=1, source_target_pairs={{0,11},{3,8},{2,13},{5,10},{4,15},{7,12},{16,27},{19,24},{18,29},{... | collective-permute-start | bytes 147464 | tf_op jit(solution)/shard_map/ppermute | solution.py:487
  11.0 0.0 copy-done
  11.0 0.0 copy-done.3
  11.1 0.0 copy-done.4
  11.1 0.0 copy-done.5
  11.1 1.8 %shard_map.84 = (bf16[3,8,6,16,128]{4,3,2,1,0:T(8,128)(2,1)S(1)}, bf16[3,6,4,16,128]{4,3,2,1,0:T(8,128)(2,1)S(1)}) custom-call(bf16[8,384]{1,0:T(8,128)(2,1)S(1)} %get-tuple-element.23.marks_ref, bf16[8,3,8,384]{3,2,1,0:T(8,128)(2,1)S(1)} %get-tuple-element.25.mine_ref, bf16[36,8,384]{2,1,0:T(8,128)(2,1)S(1)} %collective-permute-done.1.other_ref, ...), custom_call_target="tpu_custom_call" | custom-call | flops 764411904 | bytes 4194304 | tf_op jit(solution)/shard_map/pallas_call | solution.py:493
  12.9 0.0 collective-permute-done.tail_ref.tail_mine_ref
  12.9 0.1 collective-permute-start.2
  13.0 0.0 collective-permute-done.4.edge_ref
  13.0 0.0 copy-done.1
  13.0 0.0 copy-done.6
  13.1 2.0 %shard_map.87 = (bf16[3,2,2,16,128]{4,3,2,1,0:T(8,128)(2,1)S(1)}, bf16[3,2,6,16,128]{4,3,2,1,0:T(8,128)(2,1)S(1)}, bf16[4,4,8,192]{3,2,1,0:T(8,128)(2,1)S(1)}, bf16[4,4,8,192]{3,2,1,0:T(8,128)(2,1)S(1)}) custom-call(bf16[8,384]{1,0:T(8,128)(2,1)S(1)} %get-tuple-element.23.marks_ref, bf16[8,3,8,384]{3,2,1,0:T(8,128)(2,1)S(1)} %get-tuple-element.25.mine_ref, ...), custom_call_target="tpu_custom_call" | custom-call | flops 1048576 | bytes 1048576 | tf_op jit(solution)/shard_map/pallas_call | solution.py:510
  15.1 0.0 collective-permute-done.3.edge_ref
  15.1 0.0 collective-permute-done.2.tail_other_ref
  15.1 1.9 %shard_map.89 = (bf16[8,4,8,192]{3,2,1,0:T(8,128)(2,1)S(1)}, bf16[8,4,8,192]{3,2,1,0:T(8,128)(2,1)S(1)}) custom-call(bf16[8,384]{1,0:T(8,128)(2,1)S(1)} %get-tuple-element.23.marks_ref, bf16[17,8,384]{2,1,0:T(8,128)(2,1)S(1)} %collective-permute-done.tail_ref.tail_mine_ref, bf16[12,8,384]{2,1,0:T(8,128)(2,1)S(1)} %collective-permute-done.2.tail_other_ref, ...), custom_call_target="tpu_custom_call" | custom-call | flops 1274019840 | bytes 8388608 | tf_op jit(solution)/shard_map/pallas_call | solution.py:533
  17.0 0.5 %collective-permute-start.5 = (bf16[8,4,8,192]{3,2,1,0:T(8,128)(2,1)S(1)}, bf16[8,4,8,192]{3,2,1,0:T(8,128)(2,1)S(1)}, u32[]{:S(2)}, u32[]{:S(2)}) collective-permute-start(bf16[8,4,8,192]{3,2,1,0:T(8,128)(2,1)S(1)} %get-tuple-element.36), channel_id=1, source_target_pairs={{0,1},{1,0},{2,3},{3,2},{4,5},{5,4},{6,7},{7,6},{8,9},{9,8},{10,11... | collective-permute-start | bytes 294920 | tf_op jit(solution)/shard_map/ppermute | solution.py:545
  17.6 1.0 %collective-permute-done.5.got_ref = bf16[8,4,8,192]{3,2,1,0:T(8,128)(2,1)S(1)} collective-permute-done((bf16[8,4,8,192]{3,2,1,0:T(8,128)(2,1)S(1)}, bf16[8,4,8,192]{3,2,1,0:T(8,128)(2,1)S(1)}, u32[]{:S(2)}, u32[]{:S(2)}) %collective-permute-start.5) | collective-permute-done | bytes 98336 | tf_op jit(solution)/shard_map/ppermute | solution.py:545
  18.6 0.7 %shard_map.90 = bf16[8,8,8,192]{3,2,1,0:T(8,128)(2,1)} custom-call(bf16[8,4,8,192]{3,2,1,0:T(8,128)(2,1)S(1)} %get-tuple-element.35.keep_ref, bf16[8,4,8,192]{3,2,1,0:T(8,128)(2,1)S(1)} %collective-permute-done.5.got_ref), custom_call_target="tpu_custom_call" | custom-call | tf_op jit(solution)/shard_map/pallas_call | solution.py:546
  (4 shorter events, 0.1 us)
Async XLA Ops:
  0.0 1.0 %copy-start.2 = (bf16[8,8,8,192]{3,2,1,0:T(8,128)(2,1)S(1)}, bf16[8,8,8,192]{3,2,1,0:T(8,128)(2,1)}, u32[]{:S(2)}) copy-start(bf16[8,8,8,192]{3,2,1,0:T(8,128)(2,1)} %raw.1) | copy-start | bytes 589828
  1.1 4.9 %collective-permute-start.1 = (bf16[36,8,384]{2,1,0:T(8,128)(2,1)S(1)}, bf16[36,8,384]{2,1,0:T(8,128)(2,1)S(1)}, u32[]{:S(2)}, u32[]{:S(2)}) collective-permute-start(bf16[36,8,384]{2,1,0:T(8,128)(2,1)S(1)} %get-tuple-element.26), channel_id=1, source_target_pairs={{0,1},{1,0},{2,3},{3,2},{4,5},{5,4},{6,7},{7,6},{8,9},{9,8},{10,11... | collective-permute-start | bytes 663560 | tf_op jit(solution)/shard_map/ppermute | solution.py:477
  1.6 11.3 %collective-permute-start = (bf16[17,8,384]{2,1,0:T(8,128)(2,1)S(1)}, bf16[17,8,384]{2,1,0:T(8,128)(2,1)S(1)}, u32[]{:S(2)}, u32[]{:S(2)}) collective-permute-start(bf16[17,8,384]{2,1,0:T(8,128)(2,1)S(1)} %get-tuple-element.24.tail_ref), channel_id=1, source_target_pairs={{0,8},{1,9},{2,10},{3,11},{4,12},{5,13},{6,14},{7,15},{16,24},{17,... | collective-permute-start | bytes 313352 | tf_op jit(solution)/shard_map/ppermute | solution.py:476
  6.1 5.0 %copy-start = (bf16[3,3,3,192,192]{4,3,2,1,0:T(8,128)(2,1)S(1)}, bf16[3,3,3,192,192]{4,3,2,1,0:T(8,128)(2,1)}, u32[]{:S(2)}) copy-start(bf16[3,3,3,192,192]{4,3,2,1,0:T(8,128)(2,1)} %w1_ref.5) | copy-start | bytes 5971972
  6.1 5.0 %copy-start.3 = (f32[192]{0:T(256)S(1)}, f32[192]{0:T(256)}, u32[]{:S(2)}) copy-start(f32[192]{0:T(256)} %param.10) | copy-start | bytes 2308
  6.1 5.0 %copy-start.4 = (f32[192]{0:T(256)S(1)}, f32[192]{0:T(256)}, u32[]{:S(2)}) copy-start(f32[192]{0:T(256)} %param.12) | copy-start | bytes 2308
  6.1 5.0 %copy-start.5 = (f32[192]{0:T(256)S(1)}, f32[192]{0:T(256)}, u32[]{:S(2)}) copy-start(f32[192]{0:T(256)} %param.13) | copy-start | bytes 2308
  6.2 6.9 %copy-start.1 = (bf16[3,3,3,192,192]{4,3,2,1,0:T(8,128)(2,1)S(1)}, bf16[3,3,3,192,192]{4,3,2,1,0:T(8,128)(2,1)}, u32[]{:S(2)}) copy-start(bf16[3,3,3,192,192]{4,3,2,1,0:T(8,128)(2,1)} %w2_ref.3) | copy-start | bytes 5971972
  6.2 6.9 %copy-start.6 = (f32[192]{0:T(256)S(1)}, f32[192]{0:T(256)}, u32[]{:S(2)}) copy-start(f32[192]{0:T(256)} %param.15) | copy-start | bytes 2308
  6.2 6.9 %collective-permute-start.4 = (bf16[2,8,8,384]{3,2,1,0:T(8,128)(2,1)S(1)}, bf16[2,8,8,384]{3,2,1,0:T(8,128)(2,1)S(1)}, u32[]{:S(2)}, u32[]{:S(2)}) collective-permute-start(bf16[2,8,8,384]{3,2,1,0:T(8,128)(2,1)S(1)} %get-tuple-element.29), channel_id=1, source_target_pairs={{0,3},{3,0},{8,11},{11,8},{2,5},{5,2},{10,13},{13,10},{4,7},{7,4},... | collective-permute-start | bytes 294920 | tf_op jit(solution)/shard_map/ppermute | solution.py:486
  9.7 5.3 %collective-permute-start.3 = (bf16[8,8,384]{2,1,0:T(8,128)(2,1)S(1)}, bf16[8,8,384]{2,1,0:T(8,128)(2,1)S(1)}, u32[]{:S(2)}, u32[]{:S(2)}) collective-permute-start(bf16[8,8,384]{2,1,0:T(8,128)(2,1)S(1)} %get-tuple-element.28), channel_id=1, source_target_pairs={{0,11},{3,8},{2,13},{5,10},{4,15},{7,12},{16,27},{19,24},{18,29},{... | collective-permute-start | bytes 147464 | tf_op jit(solution)/shard_map/ppermute | solution.py:487
  12.9 2.2 %collective-permute-start.2 = (bf16[12,8,384]{2,1,0:T(8,128)(2,1)S(1)}, bf16[12,8,384]{2,1,0:T(8,128)(2,1)S(1)}, u32[]{:S(2)}, u32[]{:S(2)}) collective-permute-start(bf16[12,8,384]{2,1,0:T(8,128)(2,1)S(1)} %shard_map.85), channel_id=1, source_target_pairs={{0,1},{1,0},{2,3},{3,2},{4,5},{5,4},{6,7},{7,6},{8,9},{9,8},{10,11... | collective-permute-start | bytes 221192 | tf_op jit(solution)/shard_map/ppermute | solution.py:509
  17.0 1.5 %collective-permute-start.5 = (bf16[8,4,8,192]{3,2,1,0:T(8,128)(2,1)S(1)}, bf16[8,4,8,192]{3,2,1,0:T(8,128)(2,1)S(1)}, u32[]{:S(2)}, u32[]{:S(2)}) collective-permute-start(bf16[8,4,8,192]{3,2,1,0:T(8,128)(2,1)S(1)} %get-tuple-element.36), channel_id=1, source_target_pairs={{0,1},{1,0},{2,3},{3,2},{4,5},{5,4},{6,7},{7,6},{8,9},{9,8},{10,11... | collective-permute-start | bytes 294920 | tf_op jit(solution)/shard_map/ppermute | solution.py:545

commit v7 on v6

--- a/solution.py
+++ b/solution.py
@@ -10,6 +10,7 @@
 TAPS = 3
 LANES = 128
 PRODUCT = 192
+OWN = 128
 
 
 def slots_kernel(slots_ref):
@@ -118,12 +119,14 @@
     return jnp.stack([part.astype(jnp.bfloat16) for part in parts])
 
 
-def in_turn(steps):
+def in_turn(steps, beside=None):
     waiting = None
     for product, then in steps:
         result = product()
         if waiting:
             waiting[1](waiting[0])
+        elif beside:
+            beside()
         waiting = (result, then)
     waiting[1](waiting[0])
 
@@ -266,7 +269,8 @@
 
 
 def own_kernel(
-    marks_ref, mine_ref, other_ref, gain1_ref, w1_ref, bias1_ref, gain2_ref, first_ref, late_ref
+    marks_ref, mine_ref, other_ref, gain1_ref, w1_ref, bias1_ref, gain2_ref,
+    first_ref, late_ref, raw_ref,
 ):
     frames, pairs, side, packed = mine_ref.shape
     live = frame_flags(marks_ref[...], range(2, frames))
@@ -278,7 +282,7 @@
     def store(begin, end, rows):
         late_ref[:, begin:end] = rows
 
-    steps = hide(first_ref, w1_ref, bias1_ref, gain2_ref, 0, frames - 2, 2 * pairs - 2, live, store, 2 * PRODUCT // 3)
+    steps = hide(first_ref, w1_ref, bias1_ref, gain2_ref, 0, frames - 2, 2 * pairs - 2, live, store, OWN)
     each = -(-(frames - 2) // len(steps))
 
     def filled(k, product):
@@ -287,13 +291,17 @@
             return product()
         return run
 
+    def left(result):
+        raw_ref[...] = result
+
+    steps[-1] = (steps[-1][0], left)
     in_turn([(filled(k, product), then) for k, (product, then) in enumerate(steps)])
 
 
 def edge_kernel(
-    marks_ref, mine_ref, other_ref, edge_ref, first_ref, late_ref,
+    marks_ref, mine_ref, other_ref, edge_ref, first_ref, done_ref, raw_ref,
     gain1_ref, w1_ref, bias1_ref, gain2_ref, w2_ref, bias2_ref,
-    strip_ref, hidden_ref, keep_ref, send_ref, strip, operand,
+    strip_ref, hidden_ref, keep_ref, send_ref, border_ref, strip, operand, late_ref,
 ):
     core = lower_part()
     frames, pairs = mine_ref.shape[:2]
@@ -302,31 +310,37 @@
     outward, inward = pl.ds(2 * core, 2), pl.ds(2 * (1 - core), 2)
     fill_rows(strip, 0, 2 * core, edge_ref[1][:, None], edge_ref[0][:, None], gain1_ref)
     strip[:, :, inward] = first_ref[:, :, pl.ds((rows - 2) * core, 2)]
-    operand[:, :, inward] = late_ref[:, :, pl.ds((rows - 4) * core, 2)]
     live = frame_flags(marks_ref[...], range(frames))
     inside = inside_flags(2)
+    done = done_ref.shape[1]
+    late_ref[:, 0:done] = done_ref[...]
+
+    def activate():
+        flag = jnp.concatenate(live[2 + done:], axis=0)
+        late_ref[:, done:] = second_rows(raw_ref[...], flag, gain2_ref, gain2_ref.shape[-1])
+        operand[:, :, inward] = late_ref[:, :, pl.ds((rows - 4) * core, 2)]
 
     def store(begin, end, values):
         operand[:, begin:end, outward] = values
 
-    def finished(start_row, pair, count):
-        def put(ref):
-            def store(frame, row, value):
-                ref[frame - CACHE, start_row + row] = value
-            return store
-
-        def then(start, part, result):
-            targets = (put(keep_ref), put(send_ref))
-            finish(mine_ref, other_ref, live, CACHE + start, (pair, count), result, targets)
-
-        return then
+    def put(ref):
+        def store(frame, row, value):
+            ref[frame - CACHE, row] = value
+        return store
+
+    def middle(start, part, result):
+        targets = (put(keep_ref), put(send_ref))
+        finish(mine_ref, other_ref, live, CACHE + start, (1, pairs - 2), result, targets)
+
+    def border(start, part, result):
+        border_ref[start:start + part] = result
 
     flags = [flag * inside for flag in live[2:]]
-    middle, border = finished(2 * (1 - core), 1, pairs - 2), finished((rows - 4) * core, (pairs - 1) * core, 1)
     in_turn(
         hide(strip, w1_ref, bias1_ref, gain2_ref, 0, frames - 2, 2, flags, store)
         + convolved(late_ref, w2_ref, bias2_ref, 0, late, rows - 4, middle)
-        + convolved(operand, w2_ref, bias2_ref, 0, late, 2, border)
+        + convolved(operand, w2_ref, bias2_ref, 0, late, 2, border),
+        activate,
     )
     strip_ref[...] = strip[:, 0:2, outward]
     hidden_ref[:, :, pl.ds(2 * (1 - core), rows - 2)] = late_ref[:, 0:2]
@@ -347,14 +361,14 @@
 
 def early_kernel(
     marks_ref, tail_mine_ref, tail_other_ref, mine_ref, other_ref, edge_ref, first_ref, hidden_ref,
-    late_keep_ref, late_send_ref, gain1_ref, w1_ref, bias1_ref, gain2_ref, w2_ref, bias2_ref,
+    late_keep_ref, late_send_ref, late_border_ref, gain1_ref, w1_ref, bias1_ref, gain2_ref, w2_ref, bias2_ref,
     keep_ref, send_ref, plane, operand,
 ):
     core = lower_part()
     held = mine_ref.shape[1]
     rows = 2 * held
     pairs = tail_mine_ref.shape[0] // CACHE
-    live = frame_flags(marks_ref[...], range(CACHE))
+    live = frame_flags(marks_ref[...], range(mine_ref.shape[0]))
     inside = inside_flags(rows)
     earlier = lax.axis_index("tchunk") > 0
     middle, border = 2 * (1 - core), rows * core
@@ -366,12 +380,24 @@
     plane[:, :, pl.ds(border, 2)] = edge_ref[...]
     operand[:, CACHE:] = hidden_ref[...]
 
+    def put(ref, offset=0):
+        def store(frame, row, value):
+            ref[frame, offset + row] = value
+        return store
+
+    def finish_late():
+        offset = (rows - 4) * core
+        targets = (put(keep_ref, offset), put(send_ref, offset))
+        finish(mine_ref, other_ref, live, CACHE, ((held - 1) * core, 1), late_border_ref[...], targets)
+        for source, target in ((late_keep_ref, keep_ref), (late_send_ref, send_ref)):
+            target[CACHE:, pl.ds(2 * (1 - core), rows - 4)] = source[...]
+
     def fill(first, flags):
         def store(begin, end, values):
             operand[:, first + begin:first + end] = values
 
         flags = [flag * inside for flag in flags]
-        in_turn(hide(plane, w1_ref, bias1_ref, gain2_ref, first, CACHE - first, rows, flags, store))
+        in_turn(hide(plane, w1_ref, bias1_ref, gain2_ref, first, CACHE - first, rows, flags, store), finish_late)
 
     @pl.when(earlier)
     def _():
@@ -387,17 +413,10 @@
         operand[:, 0:2] = jnp.zeros(operand.shape[:1] + (2,) + operand.shape[2:], operand.dtype)
         fill(2, live[0:2])
 
-    def put(ref):
-        def store(frame, row, value):
-            ref[frame, row] = value
-        return store
-
     def then(start, part, result):
         finish(mine_ref, other_ref, live, start, (core, held - 1), result, (put(keep_ref), put(send_ref)))
 
     in_turn(convolved(operand, w2_ref, bias2_ref, 0, CACHE, rows - 2, then))
-    keep_ref[CACHE:] = late_keep_ref[...]
-    send_ref[CACHE:] = late_send_ref[...]
 
 
 def place_kernel(keep_ref, got_ref, result_ref, arrived):
@@ -490,11 +509,16 @@
         gain_first.reshape(1, channels), conv_first, bias_first.reshape(1, channels),
         gain_second.reshape(1, channels), conv_second, bias_second.reshape(1, channels),
     )
-    first, late = pl.pallas_call(
+    products = -(-(frames - 2) * half * width // OWN)
+    done = -(-(frames - 2) // products) * (products - 1)
+    first, late, raw = pl.pallas_call(
         own_kernel,
-        out_shape=(shape(3, frames, half + 2, width, LANES), shape(3, frames - 2, half, width, LANES)),
+        out_shape=(
+            shape(3, frames, half + 2, width, LANES), shape(3, done, half, width, LANES),
+            jax.ShapeDtypeStruct((frames - 2 - done, half, width, channels), jnp.float32),
+        ),
         in_specs=[vmem] * 7,
-        out_specs=(vmem,) * 2,
+        out_specs=(vmem,) * 3,
         compiler_params=limit,
         cost_estimate=cost(work * (frames - 2) * half, 4 * 2**20),
     )(marks, mine, other, *weights[:4])
@@ -507,21 +531,23 @@
         cost_estimate=cost(1, 1),
     )(tail_mine, late)
     tail_other = lax.ppermute(rest, "wa", swap)
-    strip, hidden, keep, send = pl.pallas_call(
+    strip, hidden, keep, send, border = pl.pallas_call(
         edge_kernel,
         out_shape=(
             shape(3, 2, 2, width, LANES), shape(3, 2, half + 2, width, LANES),
-            shape(frames - CACHE, half, side, channels), shape(frames - CACHE, half, side, channels),
+            shape(frames - CACHE, half - 2, side, channels), shape(frames - CACHE, half - 2, side, channels),
+            jax.ShapeDtypeStruct((frames - CACHE, 2, width, channels), jnp.float32),
         ),
-        in_specs=[vmem] * 12,
-        out_specs=(vmem,) * 4,
+        in_specs=[vmem] * 13,
+        out_specs=(vmem,) * 5,
         scratch_shapes=[
             pltpu.VMEM((3, frames, 4, width, LANES), bf16),
             pltpu.VMEM((3, frames - 2, 4, width, LANES), bf16),
+            pltpu.VMEM((3, frames - 2, half, width, LANES), bf16),
         ],
         compiler_params=limit,
         cost_estimate=cost(2**20, 2**20),
-    )(marks, mine, other, own_edge, first, late, *weights)
+    )(marks, mine, other, own_edge, first, late, raw, *weights)
     tail_edge = pl.pallas_call(
         tail_edge_kernel,
         out_shape=shape(3, CACHE + 2, 2, width, LANES),
@@ -533,7 +559,7 @@
     keep, send = pl.pallas_call(
         early_kernel,
         out_shape=(shape(frames, half, side, channels), shape(frames, half, side, channels)),
-        in_specs=[vmem] * 16,
+        in_specs=[vmem] * 17,
         out_specs=(vmem, vmem),
         scratch_shapes=[
             pltpu.VMEM((3, CACHE + 2, half + 4, width, LANES), bf16),
@@ -541,7 +567,7 @@
         ],
         compiler_params=limit,
         cost_estimate=cost(work * CACHE * (2 * half + 2), 8 * 2**20),
-    )(marks, tail_mine, tail_other, mine, other, tail_edge, first, hidden, keep, send, *weights)
+    )(marks, tail_mine, tail_other, mine, other, tail_edge, first, hidden, keep, send, border, *weights)
     got = lax.ppermute(send, "wa", swap)
     return pl.pallas_call(
         place_kernel,

time: 19.5 us -> 19.3 us (0.990)
  Pallas kernels: 6.68 us -> 6.47 us
    pallas_call x1, Pallas kernels: 1.83 us -> 1.53 us  [shards(): pl.pallas_call(own_kernel, out_shape=(shape(3, frames, half + 2, width, L...]
  transfers between devices with their start and end apart: 6 -> 6, of which waited for: 1 -> 1; matrix products, arithmetic and copies ran while one was open for 0% -> 0% of each run, Pallas kernels for 20% -> 19%
where the time goes in v7:
time: 19.3 us; the launch traced here: 19.1 us
  starting transfers between devices  10.4 us (54%)
  Pallas kernels  6.47 us (34%)
  waiting for transfers between devices  1 us (5%)
  between operations  0.92 us (5%)
  local copies, waits for them, and re-layouts  0.31 us (2%)
    ppermute x1, starting transfers between devices, shards(): tail_mine = lax.ppermute(tail, axes, straight)  4.41 us
    ppermute x1, starting transfers between devices, shards(): own_edge = lax.ppermute(own_edge, axes, across)  3.56 us
    pallas_call x1, Pallas kernels, shards(): pl.pallas_call(edge_kernel, out_shape=(shape(3, 2, 2, width, LANES), shap...  2.05 us
    pallas_call x1, Pallas kernels, shards(): pl.pallas_call(early_kernel, out_shape=(shape(frames, half, side, channel...  1.95 us
    pallas_call x1, Pallas kernels, shards(): pl.pallas_call(own_kernel, out_shape=(shape(3, frames, half + 2, width, L...  1.53 us
    ppermute x1, starting transfers between devices, shards(): tail_edge = lax.ppermute(tail_edge, axes, diagonal)  1.29 us
    ppermute x1, waiting for transfers between devices, shards(): got = lax.ppermute(send, 'wa', swap)  0.99 us
    pallas_call x1, Pallas kernels, shards(): pl.pallas_call(place_kernel, out_shape=shape(*features.shape), in_specs=[...  0.71 us
  transfers between devices with their start and end apart: 6, of which 1 were waited for; matrix products, arithmetic and copies ran while one was open for 0% of the time, Pallas kernels for 19%

profile of v7, /device:TPU:0, one launch (start us, length us, event | category | flops | bytes accessed | tf_op | source)
XLA Modules:
  0.0 19.1 jit_solution(2180771879826184740)
XLA Ops:
  0.0 0.0 copy-start.2
  0.7 0.3 %copy-done.2 = bf16[8,8,8,192]{3,2,1,0:T(8,128)(2,1)S(1)} copy-done((bf16[8,8,8,192]{3,2,1,0:T(8,128)(2,1)S(1)}, bf16[8,8,8,192]{3,2,1,0:T(8,128)(2,1)}, u32[]{:S(2)}) %copy-start.2) | copy-done | bytes 196632
  1.0 0.1 shard_map.83
  1.1 0.5 %collective-permute-start.1 = (bf16[36,8,384]{2,1,0:T(8,128)(2,1)S(1)}, bf16[36,8,384]{2,1,0:T(8,128)(2,1)S(1)}, u32[]{:S(2)}, u32[]{:S(2)}) collective-permute-start(bf16[36,8,384]{2,1,0:T(8,128)(2,1)S(1)} %get-tuple-element.28), channel_id=1, source_target_pairs={{0,1},{1,0},{2,3},{3,2},{4,5},{5,4},{6,7},{7,6},{8,9},{9,8},{10,11... | collective-permute-start | bytes 663560 | tf_op jit(solution)/shard_map/ppermute | solution.py:496
  1.6 4.4 %collective-permute-start = (bf16[17,8,384]{2,1,0:T(8,128)(2,1)S(1)}, bf16[17,8,384]{2,1,0:T(8,128)(2,1)S(1)}, u32[]{:S(2)}, u32[]{:S(2)}) collective-permute-start(bf16[17,8,384]{2,1,0:T(8,128)(2,1)S(1)} %get-tuple-element.26.tail_ref), channel_id=1, source_target_pairs={{0,8},{1,9},{2,10},{3,11},{4,12},{5,13},{6,14},{7,15},{16,24},{17,... | collective-permute-start | bytes 313352 | tf_op jit(solution)/shard_map/ppermute | solution.py:495
  6.1 0.0 collective-permute-done.1.other_ref
  6.1 0.0 copy-start
  6.1 0.0 copy-start.3
  6.1 0.0 copy-start.4
  6.1 0.0 copy-start.5
  6.2 0.0 copy-start.1
  6.2 0.0 copy-start.6
  6.2 3.6 %collective-permute-start.4 = (bf16[2,8,8,384]{3,2,1,0:T(8,128)(2,1)S(1)}, bf16[2,8,8,384]{3,2,1,0:T(8,128)(2,1)S(1)}, u32[]{:S(2)}, u32[]{:S(2)}) collective-permute-start(bf16[2,8,8,384]{3,2,1,0:T(8,128)(2,1)S(1)} %get-tuple-element.31), channel_id=1, source_target_pairs={{0,3},{3,0},{8,11},{11,8},{2,5},{5,2},{10,13},{13,10},{4,7},{7,4},... | collective-permute-start | bytes 294920 | tf_op jit(solution)/shard_map/ppermute | solution.py:505
  9.7 1.3 %collective-permute-start.3 = (bf16[8,8,384]{2,1,0:T(8,128)(2,1)S(1)}, bf16[8,8,384]{2,1,0:T(8,128)(2,1)S(1)}, u32[]{:S(2)}, u32[]{:S(2)}) collective-permute-start(bf16[8,8,384]{2,1,0:T(8,128)(2,1)S(1)} %get-tuple-element.30), channel_id=1, source_target_pairs={{0,11},{3,8},{2,13},{5,10},{4,15},{7,12},{16,27},{19,24},{18,29},{... | collective-permute-start | bytes 147464 | tf_op jit(solution)/shard_map/ppermute | solution.py:506
  11.0 0.0 copy-done
  11.0 0.0 copy-done.3
  11.1 0.0 copy-done.4
  11.1 0.0 copy-done.5
  11.1 1.5 %shard_map.84 = (bf16[3,8,6,16,128]{4,3,2,1,0:T(8,128)(2,1)S(1)}, bf16[3,4,4,16,128]{4,3,2,1,0:T(8,128)(2,1)S(1)}, f32[2,4,16,192]{3,2,1,0:T(8,128)S(1)}) custom-call(bf16[8,384]{1,0:T(8,128)(2,1)S(1)} %get-tuple-element.25.marks_ref, bf16[8,3,8,384]{3,2,1,0:T(8,128)(2,1)S(1)} %get-tuple-element.27.mine_ref, ...), custom_call_target="tpu_custom_call" | custom-call | flops 764411904 | bytes 4194304 | tf_op jit(solution)/shard_map/pallas_call | solution.py:514
  12.6 0.0 collective-permute-done.tail_ref.tail_mine_ref
  12.6 0.1 collective-permute-start.2
  12.7 0.0 collective-permute-done.4.edge_ref
  12.7 0.0 copy-done.1
  12.7 0.0 copy-done.6
  12.8 2.1 %shard_map.87 = (bf16[3,2,2,16,128]{4,3,2,1,0:T(8,128)(2,1)S(1)}, bf16[3,2,6,16,128]{4,3,2,1,0:T(8,128)(2,1)S(1)}, bf16[4,2,8,192]{3,2,1,0:T(8,128)(2,1)S(1)}, b...) custom-call(bf16[8,384]{1,0:T(8,128)(2,1)S(1)} %get-tuple-element.25.marks_ref, ...), custom_call_target="tpu_custom_call" | custom-call | flops 1048576 | bytes 1048576 | tf_op jit(solution)/shard_map/pallas_call | solution.py:534
  14.8 0.0 collective-permute-done.3.edge_ref
  14.9 0.0 collective-permute-done.2.tail_other_ref
  14.9 2.0 %shard_map.89 = (bf16[8,4,8,192]{3,2,1,0:T(8,128)(2,1)S(1)}, bf16[8,4,8,192]{3,2,1,0:T(8,128)(2,1)S(1)}) custom-call(bf16[8,384]{1,0:T(8,128)(2,1)S(1)} %get-tuple-element.25.marks_ref, bf16[17,8,384]{2,1,0:T(8,128)(2,1)S(1)} %collective-permute-done.tail_ref.tail_mine_ref, bf16[12,8,384]{2,1,0:T(8,128)(2,1)S(1)} %collective-permute-done.2.tail_other_ref, ...), custom_call_target="tpu_custom_call" | custom-call | flops 1274019840 | bytes 8388608 | tf_op jit(solution)/shard_map/pallas_call | solution.py:559
  16.8 0.5 %collective-permute-start.5 = (bf16[8,4,8,192]{3,2,1,0:T(8,128)(2,1)S(1)}, bf16[8,4,8,192]{3,2,1,0:T(8,128)(2,1)S(1)}, u32[]{:S(2)}, u32[]{:S(2)}) collective-permute-start(bf16[8,4,8,192]{3,2,1,0:T(8,128)(2,1)S(1)} %get-tuple-element.40), channel_id=1, source_target_pairs={{0,1},{1,0},{2,3},{3,2},{4,5},{5,4},{6,7},{7,6},{8,9},{9,8},{10,11... | collective-permute-start | bytes 294920 | tf_op jit(solution)/shard_map/ppermute | solution.py:571
  17.4 1.0 %collective-permute-done.5.got_ref = bf16[8,4,8,192]{3,2,1,0:T(8,128)(2,1)S(1)} collective-permute-done((bf16[8,4,8,192]{3,2,1,0:T(8,128)(2,1)S(1)}, bf16[8,4,8,192]{3,2,1,0:T(8,128)(2,1)S(1)}, u32[]{:S(2)}, u32[]{:S(2)}) %collective-permute-start.5) | collective-permute-done | bytes 98336 | tf_op jit(solution)/shard_map/ppermute | solution.py:571
  18.4 0.7 %shard_map.90 = bf16[8,8,8,192]{3,2,1,0:T(8,128)(2,1)} custom-call(bf16[8,4,8,192]{3,2,1,0:T(8,128)(2,1)S(1)} %get-tuple-element.39.keep_ref, bf16[8,4,8,192]{3,2,1,0:T(8,128)(2,1)S(1)} %collective-permute-done.5.got_ref), custom_call_target="tpu_custom_call" | custom-call | tf_op jit(solution)/shard_map/pallas_call | solution.py:572
  (4 shorter events, 0.1 us)
Async XLA Ops:
  0.0 1.0 %copy-start.2 = (bf16[8,8,8,192]{3,2,1,0:T(8,128)(2,1)S(1)}, bf16[8,8,8,192]{3,2,1,0:T(8,128)(2,1)}, u32[]{:S(2)}) copy-start(bf16[8,8,8,192]{3,2,1,0:T(8,128)(2,1)} %raw.1) | copy-start | bytes 589828
  1.1 4.9 %collective-permute-start.1 = (bf16[36,8,384]{2,1,0:T(8,128)(2,1)S(1)}, bf16[36,8,384]{2,1,0:T(8,128)(2,1)S(1)}, u32[]{:S(2)}, u32[]{:S(2)}) collective-permute-start(bf16[36,8,384]{2,1,0:T(8,128)(2,1)S(1)} %get-tuple-element.28), channel_id=1, source_target_pairs={{0,1},{1,0},{2,3},{3,2},{4,5},{5,4},{6,7},{7,6},{8,9},{9,8},{10,11... | collective-permute-start | bytes 663560 | tf_op jit(solution)/shard_map/ppermute | solution.py:496
  1.6 11.0 %collective-permute-start = (bf16[17,8,384]{2,1,0:T(8,128)(2,1)S(1)}, bf16[17,8,384]{2,1,0:T(8,128)(2,1)S(1)}, u32[]{:S(2)}, u32[]{:S(2)}) collective-permute-start(bf16[17,8,384]{2,1,0:T(8,128)(2,1)S(1)} %get-tuple-element.26.tail_ref), channel_id=1, source_target_pairs={{0,8},{1,9},{2,10},{3,11},{4,12},{5,13},{6,14},{7,15},{16,24},{17,... | collective-permute-start | bytes 313352 | tf_op jit(solution)/shard_map/ppermute | solution.py:495
  6.1 5.0 %copy-start = (bf16[3,3,3,192,192]{4,3,2,1,0:T(8,128)(2,1)S(1)}, bf16[3,3,3,192,192]{4,3,2,1,0:T(8,128)(2,1)}, u32[]{:S(2)}) copy-start(bf16[3,3,3,192,192]{4,3,2,1,0:T(8,128)(2,1)} %w1_ref.5) | copy-start | bytes 5971972
  6.1 5.0 %copy-start.3 = (f32[192]{0:T(256)S(1)}, f32[192]{0:T(256)}, u32[]{:S(2)}) copy-start(f32[192]{0:T(256)} %param.10) | copy-start | bytes 2308
  6.1 5.0 %copy-start.4 = (f32[192]{0:T(256)S(1)}, f32[192]{0:T(256)}, u32[]{:S(2)}) copy-start(f32[192]{0:T(256)} %param.12) | copy-start | bytes 2308
  6.1 5.0 %copy-start.5 = (f32[192]{0:T(256)S(1)}, f32[192]{0:T(256)}, u32[]{:S(2)}) copy-start(f32[192]{0:T(256)} %param.13) | copy-start | bytes 2308
  6.2 6.6 %copy-start.1 = (bf16[3,3,3,192,192]{4,3,2,1,0:T(8,128)(2,1)S(1)}, bf16[3,3,3,192,192]{4,3,2,1,0:T(8,128)(2,1)}, u32[]{:S(2)}) copy-start(bf16[3,3,3,192,192]{4,3,2,1,0:T(8,128)(2,1)} %w2_ref.3) | copy-start | bytes 5971972
  6.2 6.6 %copy-start.6 = (f32[192]{0:T(256)S(1)}, f32[192]{0:T(256)}, u32[]{:S(2)}) copy-start(f32[192]{0:T(256)} %param.15) | copy-start | bytes 2308
  6.2 6.6 %collective-permute-start.4 = (bf16[2,8,8,384]{3,2,1,0:T(8,128)(2,1)S(1)}, bf16[2,8,8,384]{3,2,1,0:T(8,128)(2,1)S(1)}, u32[]{:S(2)}, u32[]{:S(2)}) collective-permute-start(bf16[2,8,8,384]{3,2,1,0:T(8,128)(2,1)S(1)} %get-tuple-element.31), channel_id=1, source_target_pairs={{0,3},{3,0},{8,11},{11,8},{2,5},{5,2},{10,13},{13,10},{4,7},{7,4},... | collective-permute-start | bytes 294920 | tf_op jit(solution)/shard_map/ppermute | solution.py:505
  9.7 5.1 %collective-permute-start.3 = (bf16[8,8,384]{2,1,0:T(8,128)(2,1)S(1)}, bf16[8,8,384]{2,1,0:T(8,128)(2,1)S(1)}, u32[]{:S(2)}, u32[]{:S(2)}) collective-permute-start(bf16[8,8,384]{2,1,0:T(8,128)(2,1)S(1)} %get-tuple-element.30), channel_id=1, source_target_pairs={{0,11},{3,8},{2,13},{5,10},{4,15},{7,12},{16,27},{19,24},{18,29},{... | collective-permute-start | bytes 147464 | tf_op jit(solution)/shard_map/ppermute | solution.py:506
  12.6 2.2 %collective-permute-start.2 = (bf16[12,8,384]{2,1,0:T(8,128)(2,1)S(1)}, bf16[12,8,384]{2,1,0:T(8,128)(2,1)S(1)}, u32[]{:S(2)}, u32[]{:S(2)}) collective-permute-start(bf16[12,8,384]{2,1,0:T(8,128)(2,1)S(1)} %shard_map.85), channel_id=1, source_target_pairs={{0,1},{1,0},{2,3},{3,2},{4,5},{5,4},{6,7},{7,6},{8,9},{9,8},{10,11... | collective-permute-start | bytes 221192 | tf_op jit(solution)/shard_map/ppermute | solution.py:533
  16.8 1.5 %collective-permute-start.5 = (bf16[8,4,8,192]{3,2,1,0:T(8,128)(2,1)S(1)}, bf16[8,4,8,192]{3,2,1,0:T(8,128)(2,1)S(1)}, u32[]{:S(2)}, u32[]{:S(2)}) collective-permute-start(bf16[8,4,8,192]{3,2,1,0:T(8,128)(2,1)S(1)} %get-tuple-element.40), channel_id=1, source_target_pairs={{0,1},{1,0},{2,3},{3,2},{4,5},{5,4},{6,7},{7,6},{8,9},{9,8},{10,11... | collective-permute-start | bytes 294920 | tf_op jit(solution)/shard_map/ppermute | solution.py:571

commit v8 on v7

--- a/solution.py
+++ b/solution.py
@@ -301,7 +301,7 @@
 def edge_kernel(
     marks_ref, mine_ref, other_ref, edge_ref, first_ref, done_ref, raw_ref,
     gain1_ref, w1_ref, bias1_ref, gain2_ref, w2_ref, bias2_ref,
-    strip_ref, hidden_ref, keep_ref, send_ref, border_ref, strip, operand, late_ref,
+    strip_ref, hidden_ref, keep_ref, send_ref, border_ref, operand, strip, late_ref,
 ):
     core = lower_part()
     frames, pairs = mine_ref.shape[:2]
@@ -336,12 +336,21 @@
         border_ref[start:start + part] = result
 
     flags = [flag * inside for flag in live[2:]]
-    in_turn(
-        hide(strip, w1_ref, bias1_ref, gain2_ref, 0, frames - 2, 2, flags, store)
-        + convolved(late_ref, w2_ref, bias2_ref, 0, late, rows - 4, middle)
-        + convolved(operand, w2_ref, bias2_ref, 0, late, 2, border),
-        activate,
-    )
+    earlier = lax.axis_index("tchunk") > 0
+
+    def steps():
+        return hide(strip, w1_ref, bias1_ref, gain2_ref, 0, frames - 2, 2, flags, store) + convolved(
+            late_ref, w2_ref, bias2_ref, 0, late, rows - 4, middle
+        )
+
+    @pl.when(earlier)
+    def _():
+        in_turn(steps() + convolved(operand, w2_ref, bias2_ref, 0, late, 2, border), activate)
+
+    @pl.when(jnp.logical_not(earlier))
+    def _():
+        in_turn(steps(), activate)
+
     strip_ref[...] = strip[:, 0:2, outward]
     hidden_ref[:, :, pl.ds(2 * (1 - core), rows - 2)] = late_ref[:, 0:2]
     hidden_ref[:, :, pl.ds((rows - 2) * core, 2)] = operand[:, 0:2, outward]
@@ -361,7 +370,7 @@
 
 def early_kernel(
     marks_ref, tail_mine_ref, tail_other_ref, mine_ref, other_ref, edge_ref, first_ref, hidden_ref,
-    late_keep_ref, late_send_ref, late_border_ref, gain1_ref, w1_ref, bias1_ref, gain2_ref, w2_ref, bias2_ref,
+    late_keep_ref, late_send_ref, late_border_ref, late_operand_ref, gain1_ref, w1_ref, bias1_ref, gain2_ref, w2_ref, bias2_ref,
     keep_ref, send_ref, plane, operand,
 ):
     core = lower_part()
@@ -385,25 +394,46 @@
             ref[frame, offset + row] = value
         return store
 
-    def finish_late():
+    def late_border(start, part, result):
         offset = (rows - 4) * core
         targets = (put(keep_ref, offset), put(send_ref, offset))
-        finish(mine_ref, other_ref, live, CACHE, ((held - 1) * core, 1), late_border_ref[...], targets)
+        finish(mine_ref, other_ref, live, CACHE + start, ((held - 1) * core, 1), result, targets)
+
+    def late_middle():
         for source, target in ((late_keep_ref, keep_ref), (late_send_ref, send_ref)):
             target[CACHE:, pl.ds(2 * (1 - core), rows - 4)] = source[...]
 
-    def fill(first, flags):
+    def hidden_steps(first, flags):
         def store(begin, end, values):
             operand[:, first + begin:first + end] = values
 
         flags = [flag * inside for flag in flags]
-        in_turn(hide(plane, w1_ref, bias1_ref, gain2_ref, first, CACHE - first, rows, flags, store), finish_late)
+        return hide(plane, w1_ref, bias1_ref, gain2_ref, first, CACHE - first, rows, flags, store)
+
+    def then(start, part, result):
+        finish(mine_ref, other_ref, live, start, (core, held - 1), result, (put(keep_ref), put(send_ref)))
+
+    def result_steps():
+        return convolved(operand, w2_ref, bias2_ref, 0, CACHE, rows - 2, then)
 
     @pl.when(earlier)
     def _():
-        mine = unpacked(tail_mine_ref, pairs, core * (pairs - held))
-        fill_rows(plane, 0, middle, mine, unpacked(tail_other_ref, held, 0), gain1_ref)
-        fill(0, frame_flags(tail_mine_ref[CACHE * pairs], range(CACHE - 2, CACHE)) + live[0:2])
+        fill_rows(
+            plane, 0, middle, unpacked(tail_mine_ref, pairs, core * (pairs - held)),
+            unpacked(tail_other_ref, held, 0), gain1_ref,
+        )
+        flags = frame_flags(tail_mine_ref[CACHE * pairs], range(CACHE - 2, CACHE)) + live[0:2]
+
+        def beside():
+            late_middle()
+            late_border(0, late_border_ref.shape[0], late_border_ref[...])
+
+        hidden, results = hidden_steps(0, flags), result_steps()
+        if len(hidden) == 2 and len(results) == 2:
+            in_turn(hidden[::-1] + results[::-1], beside)
+        else:
+            in_turn(hidden, beside)
+            in_turn(results)
 
     @pl.when(jnp.logical_not(earlier))
     def _():
@@ -411,12 +441,8 @@
             plane.shape[:1] + (CACHE, rows) + plane.shape[3:], plane.dtype
         )
         operand[:, 0:2] = jnp.zeros(operand.shape[:1] + (2,) + operand.shape[2:], operand.dtype)
-        fill(2, live[0:2])
-
-    def then(start, part, result):
-        finish(mine_ref, other_ref, live, start, (core, held - 1), result, (put(keep_ref), put(send_ref)))
-
-    in_turn(convolved(operand, w2_ref, bias2_ref, 0, CACHE, rows - 2, then))
+        border = convolved(late_operand_ref, w2_ref, bias2_ref, 0, late_border_ref.shape[0], 2, late_border)
+        in_turn(hidden_steps(2, live[0:2]) + border + result_steps()[::-1], late_middle)
 
 
 def place_kernel(keep_ref, got_ref, result_ref, arrived):
@@ -531,18 +557,18 @@
         cost_estimate=cost(1, 1),
     )(tail_mine, late)
     tail_other = lax.ppermute(rest, "wa", swap)
-    strip, hidden, keep, send, border = pl.pallas_call(
+    strip, hidden, keep, send, border, late = pl.pallas_call(
         edge_kernel,
         out_shape=(
             shape(3, 2, 2, width, LANES), shape(3, 2, half + 2, width, LANES),
             shape(frames - CACHE, half - 2, side, channels), shape(frames - CACHE, half - 2, side, channels),
             jax.ShapeDtypeStruct((frames - CACHE, 2, width, channels), jnp.float32),
+            shape(3, frames - 2, 4, width, LANES),
         ),
         in_specs=[vmem] * 13,
-        out_specs=(vmem,) * 5,
+        out_specs=(vmem,) * 6,
         scratch_shapes=[
             pltpu.VMEM((3, frames, 4, width, LANES), bf16),
-            pltpu.VMEM((3, frames - 2, 4, width, LANES), bf16),
             pltpu.VMEM((3, frames - 2, half, width, LANES), bf16),
         ],
         compiler_params=limit,
@@ -559,7 +585,7 @@
     keep, send = pl.pallas_call(
         early_kernel,
         out_shape=(shape(frames, half, side, channels), shape(frames, half, side, channels)),
-        in_specs=[vmem] * 17,
+        in_specs=[vmem] * 18,
         out_specs=(vmem, vmem),
         scratch_shapes=[
             pltpu.VMEM((3, CACHE + 2, half + 4, width, LANES), bf16),
@@ -567,7 +593,7 @@
         ],
         compiler_params=limit,
         cost_estimate=cost(work * CACHE * (2 * half + 2), 8 * 2**20),
-    )(marks, tail_mine, tail_other, mine, other, tail_edge, first, hidden, keep, send, border, *weights)
+    )(marks, tail_mine, tail_other, mine, other, tail_edge, first, hidden, keep, send, border, late, *weights)
     got = lax.ppermute(send, "wa", swap)
     return pl.pallas_call(
         place_kernel,

time: 19.3 us -> 18.8 us (0.974)
  Pallas kernels: 6.47 us -> 5.97 us
    pallas_call x1, Pallas kernels: 2.05 us -> 1.4 us  [shards(): pl.pallas_call(edge_kernel, out_shape=(shape(3, 2, 2, width, LANES), shap...]
  transfers between devices with their start and end apart: 6 -> 6, of which waited for: 1 -> 1; matrix products, arithmetic and copies ran while one was open for 0% -> 0% of each run, Pallas kernels for 19% -> 16%
where the time goes in v8:
time: 18.8 us; the launch traced here: 18.6 us
  starting transfers between devices  10.4 us (55%)
  Pallas kernels  5.97 us (32%)
  waiting for transfers between devices  1 us (5%)
  between operations  0.91 us (5%)
  local copies, waits for them, and re-layouts  0.31 us (2%)
    ppermute x1, starting transfers between devices, shards(): tail_mine = lax.ppermute(tail, axes, straight)  4.41 us
    ppermute x1, starting transfers between devices, shards(): own_edge = lax.ppermute(own_edge, axes, across)  3.56 us
    pallas_call x1, Pallas kernels, shards(): pl.pallas_call(early_kernel, out_shape=(shape(frames, half, side, channel...  2.1 us
    pallas_call x1, Pallas kernels, shards(): pl.pallas_call(own_kernel, out_shape=(shape(3, frames, half + 2, width, L...  1.53 us
    pallas_call x1, Pallas kernels, shards(): pl.pallas_call(edge_kernel, out_shape=(shape(3, 2, 2, width, LANES), shap...  1.4 us
    ppermute x1, starting transfers between devices, shards(): tail_edge = lax.ppermute(tail_edge, axes, diagonal)  1.29 us
    ppermute x1, waiting for transfers between devices, shards(): got = lax.ppermute(send, 'wa', swap)  0.99 us
    pallas_call x1, Pallas kernels, shards(): pl.pallas_call(place_kernel, out_shape=shape(*features.shape), in_specs=[...  0.71 us
  transfers between devices with their start and end apart: 6, of which 1 were waited for; matrix products, arithmetic and copies ran while one was open for 0% of the time, Pallas kernels for 16%

profile of v8, /device:TPU:0, one launch (start us, length us, event | category | flops | bytes accessed | tf_op | source)
XLA Modules:
  0.0 18.6 jit_solution(13063536095633319612)
XLA Ops:
  0.0 0.0 copy-start.2
  0.7 0.3 %copy-done.2 = bf16[8,8,8,192]{3,2,1,0:T(8,128)(2,1)S(1)} copy-done((bf16[8,8,8,192]{3,2,1,0:T(8,128)(2,1)S(1)}, bf16[8,8,8,192]{3,2,1,0:T(8,128)(2,1)}, u32[]{:S(2)}) %copy-start.2) | copy-done | bytes 196632
  1.0 0.1 shard_map.83
  1.1 0.5 %collective-permute-start.1 = (bf16[36,8,384]{2,1,0:T(8,128)(2,1)S(1)}, bf16[36,8,384]{2,1,0:T(8,128)(2,1)S(1)}, u32[]{:S(2)}, u32[]{:S(2)}) collective-permute-start(bf16[36,8,384]{2,1,0:T(8,128)(2,1)S(1)} %get-tuple-element.29), channel_id=1, source_target_pairs={{0,1},{1,0},{2,3},{3,2},{4,5},{5,4},{6,7},{7,6},{8,9},{9,8},{10,11... | collective-permute-start | bytes 663560 | tf_op jit(solution)/shard_map/ppermute | solution.py:522
  1.6 4.4 %collective-permute-start = (bf16[17,8,384]{2,1,0:T(8,128)(2,1)S(1)}, bf16[17,8,384]{2,1,0:T(8,128)(2,1)S(1)}, u32[]{:S(2)}, u32[]{:S(2)}) collective-permute-start(bf16[17,8,384]{2,1,0:T(8,128)(2,1)S(1)} %get-tuple-element.27.tail_ref), channel_id=1, source_target_pairs={{0,8},{1,9},{2,10},{3,11},{4,12},{5,13},{6,14},{7,15},{16,24},{17,... | collective-permute-start | bytes 313352 | tf_op jit(solution)/shard_map/ppermute | solution.py:521
  6.1 0.0 collective-permute-done.1.other_ref
  6.1 0.0 copy-start
  6.1 0.0 copy-start.3
  6.1 0.0 copy-start.4
  6.1 0.0 copy-start.5
  6.2 0.0 copy-start.1
  6.2 0.0 copy-start.6
  6.2 3.6 %collective-permute-start.4 = (bf16[2,8,8,384]{3,2,1,0:T(8,128)(2,1)S(1)}, bf16[2,8,8,384]{3,2,1,0:T(8,128)(2,1)S(1)}, u32[]{:S(2)}, u32[]{:S(2)}) collective-permute-start(bf16[2,8,8,384]{3,2,1,0:T(8,128)(2,1)S(1)} %get-tuple-element.32), channel_id=1, source_target_pairs={{0,3},{3,0},{8,11},{11,8},{2,5},{5,2},{10,13},{13,10},{4,7},{7,4},... | collective-permute-start | bytes 294920 | tf_op jit(solution)/shard_map/ppermute | solution.py:531
  9.7 1.3 %collective-permute-start.3 = (bf16[8,8,384]{2,1,0:T(8,128)(2,1)S(1)}, bf16[8,8,384]{2,1,0:T(8,128)(2,1)S(1)}, u32[]{:S(2)}, u32[]{:S(2)}) collective-permute-start(bf16[8,8,384]{2,1,0:T(8,128)(2,1)S(1)} %get-tuple-element.31), channel_id=1, source_target_pairs={{0,11},{3,8},{2,13},{5,10},{4,15},{7,12},{16,27},{19,24},{18,29},{... | collective-permute-start | bytes 147464 | tf_op jit(solution)/shard_map/ppermute | solution.py:532
  11.0 0.0 copy-done
  11.0 0.0 copy-done.3
  11.1 0.0 copy-done.4
  11.1 0.0 copy-done.5
  11.1 1.5 %shard_map.84 = (bf16[3,8,6,16,128]{4,3,2,1,0:T(8,128)(2,1)S(1)}, bf16[3,4,4,16,128]{4,3,2,1,0:T(8,128)(2,1)S(1)}, f32[2,4,16,192]{3,2,1,0:T(8,128)S(1)}) custom-call(bf16[8,384]{1,0:T(8,128)(2,1)S(1)} %get-tuple-element.26.marks_ref, bf16[8,3,8,384]{3,2,1,0:T(8,128)(2,1)S(1)} %get-tuple-element.28.mine_ref, ...), custom_call_target="tpu_custom_call" | custom-call | flops 764411904 | bytes 4194304 | tf_op jit(solution)/shard_map/pallas_call | solution.py:540
  12.6 0.0 collective-permute-done.tail_ref.tail_mine_ref
  12.6 0.1 collective-permute-start.2
  12.7 0.0 collective-permute-done.4.edge_ref
  12.7 0.0 copy-done.1
  12.7 0.0 copy-done.6
  12.8 1.4 %shard_map.87 = (bf16[3,2,2,16,128]{4,3,2,1,0:T(8,128)(2,1)S(1)}, bf16[3,2,6,16,128]{4,3,2,1,0:T(8,128)(2,1)S(1)}, bf16[4,2,8,192]{3,2,1,0:T(8,128)(2,1)S(1)}, b...) custom-call(bf16[8,384]{1,0:T(8,128)(2,1)S(1)} %get-tuple-element.26.marks_, ...), custom_call_target="tpu_custom_call" | custom-call | flops 1048576 | bytes 1048576 | tf_op jit(solution)/shard_map/pallas_call | solution.py:560
  14.2 0.0 collective-permute-done.3.edge_ref
  14.2 0.0 collective-permute-done.2.tail_other_ref
  14.2 2.1 %shard_map.89 = (bf16[8,4,8,192]{3,2,1,0:T(8,128)(2,1)S(1)}, bf16[8,4,8,192]{3,2,1,0:T(8,128)(2,1)S(1)}) custom-call(bf16[8,384]{1,0:T(8,128)(2,1)S(1)} %get-tuple-element.26.marks_ref, bf16[17,8,384]{2,1,0:T(8,128)(2,1)S(1)} %collective-permute-done.tail_ref.tail_mine_ref, bf16[12,8,384]{2,1,0:T(8,128)(2,1)S(1)} %collective-permute-done.2.tail_other_ref, ...), custom_call_target="tpu_custom_call" | custom-call | flops 1274019840 | bytes 8388608 | tf_op jit(solution)/shard_map/pallas_call | solution.py:585
  16.3 0.5 %collective-permute-start.5 = (bf16[8,4,8,192]{3,2,1,0:T(8,128)(2,1)S(1)}, bf16[8,4,8,192]{3,2,1,0:T(8,128)(2,1)S(1)}, u32[]{:S(2)}, u32[]{:S(2)}) collective-permute-start(bf16[8,4,8,192]{3,2,1,0:T(8,128)(2,1)S(1)} %get-tuple-element.42), channel_id=1, source_target_pairs={{0,1},{1,0},{2,3},{3,2},{4,5},{5,4},{6,7},{7,6},{8,9},{9,8},{10,11... | collective-permute-start | bytes 294920 | tf_op jit(solution)/shard_map/ppermute | solution.py:597
  16.9 1.0 %collective-permute-done.5.got_ref = bf16[8,4,8,192]{3,2,1,0:T(8,128)(2,1)S(1)} collective-permute-done((bf16[8,4,8,192]{3,2,1,0:T(8,128)(2,1)S(1)}, bf16[8,4,8,192]{3,2,1,0:T(8,128)(2,1)S(1)}, u32[]{:S(2)}, u32[]{:S(2)}) %collective-permute-start.5) | collective-permute-done | bytes 98336 | tf_op jit(solution)/shard_map/ppermute | solution.py:597
  17.8 0.7 %shard_map.90 = bf16[8,8,8,192]{3,2,1,0:T(8,128)(2,1)} custom-call(bf16[8,4,8,192]{3,2,1,0:T(8,128)(2,1)S(1)} %get-tuple-element.41.keep_ref, bf16[8,4,8,192]{3,2,1,0:T(8,128)(2,1)S(1)} %collective-permute-done.5.got_ref), custom_call_target="tpu_custom_call" | custom-call | tf_op jit(solution)/shard_map/pallas_call | solution.py:598
  (4 shorter events, 0.1 us)
Async XLA Ops:
  0.0 1.0 %copy-start.2 = (bf16[8,8,8,192]{3,2,1,0:T(8,128)(2,1)S(1)}, bf16[8,8,8,192]{3,2,1,0:T(8,128)(2,1)}, u32[]{:S(2)}) copy-start(bf16[8,8,8,192]{3,2,1,0:T(8,128)(2,1)} %raw.1) | copy-start | bytes 589828
  1.1 4.9 %collective-permute-start.1 = (bf16[36,8,384]{2,1,0:T(8,128)(2,1)S(1)}, bf16[36,8,384]{2,1,0:T(8,128)(2,1)S(1)}, u32[]{:S(2)}, u32[]{:S(2)}) collective-permute-start(bf16[36,8,384]{2,1,0:T(8,128)(2,1)S(1)} %get-tuple-element.29), channel_id=1, source_target_pairs={{0,1},{1,0},{2,3},{3,2},{4,5},{5,4},{6,7},{7,6},{8,9},{9,8},{10,11... | collective-permute-start | bytes 663560 | tf_op jit(solution)/shard_map/ppermute | solution.py:522
  1.6 11.0 %collective-permute-start = (bf16[17,8,384]{2,1,0:T(8,128)(2,1)S(1)}, bf16[17,8,384]{2,1,0:T(8,128)(2,1)S(1)}, u32[]{:S(2)}, u32[]{:S(2)}) collective-permute-start(bf16[17,8,384]{2,1,0:T(8,128)(2,1)S(1)} %get-tuple-element.27.tail_ref), channel_id=1, source_target_pairs={{0,8},{1,9},{2,10},{3,11},{4,12},{5,13},{6,14},{7,15},{16,24},{17,... | collective-permute-start | bytes 313352 | tf_op jit(solution)/shard_map/ppermute | solution.py:521
  6.1 5.0 %copy-start = (bf16[3,3,3,192,192]{4,3,2,1,0:T(8,128)(2,1)S(1)}, bf16[3,3,3,192,192]{4,3,2,1,0:T(8,128)(2,1)}, u32[]{:S(2)}) copy-start(bf16[3,3,3,192,192]{4,3,2,1,0:T(8,128)(2,1)} %w1_ref.5) | copy-start | bytes 5971972
  6.1 5.0 %copy-start.3 = (f32[192]{0:T(256)S(1)}, f32[192]{0:T(256)}, u32[]{:S(2)}) copy-start(f32[192]{0:T(256)} %param.10) | copy-start | bytes 2308
  6.1 5.0 %copy-start.4 = (f32[192]{0:T(256)S(1)}, f32[192]{0:T(256)}, u32[]{:S(2)}) copy-start(f32[192]{0:T(256)} %param.12) | copy-start | bytes 2308
  6.1 5.0 %copy-start.5 = (f32[192]{0:T(256)S(1)}, f32[192]{0:T(256)}, u32[]{:S(2)}) copy-start(f32[192]{0:T(256)} %param.13) | copy-start | bytes 2308
  6.2 6.6 %copy-start.1 = (bf16[3,3,3,192,192]{4,3,2,1,0:T(8,128)(2,1)S(1)}, bf16[3,3,3,192,192]{4,3,2,1,0:T(8,128)(2,1)}, u32[]{:S(2)}) copy-start(bf16[3,3,3,192,192]{4,3,2,1,0:T(8,128)(2,1)} %w2_ref.3) | copy-start | bytes 5971972
  6.2 6.6 %copy-start.6 = (f32[192]{0:T(256)S(1)}, f32[192]{0:T(256)}, u32[]{:S(2)}) copy-start(f32[192]{0:T(256)} %param.15) | copy-start | bytes 2308
  6.2 6.6 %collective-permute-start.4 = (bf16[2,8,8,384]{3,2,1,0:T(8,128)(2,1)S(1)}, bf16[2,8,8,384]{3,2,1,0:T(8,128)(2,1)S(1)}, u32[]{:S(2)}, u32[]{:S(2)}) collective-permute-start(bf16[2,8,8,384]{3,2,1,0:T(8,128)(2,1)S(1)} %get-tuple-element.32), channel_id=1, source_target_pairs={{0,3},{3,0},{8,11},{11,8},{2,5},{5,2},{10,13},{13,10},{4,7},{7,4},... | collective-permute-start | bytes 294920 | tf_op jit(solution)/shard_map/ppermute | solution.py:531
  9.7 4.4 %collective-permute-start.3 = (bf16[8,8,384]{2,1,0:T(8,128)(2,1)S(1)}, bf16[8,8,384]{2,1,0:T(8,128)(2,1)S(1)}, u32[]{:S(2)}, u32[]{:S(2)}) collective-permute-start(bf16[8,8,384]{2,1,0:T(8,128)(2,1)S(1)} %get-tuple-element.31), channel_id=1, source_target_pairs={{0,11},{3,8},{2,13},{5,10},{4,15},{7,12},{16,27},{19,24},{18,29},{... | collective-permute-start | bytes 147464 | tf_op jit(solution)/shard_map/ppermute | solution.py:532
  12.6 1.6 %collective-permute-start.2 = (bf16[12,8,384]{2,1,0:T(8,128)(2,1)S(1)}, bf16[12,8,384]{2,1,0:T(8,128)(2,1)S(1)}, u32[]{:S(2)}, u32[]{:S(2)}) collective-permute-start(bf16[12,8,384]{2,1,0:T(8,128)(2,1)S(1)} %shard_map.85), channel_id=1, source_target_pairs={{0,1},{1,0},{2,3},{3,2},{4,5},{5,4},{6,7},{7,6},{8,9},{9,8},{10,11... | collective-permute-start | bytes 221192 | tf_op jit(solution)/shard_map/ppermute | solution.py:559
  16.3 1.5 %collective-permute-start.5 = (bf16[8,4,8,192]{3,2,1,0:T(8,128)(2,1)S(1)}, bf16[8,4,8,192]{3,2,1,0:T(8,128)(2,1)S(1)}, u32[]{:S(2)}, u32[]{:S(2)}) collective-permute-start(bf16[8,4,8,192]{3,2,1,0:T(8,128)(2,1)S(1)} %get-tuple-element.42), channel_id=1, source_target_pairs={{0,1},{1,0},{2,3},{3,2},{4,5},{5,4},{6,7},{7,6},{8,9},{9,8},{10,11... | collective-permute-start | bytes 294920 | tf_op jit(solution)/shard_map/ppermute | solution.py:597

commit v9 on v8

--- a/solution.py
+++ b/solution.py
@@ -10,7 +10,7 @@
 TAPS = 3
 LANES = 128
 PRODUCT = 192
-OWN = 128
+OWN = 192
 
 
 def slots_kernel(slots_ref):
@@ -174,15 +174,11 @@
             rights.append(jnp.zeros((rest, channels), jnp.bfloat16))
         return jnp.concatenate(rights, axis=0)
 
-    half = len(groups) // 2
-    parts = [(part, operands(part)) for part in (groups[:half], groups[half:])]
+    left = operands(groups)
     products = []
     for j in range(TAPS):
-        total = None
-        for part, left in parts if j % 2 == 0 else parts[::-1]:
-            product = jnp.dot(left, weights(part, j, left.shape[1]), preferred_element_type=jnp.float32)
-            total = product if total is None else total + product
-        products.append(total.reshape(frames * rows, width, channels))
+        product = jnp.dot(left, weights(groups, j, left.shape[1]), preferred_element_type=jnp.float32)
+        products.append(product.reshape(frames * rows, width, channels))
     column = lax.broadcasted_iota(jnp.int32, (1, width, 1), 1)
     before = jnp.where(column == 0, 0.0, pltpu.roll(products[0], 1, 1))
     after = jnp.where(column == width - 1, 0.0, pltpu.roll(products[2], width - 1, 1))

time: 18.8 us -> 18.9 us (level)
  transfers between devices with their start and end apart: 6 -> 6, of which waited for: 1 -> 1; matrix products, arithmetic and copies ran while one was open for 0% -> 0% of each run, Pallas kernels for 16% -> 17%
where the time goes in v9:
time: 18.9 us; the launch traced here: 18.7 us
  starting transfers between devices  10.4 us (55%)
  Pallas kernels  6.07 us (32%)
  waiting for transfers between devices  1 us (5%)
  between operations  0.91 us (5%)
  local copies, waits for them, and re-layouts  0.31 us (2%)
    ppermute x1, starting transfers between devices, shards(): tail_mine = lax.ppermute(tail, axes, straight)  4.41 us
    ppermute x1, starting transfers between devices, shards(): own_edge = lax.ppermute(own_edge, axes, across)  3.56 us
    pallas_call x1, Pallas kernels, shards(): pl.pallas_call(early_kernel, out_shape=(shape(frames, half, side, channel...  2.12 us
    pallas_call x1, Pallas kernels, shards(): pl.pallas_call(own_kernel, out_shape=(shape(3, frames, half + 2, width, L...  1.59 us
    pallas_call x1, Pallas kernels, shards(): pl.pallas_call(edge_kernel, out_shape=(shape(3, 2, 2, width, LANES), shap...  1.43 us
    ppermute x1, starting transfers between devices, shards(): tail_edge = lax.ppermute(tail_edge, axes, diagonal)  1.29 us
    ppermute x1, waiting for transfers between devices, shards(): got = lax.ppermute(send, 'wa', swap)  0.99 us
    pallas_call x1, Pallas kernels, shards(): pl.pallas_call(place_kernel, out_shape=shape(*features.shape), in_specs=[...  0.71 us
  transfers between devices with their start and end apart: 6, of which 1 were waited for; matrix products, arithmetic and copies ran while one was open for 0% of the time, Pallas kernels for 17%

profile of v9, /device:TPU:0, one launch (start us, length us, event | category | flops | bytes accessed | tf_op | source)
XLA Modules:
  0.0 18.7 jit_solution(13087917986100480051)
XLA Ops:
  0.0 0.0 copy-start.2
  0.7 0.3 %copy-done.2 = bf16[8,8,8,192]{3,2,1,0:T(8,128)(2,1)S(1)} copy-done((bf16[8,8,8,192]{3,2,1,0:T(8,128)(2,1)S(1)}, bf16[8,8,8,192]{3,2,1,0:T(8,128)(2,1)}, u32[]{:S(2)}) %copy-start.2) | copy-done | bytes 196632
  1.0 0.1 shard_map.83
  1.1 0.5 %collective-permute-start.1 = (bf16[36,8,384]{2,1,0:T(8,128)(2,1)S(1)}, bf16[36,8,384]{2,1,0:T(8,128)(2,1)S(1)}, u32[]{:S(2)}, u32[]{:S(2)}) collective-permute-start(bf16[36,8,384]{2,1,0:T(8,128)(2,1)S(1)} %get-tuple-element.29), channel_id=1, source_target_pairs={{0,1},{1,0},{2,3},{3,2},{4,5},{5,4},{6,7},{7,6},{8,9},{9,8},{10,11... | collective-permute-start | bytes 663560 | tf_op jit(solution)/shard_map/ppermute | solution.py:518
  1.6 4.4 %collective-permute-start = (bf16[17,8,384]{2,1,0:T(8,128)(2,1)S(1)}, bf16[17,8,384]{2,1,0:T(8,128)(2,1)S(1)}, u32[]{:S(2)}, u32[]{:S(2)}) collective-permute-start(bf16[17,8,384]{2,1,0:T(8,128)(2,1)S(1)} %get-tuple-element.27.tail_ref), channel_id=1, source_target_pairs={{0,8},{1,9},{2,10},{3,11},{4,12},{5,13},{6,14},{7,15},{16,24},{17,... | collective-permute-start | bytes 313352 | tf_op jit(solution)/shard_map/ppermute | solution.py:517
  6.1 0.0 collective-permute-done.1.other_ref
  6.1 0.0 copy-start
  6.1 0.0 copy-start.3
  6.1 0.0 copy-start.4
  6.1 0.0 copy-start.5
  6.2 0.0 copy-start.1
  6.2 0.0 copy-start.6
  6.2 3.6 %collective-permute-start.4 = (bf16[2,8,8,384]{3,2,1,0:T(8,128)(2,1)S(1)}, bf16[2,8,8,384]{3,2,1,0:T(8,128)(2,1)S(1)}, u32[]{:S(2)}, u32[]{:S(2)}) collective-permute-start(bf16[2,8,8,384]{3,2,1,0:T(8,128)(2,1)S(1)} %get-tuple-element.32), channel_id=1, source_target_pairs={{0,3},{3,0},{8,11},{11,8},{2,5},{5,2},{10,13},{13,10},{4,7},{7,4},... | collective-permute-start | bytes 294920 | tf_op jit(solution)/shard_map/ppermute | solution.py:527
  9.7 1.3 %collective-permute-start.3 = (bf16[8,8,384]{2,1,0:T(8,128)(2,1)S(1)}, bf16[8,8,384]{2,1,0:T(8,128)(2,1)S(1)}, u32[]{:S(2)}, u32[]{:S(2)}) collective-permute-start(bf16[8,8,384]{2,1,0:T(8,128)(2,1)S(1)} %get-tuple-element.31), channel_id=1, source_target_pairs={{0,11},{3,8},{2,13},{5,10},{4,15},{7,12},{16,27},{19,24},{18,29},{... | collective-permute-start | bytes 147464 | tf_op jit(solution)/shard_map/ppermute | solution.py:528
  11.0 0.0 copy-done
  11.0 0.0 copy-done.3
  11.1 0.0 copy-done.4
  11.1 0.0 copy-done.5
  11.1 1.6 %shard_map.84 = (bf16[3,8,6,16,128]{4,3,2,1,0:T(8,128)(2,1)S(1)}, bf16[3,3,4,16,128]{4,3,2,1,0:T(8,128)(2,1)S(1)}, f32[3,4,16,192]{3,2,1,0:T(8,128)S(1)}) custom-call(bf16[8,384]{1,0:T(8,128)(2,1)S(1)} %get-tuple-element.26.marks_ref, bf16[8,3,8,384]{3,2,1,0:T(8,128)(2,1)S(1)} %get-tuple-element.28.mine_ref, ...), custom_call_target="tpu_custom_call" | custom-call | flops 764411904 | bytes 4194304 | tf_op jit(solution)/shard_map/pallas_call | solution.py:536
  12.7 0.0 collective-permute-done.tail_ref.tail_mine_ref
  12.7 0.1 collective-permute-start.2
  12.8 0.0 collective-permute-done.4.edge_ref
  12.8 0.0 copy-done.1
  12.8 0.0 copy-done.6
  12.8 1.4 %shard_map.87 = (bf16[3,2,2,16,128]{4,3,2,1,0:T(8,128)(2,1)S(1)}, bf16[3,2,6,16,128]{4,3,2,1,0:T(8,128)(2,1)S(1)}, bf16[4,2,8,192]{3,2,1,0:T(8,128)(2,1)S(1)}, b...) custom-call(bf16[8,384]{1,0:T(8,128)(2,1)S(1)} %get-tuple-element.26.marks_, ...), custom_call_target="tpu_custom_call" | custom-call | flops 1048576 | bytes 1048576 | tf_op jit(solution)/shard_map/pallas_call | solution.py:556
  14.3 0.0 collective-permute-done.3.edge_ref
  14.3 0.0 collective-permute-done.2.tail_other_ref
  14.3 2.1 %shard_map.89 = (bf16[8,4,8,192]{3,2,1,0:T(8,128)(2,1)S(1)}, bf16[8,4,8,192]{3,2,1,0:T(8,128)(2,1)S(1)}) custom-call(bf16[8,384]{1,0:T(8,128)(2,1)S(1)} %get-tuple-element.26.marks_ref, bf16[17,8,384]{2,1,0:T(8,128)(2,1)S(1)} %collective-permute-done.tail_ref.tail_mine_ref, bf16[12,8,384]{2,1,0:T(8,128)(2,1)S(1)} %collective-permute-done.2.tail_other_ref, ...), custom_call_target="tpu_custom_call" | custom-call | flops 1274019840 | bytes 8388608 | tf_op jit(solution)/shard_map/pallas_call | solution.py:581
  16.4 0.5 %collective-permute-start.5 = (bf16[8,4,8,192]{3,2,1,0:T(8,128)(2,1)S(1)}, bf16[8,4,8,192]{3,2,1,0:T(8,128)(2,1)S(1)}, u32[]{:S(2)}, u32[]{:S(2)}) collective-permute-start(bf16[8,4,8,192]{3,2,1,0:T(8,128)(2,1)S(1)} %get-tuple-element.42), channel_id=1, source_target_pairs={{0,1},{1,0},{2,3},{3,2},{4,5},{5,4},{6,7},{7,6},{8,9},{9,8},{10,11... | collective-permute-start | bytes 294920 | tf_op jit(solution)/shard_map/ppermute | solution.py:593
  17.0 1.0 %collective-permute-done.5.got_ref = bf16[8,4,8,192]{3,2,1,0:T(8,128)(2,1)S(1)} collective-permute-done((bf16[8,4,8,192]{3,2,1,0:T(8,128)(2,1)S(1)}, bf16[8,4,8,192]{3,2,1,0:T(8,128)(2,1)S(1)}, u32[]{:S(2)}, u32[]{:S(2)}) %collective-permute-start.5) | collective-permute-done | bytes 98336 | tf_op jit(solution)/shard_map/ppermute | solution.py:593
  18.0 0.7 %shard_map.90 = bf16[8,8,8,192]{3,2,1,0:T(8,128)(2,1)} custom-call(bf16[8,4,8,192]{3,2,1,0:T(8,128)(2,1)S(1)} %get-tuple-element.41.keep_ref, bf16[8,4,8,192]{3,2,1,0:T(8,128)(2,1)S(1)} %collective-permute-done.5.got_ref), custom_call_target="tpu_custom_call" | custom-call | tf_op jit(solution)/shard_map/pallas_call | solution.py:594
  (4 shorter events, 0.1 us)
Async XLA Ops:
  0.0 1.0 %copy-start.2 = (bf16[8,8,8,192]{3,2,1,0:T(8,128)(2,1)S(1)}, bf16[8,8,8,192]{3,2,1,0:T(8,128)(2,1)}, u32[]{:S(2)}) copy-start(bf16[8,8,8,192]{3,2,1,0:T(8,128)(2,1)} %raw.1) | copy-start | bytes 589828
  1.1 4.9 %collective-permute-start.1 = (bf16[36,8,384]{2,1,0:T(8,128)(2,1)S(1)}, bf16[36,8,384]{2,1,0:T(8,128)(2,1)S(1)}, u32[]{:S(2)}, u32[]{:S(2)}) collective-permute-start(bf16[36,8,384]{2,1,0:T(8,128)(2,1)S(1)} %get-tuple-element.29), channel_id=1, source_target_pairs={{0,1},{1,0},{2,3},{3,2},{4,5},{5,4},{6,7},{7,6},{8,9},{9,8},{10,11... | collective-permute-start | bytes 663560 | tf_op jit(solution)/shard_map/ppermute | solution.py:518
  1.6 11.0 %collective-permute-start = (bf16[17,8,384]{2,1,0:T(8,128)(2,1)S(1)}, bf16[17,8,384]{2,1,0:T(8,128)(2,1)S(1)}, u32[]{:S(2)}, u32[]{:S(2)}) collective-permute-start(bf16[17,8,384]{2,1,0:T(8,128)(2,1)S(1)} %get-tuple-element.27.tail_ref), channel_id=1, source_target_pairs={{0,8},{1,9},{2,10},{3,11},{4,12},{5,13},{6,14},{7,15},{16,24},{17,... | collective-permute-start | bytes 313352 | tf_op jit(solution)/shard_map/ppermute | solution.py:517
  6.1 5.0 %copy-start = (bf16[3,3,3,192,192]{4,3,2,1,0:T(8,128)(2,1)S(1)}, bf16[3,3,3,192,192]{4,3,2,1,0:T(8,128)(2,1)}, u32[]{:S(2)}) copy-start(bf16[3,3,3,192,192]{4,3,2,1,0:T(8,128)(2,1)} %w1_ref.5) | copy-start | bytes 5971972
  6.1 5.0 %copy-start.3 = (f32[192]{0:T(256)S(1)}, f32[192]{0:T(256)}, u32[]{:S(2)}) copy-start(f32[192]{0:T(256)} %param.10) | copy-start | bytes 2308
  6.1 5.0 %copy-start.4 = (f32[192]{0:T(256)S(1)}, f32[192]{0:T(256)}, u32[]{:S(2)}) copy-start(f32[192]{0:T(256)} %param.12) | copy-start | bytes 2308
  6.1 5.0 %copy-start.5 = (f32[192]{0:T(256)S(1)}, f32[192]{0:T(256)}, u32[]{:S(2)}) copy-start(f32[192]{0:T(256)} %param.13) | copy-start | bytes 2308
  6.2 6.7 %copy-start.1 = (bf16[3,3,3,192,192]{4,3,2,1,0:T(8,128)(2,1)S(1)}, bf16[3,3,3,192,192]{4,3,2,1,0:T(8,128)(2,1)}, u32[]{:S(2)}) copy-start(bf16[3,3,3,192,192]{4,3,2,1,0:T(8,128)(2,1)} %w2_ref.3) | copy-start | bytes 5971972
  6.2 6.7 %copy-start.6 = (f32[192]{0:T(256)S(1)}, f32[192]{0:T(256)}, u32[]{:S(2)}) copy-start(f32[192]{0:T(256)} %param.15) | copy-start | bytes 2308
  6.2 6.6 %collective-permute-start.4 = (bf16[2,8,8,384]{3,2,1,0:T(8,128)(2,1)S(1)}, bf16[2,8,8,384]{3,2,1,0:T(8,128)(2,1)S(1)}, u32[]{:S(2)}, u32[]{:S(2)}) collective-permute-start(bf16[2,8,8,384]{3,2,1,0:T(8,128)(2,1)S(1)} %get-tuple-element.32), channel_id=1, source_target_pairs={{0,3},{3,0},{8,11},{11,8},{2,5},{5,2},{10,13},{13,10},{4,7},{7,4},... | collective-permute-start | bytes 294920 | tf_op jit(solution)/shard_map/ppermute | solution.py:527
  9.7 4.5 %collective-permute-start.3 = (bf16[8,8,384]{2,1,0:T(8,128)(2,1)S(1)}, bf16[8,8,384]{2,1,0:T(8,128)(2,1)S(1)}, u32[]{:S(2)}, u32[]{:S(2)}) collective-permute-start(bf16[8,8,384]{2,1,0:T(8,128)(2,1)S(1)} %get-tuple-element.31), channel_id=1, source_target_pairs={{0,11},{3,8},{2,13},{5,10},{4,15},{7,12},{16,27},{19,24},{18,29},{... | collective-permute-start | bytes 147464 | tf_op jit(solution)/shard_map/ppermute | solution.py:528
  12.7 1.6 %collective-permute-start.2 = (bf16[12,8,384]{2,1,0:T(8,128)(2,1)S(1)}, bf16[12,8,384]{2,1,0:T(8,128)(2,1)S(1)}, u32[]{:S(2)}, u32[]{:S(2)}) collective-permute-start(bf16[12,8,384]{2,1,0:T(8,128)(2,1)S(1)} %shard_map.85), channel_id=1, source_target_pairs={{0,1},{1,0},{2,3},{3,2},{4,5},{5,4},{6,7},{7,6},{8,9},{9,8},{10,11... | collective-permute-start | bytes 221192 | tf_op jit(solution)/shard_map/ppermute | solution.py:555
  16.4 1.5 %collective-permute-start.5 = (bf16[8,4,8,192]{3,2,1,0:T(8,128)(2,1)S(1)}, bf16[8,4,8,192]{3,2,1,0:T(8,128)(2,1)S(1)}, u32[]{:S(2)}, u32[]{:S(2)}) collective-permute-start(bf16[8,4,8,192]{3,2,1,0:T(8,128)(2,1)S(1)} %get-tuple-element.42), channel_id=1, source_target_pairs={{0,1},{1,0},{2,3},{3,2},{4,5},{5,4},{6,7},{7,6},{8,9},{9,8},{10,11... | collective-permute-start | bytes 294920 | tf_op jit(solution)/shard_map/ppermute | solution.py:593

commit v10 on v8

--- a/solution.py
+++ b/solution.py
@@ -445,16 +445,18 @@
         in_turn(hidden_steps(2, live[0:2]) + border + result_steps()[::-1], late_middle)
 
 
-def place_kernel(keep_ref, got_ref, result_ref, arrived):
-    core, half = lower_part(), keep_ref.shape[1]
-    copies = [
-        pltpu.make_async_copy(keep_ref, result_ref.at[:, pl.ds(half * core, half)], arrived.at[0]),
-        pltpu.make_async_copy(got_ref, result_ref.at[:, pl.ds(half * (1 - core), half)], arrived.at[1]),
-    ]
-    for copy in copies:
-        copy.start()
-    for copy in copies:
-        copy.wait()
+def keep_kernel(keep_ref, result_ref, arrived):
+    half = keep_ref.shape[1]
+    copy = pltpu.make_async_copy(keep_ref, result_ref.at[:, pl.ds(half * lower_part(), half)], arrived)
+    copy.start()
+    copy.wait()
+
+
+def got_kernel(got_ref, kept_ref, result_ref, arrived):
+    half = got_ref.shape[1]
+    copy = pltpu.make_async_copy(got_ref, result_ref.at[:, pl.ds(half * (1 - lower_part()), half)], arrived)
+    copy.start()
+    copy.wait()
 
 
 def shards(features, frame_counts, gain_first, conv_first, bias_first, gain_second, conv_second, bias_second):
@@ -595,14 +597,25 @@
         cost_estimate=cost(work * CACHE * (2 * half + 2), 8 * 2**20),
     )(marks, tail_mine, tail_other, mine, other, tail_edge, first, hidden, keep, send, border, late, *weights)
     got = lax.ppermute(send, "wa", swap)
+    hbm = pl.BlockSpec(memory_space=pltpu.HBM)
+    kept = pl.pallas_call(
+        keep_kernel,
+        out_shape=shape(*features.shape),
+        in_specs=[vmem],
+        out_specs=hbm,
+        scratch_shapes=[pltpu.SemaphoreType.DMA],
+        compiler_params=limit,
+        cost_estimate=cost(2**28, 2**20),
+    )(keep)
     return pl.pallas_call(
-        place_kernel,
+        got_kernel,
         out_shape=shape(*features.shape),
-        in_specs=[vmem, vmem],
-        out_specs=pl.BlockSpec(memory_space=pltpu.HBM),
-        scratch_shapes=[pltpu.SemaphoreType.DMA((2,))],
-        compiler_params=limit,
-    )(keep, got)
+        in_specs=[vmem, hbm],
+        out_specs=hbm,
+        input_output_aliases={1: 0},
+        scratch_shapes=[pltpu.SemaphoreType.DMA],
+        compiler_params=limit,
+    )(got, kept)
 
 
 def solution(mesh):

time: 18.8 us -> 18.7 us (level)
  waiting for transfers between devices: 1 us -> 0.33 us
  Pallas kernels: 5.97 us -> 6.58 us
    ppermute x1, waiting for transfers between devices: 0.99 us -> 0.32 us  [shards(): got = lax.ppermute(send, 'wa', swap)]
    pallas_call x1 -> x2, Pallas kernels: 0.71 us -> 1.32 us  [the longest x1 0.66 us: shards(): pl.pallas_call(keep_kernel, out_shape=shape(*features.shape), in_specs=[v...]
  transfers between devices with their start and end apart: 6 -> 6, of which waited for: 1 -> 1; matrix products, arithmetic and copies ran while one was open for 0% -> 0% of each run, Pallas kernels for 16% -> 20%
where the time goes in v10:
time: 18.7 us; the launch traced here: 18.5 us
  starting transfers between devices  10.4 us (56%)
  Pallas kernels  6.58 us (35%)
  between operations  0.92 us (5%)
  waiting for transfers between devices  0.33 us (2%)
  local copies, waits for them, and re-layouts  0.31 us (2%)
    ppermute x1, starting transfers between devices, shards(): tail_mine = lax.ppermute(tail, axes, straight)  4.41 us
    ppermute x1, starting transfers between devices, shards(): own_edge = lax.ppermute(own_edge, axes, across)  3.56 us
    pallas_call x1, Pallas kernels, shards(): pl.pallas_call(early_kernel, out_shape=(shape(frames, half, side, channel...  2.1 us
    pallas_call x1, Pallas kernels, shards(): pl.pallas_call(own_kernel, out_shape=(shape(3, frames, half + 2, width, L...  1.53 us
    pallas_call x1, Pallas kernels, shards(): pl.pallas_call(edge_kernel, out_shape=(shape(3, 2, 2, width, LANES), shap...  1.4 us
    ppermute x1, starting transfers between devices, shards(): tail_edge = lax.ppermute(tail_edge, axes, diagonal)  1.29 us
    pallas_call x1, Pallas kernels, shards(): pl.pallas_call(keep_kernel, out_shape=shape(*features.shape), in_specs=[v...  0.66 us
    pallas_call x1, Pallas kernels, shards(): pl.pallas_call(got_kernel, out_shape=shape(*features.shape), in_specs=[vm...  0.66 us
  transfers between devices with their start and end apart: 6, of which 1 were waited for; matrix products, arithmetic and copies ran while one was open for 0% of the time, Pallas kernels for 20%

profile of v10, /device:TPU:0, one launch (start us, length us, event | category | flops | bytes accessed | tf_op | source)
XLA Modules:
  0.0 18.5 jit_solution(15482586876910529967)
XLA Ops:
  0.0 0.0 copy-start.2
  0.7 0.3 %copy-done.2 = bf16[8,8,8,192]{3,2,1,0:T(8,128)(2,1)S(1)} copy-done((bf16[8,8,8,192]{3,2,1,0:T(8,128)(2,1)S(1)}, bf16[8,8,8,192]{3,2,1,0:T(8,128)(2,1)}, u32[]{:S(2)}) %copy-start.2) | copy-done | bytes 196632
  1.0 0.1 shard_map.83
  1.1 0.5 %collective-permute-start.1 = (bf16[36,8,384]{2,1,0:T(8,128)(2,1)S(1)}, bf16[36,8,384]{2,1,0:T(8,128)(2,1)S(1)}, u32[]{:S(2)}, u32[]{:S(2)}) collective-permute-start(bf16[36,8,384]{2,1,0:T(8,128)(2,1)S(1)} %get-tuple-element.29), channel_id=1, source_target_pairs={{0,1},{1,0},{2,3},{3,2},{4,5},{5,4},{6,7},{7,6},{8,9},{9,8},{10,11... | collective-permute-start | bytes 663560 | tf_op jit(solution)/shard_map/ppermute | solution.py:524
  1.6 4.4 %collective-permute-start = (bf16[17,8,384]{2,1,0:T(8,128)(2,1)S(1)}, bf16[17,8,384]{2,1,0:T(8,128)(2,1)S(1)}, u32[]{:S(2)}, u32[]{:S(2)}) collective-permute-start(bf16[17,8,384]{2,1,0:T(8,128)(2,1)S(1)} %get-tuple-element.27.tail_ref), channel_id=1, source_target_pairs={{0,8},{1,9},{2,10},{3,11},{4,12},{5,13},{6,14},{7,15},{16,24},{17,... | collective-permute-start | bytes 313352 | tf_op jit(solution)/shard_map/ppermute | solution.py:523
  6.1 0.0 collective-permute-done.1.other_ref
  6.1 0.0 copy-start
  6.1 0.0 copy-start.3
  6.1 0.0 copy-start.4
  6.1 0.0 copy-start.5
  6.2 0.0 copy-start.1
  6.2 0.0 copy-start.6
  6.2 3.6 %collective-permute-start.4 = (bf16[2,8,8,384]{3,2,1,0:T(8,128)(2,1)S(1)}, bf16[2,8,8,384]{3,2,1,0:T(8,128)(2,1)S(1)}, u32[]{:S(2)}, u32[]{:S(2)}) collective-permute-start(bf16[2,8,8,384]{3,2,1,0:T(8,128)(2,1)S(1)} %get-tuple-element.32), channel_id=1, source_target_pairs={{0,3},{3,0},{8,11},{11,8},{2,5},{5,2},{10,13},{13,10},{4,7},{7,4},... | collective-permute-start | bytes 294920 | tf_op jit(solution)/shard_map/ppermute | solution.py:533
  9.7 1.3 %collective-permute-start.3 = (bf16[8,8,384]{2,1,0:T(8,128)(2,1)S(1)}, bf16[8,8,384]{2,1,0:T(8,128)(2,1)S(1)}, u32[]{:S(2)}, u32[]{:S(2)}) collective-permute-start(bf16[8,8,384]{2,1,0:T(8,128)(2,1)S(1)} %get-tuple-element.31), channel_id=1, source_target_pairs={{0,11},{3,8},{2,13},{5,10},{4,15},{7,12},{16,27},{19,24},{18,29},{... | collective-permute-start | bytes 147464 | tf_op jit(solution)/shard_map/ppermute | solution.py:534
  11.0 0.0 copy-done
  11.0 0.0 copy-done.3
  11.1 0.0 copy-done.4
  11.1 0.0 copy-done.5
  11.1 1.5 %shard_map.84 = (bf16[3,8,6,16,128]{4,3,2,1,0:T(8,128)(2,1)S(1)}, bf16[3,4,4,16,128]{4,3,2,1,0:T(8,128)(2,1)S(1)}, f32[2,4,16,192]{3,2,1,0:T(8,128)S(1)}) custom-call(bf16[8,384]{1,0:T(8,128)(2,1)S(1)} %get-tuple-element.26.marks_ref, bf16[8,3,8,384]{3,2,1,0:T(8,128)(2,1)S(1)} %get-tuple-element.28.mine_ref, ...), custom_call_target="tpu_custom_call" | custom-call | flops 764411904 | bytes 4194304 | tf_op jit(solution)/shard_map/pallas_call | solution.py:542
  12.6 0.0 collective-permute-done.tail_ref.tail_mine_ref
  12.6 0.1 collective-permute-start.2
  12.7 0.0 collective-permute-done.4.edge_ref
  12.7 0.0 copy-done.1
  12.7 0.0 copy-done.6
  12.8 1.4 %shard_map.87 = (bf16[3,2,2,16,128]{4,3,2,1,0:T(8,128)(2,1)S(1)}, bf16[3,2,6,16,128]{4,3,2,1,0:T(8,128)(2,1)S(1)}, bf16[4,2,8,192]{3,2,1,0:T(8,128)(2,1)S(1)}, b...) custom-call(bf16[8,384]{1,0:T(8,128)(2,1)S(1)} %get-tuple-element.26.marks_, ...), custom_call_target="tpu_custom_call" | custom-call | flops 1048576 | bytes 1048576 | tf_op jit(solution)/shard_map/pallas_call | solution.py:562
  14.2 0.0 collective-permute-done.3.edge_ref
  14.2 0.0 collective-permute-done.2.tail_other_ref
  14.2 2.1 %shard_map.89 = (bf16[8,4,8,192]{3,2,1,0:T(8,128)(2,1)S(1)}, bf16[8,4,8,192]{3,2,1,0:T(8,128)(2,1)S(1)}) custom-call(bf16[8,384]{1,0:T(8,128)(2,1)S(1)} %get-tuple-element.26.marks_ref, bf16[17,8,384]{2,1,0:T(8,128)(2,1)S(1)} %collective-permute-done.tail_ref.tail_mine_ref, bf16[12,8,384]{2,1,0:T(8,128)(2,1)S(1)} %collective-permute-done.2.tail_other_ref, ...), custom_call_target="tpu_custom_call" | custom-call | flops 1274019840 | bytes 8388608 | tf_op jit(solution)/shard_map/pallas_call | solution.py:587
  16.3 0.5 %collective-permute-start.5 = (bf16[8,4,8,192]{3,2,1,0:T(8,128)(2,1)S(1)}, bf16[8,4,8,192]{3,2,1,0:T(8,128)(2,1)S(1)}, u32[]{:S(2)}, u32[]{:S(2)}) collective-permute-start(bf16[8,4,8,192]{3,2,1,0:T(8,128)(2,1)S(1)} %get-tuple-element.41), channel_id=1, source_target_pairs={{0,1},{1,0},{2,3},{3,2},{4,5},{5,4},{6,7},{7,6},{8,9},{9,8},{10,11... | collective-permute-start | bytes 294920 | tf_op jit(solution)/shard_map/ppermute | solution.py:599
  16.9 0.7 %shard_map.90.kept_ref = bf16[8,8,8,192]{3,2,1,0:T(8,128)(2,1)} custom-call(bf16[8,4,8,192]{3,2,1,0:T(8,128)(2,1)S(1)} %get-tuple-element.42.keep_ref), custom_call_target="tpu_custom_call" | custom-call | flops 268435456 | bytes 1048576 | tf_op jit(solution)/shard_map/pallas_call | solution.py:601
  17.5 0.3 %collective-permute-done.5.got_ref = bf16[8,4,8,192]{3,2,1,0:T(8,128)(2,1)S(1)} collective-permute-done((bf16[8,4,8,192]{3,2,1,0:T(8,128)(2,1)S(1)}, bf16[8,4,8,192]{3,2,1,0:T(8,128)(2,1)S(1)}, u32[]{:S(2)}, u32[]{:S(2)}) %collective-permute-start.5) | collective-permute-done | bytes 98336 | tf_op jit(solution)/shard_map/ppermute | solution.py:599
  17.8 0.7 %shard_map.91 = bf16[8,8,8,192]{3,2,1,0:T(8,128)(2,1)} custom-call(bf16[8,4,8,192]{3,2,1,0:T(8,128)(2,1)S(1)} %collective-permute-done.5.got_ref, bf16[8,8,8,192]{3,2,1,0:T(8,128)(2,1)} %shard_map.90.kept_ref), custom_call_target="tpu_custom_call", output_to_operand_aliasing={{}: (1, {})} | custom-call | tf_op jit(solution)/shard_map/pallas_call | solution.py:610
  (4 shorter events, 0.1 us)
Async XLA Ops:
  0.0 1.0 %copy-start.2 = (bf16[8,8,8,192]{3,2,1,0:T(8,128)(2,1)S(1)}, bf16[8,8,8,192]{3,2,1,0:T(8,128)(2,1)}, u32[]{:S(2)}) copy-start(bf16[8,8,8,192]{3,2,1,0:T(8,128)(2,1)} %raw.1) | copy-start | bytes 589828
  1.1 4.9 %collective-permute-start.1 = (bf16[36,8,384]{2,1,0:T(8,128)(2,1)S(1)}, bf16[36,8,384]{2,1,0:T(8,128)(2,1)S(1)}, u32[]{:S(2)}, u32[]{:S(2)}) collective-permute-start(bf16[36,8,384]{2,1,0:T(8,128)(2,1)S(1)} %get-tuple-element.29), channel_id=1, source_target_pairs={{0,1},{1,0},{2,3},{3,2},{4,5},{5,4},{6,7},{7,6},{8,9},{9,8},{10,11... | collective-permute-start | bytes 663560 | tf_op jit(solution)/shard_map/ppermute | solution.py:524
  1.6 11.0 %collective-permute-start = (bf16[17,8,384]{2,1,0:T(8,128)(2,1)S(1)}, bf16[17,8,384]{2,1,0:T(8,128)(2,1)S(1)}, u32[]{:S(2)}, u32[]{:S(2)}) collective-permute-start(bf16[17,8,384]{2,1,0:T(8,128)(2,1)S(1)} %get-tuple-element.27.tail_ref), channel_id=1, source_target_pairs={{0,8},{1,9},{2,10},{3,11},{4,12},{5,13},{6,14},{7,15},{16,24},{17,... | collective-permute-start | bytes 313352 | tf_op jit(solution)/shard_map/ppermute | solution.py:523
  6.1 5.0 %copy-start = (bf16[3,3,3,192,192]{4,3,2,1,0:T(8,128)(2,1)S(1)}, bf16[3,3,3,192,192]{4,3,2,1,0:T(8,128)(2,1)}, u32[]{:S(2)}) copy-start(bf16[3,3,3,192,192]{4,3,2,1,0:T(8,128)(2,1)} %w1_ref.5) | copy-start | bytes 5971972
  6.1 5.0 %copy-start.3 = (f32[192]{0:T(256)S(1)}, f32[192]{0:T(256)}, u32[]{:S(2)}) copy-start(f32[192]{0:T(256)} %param.10) | copy-start | bytes 2308
  6.1 5.0 %copy-start.4 = (f32[192]{0:T(256)S(1)}, f32[192]{0:T(256)}, u32[]{:S(2)}) copy-start(f32[192]{0:T(256)} %param.12) | copy-start | bytes 2308
  6.1 5.0 %copy-start.5 = (f32[192]{0:T(256)S(1)}, f32[192]{0:T(256)}, u32[]{:S(2)}) copy-start(f32[192]{0:T(256)} %param.13) | copy-start | bytes 2308
  6.2 6.6 %copy-start.1 = (bf16[3,3,3,192,192]{4,3,2,1,0:T(8,128)(2,1)S(1)}, bf16[3,3,3,192,192]{4,3,2,1,0:T(8,128)(2,1)}, u32[]{:S(2)}) copy-start(bf16[3,3,3,192,192]{4,3,2,1,0:T(8,128)(2,1)} %w2_ref.3) | copy-start | bytes 5971972
  6.2 6.6 %copy-start.6 = (f32[192]{0:T(256)S(1)}, f32[192]{0:T(256)}, u32[]{:S(2)}) copy-start(f32[192]{0:T(256)} %param.15) | copy-start | bytes 2308
  6.2 6.6 %collective-permute-start.4 = (bf16[2,8,8,384]{3,2,1,0:T(8,128)(2,1)S(1)}, bf16[2,8,8,384]{3,2,1,0:T(8,128)(2,1)S(1)}, u32[]{:S(2)}, u32[]{:S(2)}) collective-permute-start(bf16[2,8,8,384]{3,2,1,0:T(8,128)(2,1)S(1)} %get-tuple-element.32), channel_id=1, source_target_pairs={{0,3},{3,0},{8,11},{11,8},{2,5},{5,2},{10,13},{13,10},{4,7},{7,4},... | collective-permute-start | bytes 294920 | tf_op jit(solution)/shard_map/ppermute | solution.py:533
  9.7 4.4 %collective-permute-start.3 = (bf16[8,8,384]{2,1,0:T(8,128)(2,1)S(1)}, bf16[8,8,384]{2,1,0:T(8,128)(2,1)S(1)}, u32[]{:S(2)}, u32[]{:S(2)}) collective-permute-start(bf16[8,8,384]{2,1,0:T(8,128)(2,1)S(1)} %get-tuple-element.31), channel_id=1, source_target_pairs={{0,11},{3,8},{2,13},{5,10},{4,15},{7,12},{16,27},{19,24},{18,29},{... | collective-permute-start | bytes 147464 | tf_op jit(solution)/shard_map/ppermute | solution.py:534
  12.6 1.6 %collective-permute-start.2 = (bf16[12,8,384]{2,1,0:T(8,128)(2,1)S(1)}, bf16[12,8,384]{2,1,0:T(8,128)(2,1)S(1)}, u32[]{:S(2)}, u32[]{:S(2)}) collective-permute-start(bf16[12,8,384]{2,1,0:T(8,128)(2,1)S(1)} %shard_map.85), channel_id=1, source_target_pairs={{0,1},{1,0},{2,3},{3,2},{4,5},{5,4},{6,7},{7,6},{8,9},{9,8},{10,11... | collective-permute-start | bytes 221192 | tf_op jit(solution)/shard_map/ppermute | solution.py:561
  16.3 1.5 %collective-permute-start.5 = (bf16[8,4,8,192]{3,2,1,0:T(8,128)(2,1)S(1)}, bf16[8,4,8,192]{3,2,1,0:T(8,128)(2,1)S(1)}, u32[]{:S(2)}, u32[]{:S(2)}) collective-permute-start(bf16[8,4,8,192]{3,2,1,0:T(8,128)(2,1)S(1)} %get-tuple-element.41), channel_id=1, source_target_pairs={{0,1},{1,0},{2,3},{3,2},{4,5},{5,4},{6,7},{7,6},{8,9},{9,8},{10,11... | collective-permute-start | bytes 294920 | tf_op jit(solution)/shard_map/ppermute | solution.py:599

commit v11 on v10

--- a/solution.py
+++ b/solution.py
@@ -285,17 +285,15 @@
     steps = hide(first_ref, w1_ref, bias1_ref, gain2_ref, 0, frames - 2, 2 * pairs - 2, live, store, OWN)
     each = -(-(frames - 2) // len(steps))
 
-    def filled(k, product):
-        def run():
-            fill(min(frames, each * k + (2 if k else 0)), min(frames, each * (k + 1) + 2))
-            return product()
-        return run
-
-    def left(result):
-        raw_ref[...] = result
-
-    steps[-1] = (steps[-1][0], left)
-    in_turn([(filled(k, product), then) for k, (product, then) in enumerate(steps)])
+    position, result = 0, None
+    for k, (product, _) in enumerate(steps[:-1]):
+        fill(position, each * (k + 1) + 2)
+        position = each * (k + 1) + 2
+        before, result = result, product()
+        if k:
+            steps[k - 1][1](before)
+    fill(position, frames)
+    raw_ref[...] = result
 
 
 def edge_kernel(
@@ -308,17 +306,21 @@
     rows = 2 * pairs
     late = frames - CACHE
     outward, inward = pl.ds(2 * core, 2), pl.ds(2 * (1 - core), 2)
-    fill_rows(strip, 0, 2 * core, edge_ref[1][:, None], edge_ref[0][:, None], gain1_ref)
-    strip[:, :, inward] = first_ref[:, :, pl.ds((rows - 2) * core, 2)]
     live = frame_flags(marks_ref[...], range(frames))
     inside = inside_flags(2)
-    done = done_ref.shape[1]
-    late_ref[:, 0:done] = done_ref[...]
+    done, made = done_ref.shape[1], done_ref.shape[1] + raw_ref.shape[0]
 
     def activate():
-        flag = jnp.concatenate(live[2 + done:], axis=0)
-        late_ref[:, done:] = second_rows(raw_ref[...], flag, gain2_ref, gain2_ref.shape[-1])
-        operand[:, :, inward] = late_ref[:, :, pl.ds((rows - 4) * core, 2)]
+        fill_rows(strip, 0, 2 * core, edge_ref[1][:, None], edge_ref[0][:, None], gain1_ref)
+        strip[:, :, inward] = first_ref[:, :, pl.ds((rows - 2) * core, 2)]
+        late_ref[:, 0:done] = done_ref[...]
+        flag = jnp.concatenate(live[2 + done:2 + made], axis=0)
+        late_ref[:, done:made] = second_rows(raw_ref[...], flag, gain2_ref, gain2_ref.shape[-1])
+
+    def store_last(begin, end, values):
+        late_ref[:, made + begin:made + end] = values
+        if made + end == frames - 2:
+            operand[:, :, inward] = late_ref[:, :, pl.ds((rows - 4) * core, 2)]
 
     def store(begin, end, values):
         operand[:, begin:end, outward] = values
@@ -339,8 +341,11 @@
     earlier = lax.axis_index("tchunk") > 0
 
     def steps():
-        return hide(strip, w1_ref, bias1_ref, gain2_ref, 0, frames - 2, 2, flags, store) + convolved(
-            late_ref, w2_ref, bias2_ref, 0, late, rows - 4, middle
+        left = frames - 2 - made
+        return (
+            hide(first_ref, w1_ref, bias1_ref, gain2_ref, made, left, rows - 2, live[2 + made:], store_last, OWN)
+            + hide(strip, w1_ref, bias1_ref, gain2_ref, 0, frames - 2, 2, flags, store)
+            + convolved(late_ref, w2_ref, bias2_ref, 0, late, rows - 4, middle)
         )
 
     @pl.when(earlier)
@@ -538,12 +543,13 @@
         gain_second.reshape(1, channels), conv_second, bias_second.reshape(1, channels),
     )
     products = -(-(frames - 2) * half * width // OWN)
-    done = -(-(frames - 2) // products) * (products - 1)
+    each = -(-(frames - 2) // products)
+    done = each * (products - 2)
     first, late, raw = pl.pallas_call(
         own_kernel,
         out_shape=(
             shape(3, frames, half + 2, width, LANES), shape(3, done, half, width, LANES),
-            jax.ShapeDtypeStruct((frames - 2 - done, half, width, channels), jnp.float32),
+            jax.ShapeDtypeStruct((each, half, width, channels), jnp.float32),
         ),
         in_specs=[vmem] * 7,
         out_specs=(vmem,) * 3,

time: 18.7 us -> 18.7 us (level)
    pallas_call x1, Pallas kernels: 1.53 us -> 1.23 us  [shards(): pl.pallas_call(own_kernel, out_shape=(shape(3, frames, half + 2, width, L...]
    pallas_call x1, Pallas kernels: 1.4 us -> 1.64 us  [shards(): pl.pallas_call(edge_kernel, out_shape=(shape(3, 2, 2, width, LANES), shap...]
  transfers between devices with their start and end apart: 6 -> 6, of which waited for: 1 -> 1; matrix products, arithmetic and copies ran while one was open for 0% -> 0% of each run, Pallas kernels for 20% -> 19%
where the time goes in v11:
time: 18.7 us; the launch traced here: 18.5 us
  starting transfers between devices  10.4 us (56%)
  Pallas kernels  6.55 us (35%)
  between operations  0.91 us (5%)
  waiting for transfers between devices  0.33 us (2%)
  local copies, waits for them, and re-layouts  0.31 us (2%)
    ppermute x1, starting transfers between devices, shards(): tail_mine = lax.ppermute(tail, axes, straight)  4.41 us
    ppermute x1, starting transfers between devices, shards(): own_edge = lax.ppermute(own_edge, axes, across)  3.56 us
    pallas_call x1, Pallas kernels, shards(): pl.pallas_call(early_kernel, out_shape=(shape(frames, half, side, channel...  2.13 us
    pallas_call x1, Pallas kernels, shards(): pl.pallas_call(edge_kernel, out_shape=(shape(3, 2, 2, width, LANES), shap...  1.64 us
    ppermute x1, starting transfers between devices, shards(): tail_edge = lax.ppermute(tail_edge, axes, diagonal)  1.29 us
    pallas_call x1, Pallas kernels, shards(): pl.pallas_call(own_kernel, out_shape=(shape(3, frames, half + 2, width, L...  1.23 us
    pallas_call x1, Pallas kernels, shards(): pl.pallas_call(keep_kernel, out_shape=shape(*features.shape), in_specs=[v...  0.66 us
    pallas_call x1, Pallas kernels, shards(): pl.pallas_call(got_kernel, out_shape=shape(*features.shape), in_specs=[vm...  0.66 us
  transfers between devices with their start and end apart: 6, of which 1 were waited for; matrix products, arithmetic and copies ran while one was open for 0% of the time, Pallas kernels for 19%

profile of v11, /device:TPU:0, one launch (start us, length us, event | category | flops | bytes accessed | tf_op | source)
XLA Modules:
  0.0 18.5 jit_solution(10853856883118547509)
XLA Ops:
  0.0 0.0 copy-start.2
  0.7 0.3 %copy-done.2 = bf16[8,8,8,192]{3,2,1,0:T(8,128)(2,1)S(1)} copy-done((bf16[8,8,8,192]{3,2,1,0:T(8,128)(2,1)S(1)}, bf16[8,8,8,192]{3,2,1,0:T(8,128)(2,1)}, u32[]{:S(2)}) %copy-start.2) | copy-done | bytes 196632
  1.0 0.1 shard_map.83
  1.1 0.5 %collective-permute-start.1 = (bf16[36,8,384]{2,1,0:T(8,128)(2,1)S(1)}, bf16[36,8,384]{2,1,0:T(8,128)(2,1)S(1)}, u32[]{:S(2)}, u32[]{:S(2)}) collective-permute-start(bf16[36,8,384]{2,1,0:T(8,128)(2,1)S(1)} %get-tuple-element.29), channel_id=1, source_target_pairs={{0,1},{1,0},{2,3},{3,2},{4,5},{5,4},{6,7},{7,6},{8,9},{9,8},{10,11... | collective-permute-start | bytes 663560 | tf_op jit(solution)/shard_map/ppermute | solution.py:529
  1.6 4.4 %collective-permute-start = (bf16[17,8,384]{2,1,0:T(8,128)(2,1)S(1)}, bf16[17,8,384]{2,1,0:T(8,128)(2,1)S(1)}, u32[]{:S(2)}, u32[]{:S(2)}) collective-permute-start(bf16[17,8,384]{2,1,0:T(8,128)(2,1)S(1)} %get-tuple-element.27.tail_ref), channel_id=1, source_target_pairs={{0,8},{1,9},{2,10},{3,11},{4,12},{5,13},{6,14},{7,15},{16,24},{17,... | collective-permute-start | bytes 313352 | tf_op jit(solution)/shard_map/ppermute | solution.py:528
  6.1 0.0 collective-permute-done.1.other_ref
  6.1 0.0 copy-start
  6.1 0.0 copy-start.3
  6.1 0.0 copy-start.4
  6.1 0.0 copy-start.5
  6.2 0.0 copy-start.1
  6.2 0.0 copy-start.6
  6.2 3.6 %collective-permute-start.4 = (bf16[2,8,8,384]{3,2,1,0:T(8,128)(2,1)S(1)}, bf16[2,8,8,384]{3,2,1,0:T(8,128)(2,1)S(1)}, u32[]{:S(2)}, u32[]{:S(2)}) collective-permute-start(bf16[2,8,8,384]{3,2,1,0:T(8,128)(2,1)S(1)} %get-tuple-element.32), channel_id=1, source_target_pairs={{0,3},{3,0},{8,11},{11,8},{2,5},{5,2},{10,13},{13,10},{4,7},{7,4},... | collective-permute-start | bytes 294920 | tf_op jit(solution)/shard_map/ppermute | solution.py:538
  9.7 1.3 %collective-permute-start.3 = (bf16[8,8,384]{2,1,0:T(8,128)(2,1)S(1)}, bf16[8,8,384]{2,1,0:T(8,128)(2,1)S(1)}, u32[]{:S(2)}, u32[]{:S(2)}) collective-permute-start(bf16[8,8,384]{2,1,0:T(8,128)(2,1)S(1)} %get-tuple-element.31), channel_id=1, source_target_pairs={{0,11},{3,8},{2,13},{5,10},{4,15},{7,12},{16,27},{19,24},{18,29},{... | collective-permute-start | bytes 147464 | tf_op jit(solution)/shard_map/ppermute | solution.py:539
  11.0 0.0 copy-done
  11.0 0.0 copy-done.3
  11.1 0.0 copy-done.4
  11.1 0.0 copy-done.5
  11.1 1.2 %shard_map.84 = (bf16[3,8,6,16,128]{4,3,2,1,0:T(8,128)(2,1)S(1)}, bf16[3,2,4,16,128]{4,3,2,1,0:T(8,128)(2,1)S(1)}, f32[2,4,16,192]{3,2,1,0:T(8,128)S(1)}) custom-call(bf16[8,384]{1,0:T(8,128)(2,1)S(1)} %get-tuple-element.26.marks_ref, bf16[8,3,8,384]{3,2,1,0:T(8,128)(2,1)S(1)} %get-tuple-element.28.mine_ref, ...), custom_call_target="tpu_custom_call" | custom-call | flops 764411904 | bytes 4194304 | tf_op jit(solution)/shard_map/pallas_call | solution.py:548
  12.3 0.0 collective-permute-done.tail_ref.tail_mine_ref
  12.3 0.1 collective-permute-start.2
  12.4 0.0 collective-permute-done.4.edge_ref
  12.4 0.0 copy-done.1
  12.4 0.0 copy-done.6
  12.5 1.6 %shard_map.87 = (bf16[3,2,2,16,128]{4,3,2,1,0:T(8,128)(2,1)S(1)}, bf16[3,2,6,16,128]{4,3,2,1,0:T(8,128)(2,1)S(1)}, bf16[4,2,8,192]{3,2,1,0:T(8,128)(2,1)S(1)}, b...) custom-call(bf16[8,384]{1,0:T(8,128)(2,1)S(1)} %get-tuple-element.26.marks_, ...), custom_call_target="tpu_custom_call" | custom-call | flops 1048576 | bytes 1048576 | tf_op jit(solution)/shard_map/pallas_call | solution.py:568
  14.1 0.0 collective-permute-done.3.edge_ref
  14.1 0.0 collective-permute-done.2.tail_other_ref
  14.2 2.1 %shard_map.89 = (bf16[8,4,8,192]{3,2,1,0:T(8,128)(2,1)S(1)}, bf16[8,4,8,192]{3,2,1,0:T(8,128)(2,1)S(1)}) custom-call(bf16[8,384]{1,0:T(8,128)(2,1)S(1)} %get-tuple-element.26.marks_ref, bf16[17,8,384]{2,1,0:T(8,128)(2,1)S(1)} %collective-permute-done.tail_ref.tail_mine_ref, bf16[12,8,384]{2,1,0:T(8,128)(2,1)S(1)} %collective-permute-done.2.tail_other_ref, ...), custom_call_target="tpu_custom_call" | custom-call | flops 1274019840 | bytes 8388608 | tf_op jit(solution)/shard_map/pallas_call | solution.py:593
  16.3 0.5 %collective-permute-start.5 = (bf16[8,4,8,192]{3,2,1,0:T(8,128)(2,1)S(1)}, bf16[8,4,8,192]{3,2,1,0:T(8,128)(2,1)S(1)}, u32[]{:S(2)}, u32[]{:S(2)}) collective-permute-start(bf16[8,4,8,192]{3,2,1,0:T(8,128)(2,1)S(1)} %get-tuple-element.41), channel_id=1, source_target_pairs={{0,1},{1,0},{2,3},{3,2},{4,5},{5,4},{6,7},{7,6},{8,9},{9,8},{10,11... | collective-permute-start | bytes 294920 | tf_op jit(solution)/shard_map/ppermute | solution.py:605
  16.8 0.7 %shard_map.90.kept_ref = bf16[8,8,8,192]{3,2,1,0:T(8,128)(2,1)} custom-call(bf16[8,4,8,192]{3,2,1,0:T(8,128)(2,1)S(1)} %get-tuple-element.42.keep_ref), custom_call_target="tpu_custom_call" | custom-call | flops 268435456 | bytes 1048576 | tf_op jit(solution)/shard_map/pallas_call | solution.py:607
  17.5 0.3 %collective-permute-done.5.got_ref = bf16[8,4,8,192]{3,2,1,0:T(8,128)(2,1)S(1)} collective-permute-done((bf16[8,4,8,192]{3,2,1,0:T(8,128)(2,1)S(1)}, bf16[8,4,8,192]{3,2,1,0:T(8,128)(2,1)S(1)}, u32[]{:S(2)}, u32[]{:S(2)}) %collective-permute-start.5) | collective-permute-done | bytes 98336 | tf_op jit(solution)/shard_map/ppermute | solution.py:605
  17.8 0.7 %shard_map.91 = bf16[8,8,8,192]{3,2,1,0:T(8,128)(2,1)} custom-call(bf16[8,4,8,192]{3,2,1,0:T(8,128)(2,1)S(1)} %collective-permute-done.5.got_ref, bf16[8,8,8,192]{3,2,1,0:T(8,128)(2,1)} %shard_map.90.kept_ref), custom_call_target="tpu_custom_call", output_to_operand_aliasing={{}: (1, {})} | custom-call | tf_op jit(solution)/shard_map/pallas_call | solution.py:616
  (4 shorter events, 0.1 us)
Async XLA Ops:
  0.0 1.0 %copy-start.2 = (bf16[8,8,8,192]{3,2,1,0:T(8,128)(2,1)S(1)}, bf16[8,8,8,192]{3,2,1,0:T(8,128)(2,1)}, u32[]{:S(2)}) copy-start(bf16[8,8,8,192]{3,2,1,0:T(8,128)(2,1)} %raw.1) | copy-start | bytes 589828
  1.1 4.9 %collective-permute-start.1 = (bf16[36,8,384]{2,1,0:T(8,128)(2,1)S(1)}, bf16[36,8,384]{2,1,0:T(8,128)(2,1)S(1)}, u32[]{:S(2)}, u32[]{:S(2)}) collective-permute-start(bf16[36,8,384]{2,1,0:T(8,128)(2,1)S(1)} %get-tuple-element.29), channel_id=1, source_target_pairs={{0,1},{1,0},{2,3},{3,2},{4,5},{5,4},{6,7},{7,6},{8,9},{9,8},{10,11... | collective-permute-start | bytes 663560 | tf_op jit(solution)/shard_map/ppermute | solution.py:529
  1.6 10.7 %collective-permute-start = (bf16[17,8,384]{2,1,0:T(8,128)(2,1)S(1)}, bf16[17,8,384]{2,1,0:T(8,128)(2,1)S(1)}, u32[]{:S(2)}, u32[]{:S(2)}) collective-permute-start(bf16[17,8,384]{2,1,0:T(8,128)(2,1)S(1)} %get-tuple-element.27.tail_ref), channel_id=1, source_target_pairs={{0,8},{1,9},{2,10},{3,11},{4,12},{5,13},{6,14},{7,15},{16,24},{17,... | collective-permute-start | bytes 313352 | tf_op jit(solution)/shard_map/ppermute | solution.py:528
  6.1 5.0 %copy-start = (bf16[3,3,3,192,192]{4,3,2,1,0:T(8,128)(2,1)S(1)}, bf16[3,3,3,192,192]{4,3,2,1,0:T(8,128)(2,1)}, u32[]{:S(2)}) copy-start(bf16[3,3,3,192,192]{4,3,2,1,0:T(8,128)(2,1)} %w1_ref.5) | copy-start | bytes 5971972
  6.1 5.0 %copy-start.3 = (f32[192]{0:T(256)S(1)}, f32[192]{0:T(256)}, u32[]{:S(2)}) copy-start(f32[192]{0:T(256)} %param.10) | copy-start | bytes 2308
  6.1 5.0 %copy-start.4 = (f32[192]{0:T(256)S(1)}, f32[192]{0:T(256)}, u32[]{:S(2)}) copy-start(f32[192]{0:T(256)} %param.12) | copy-start | bytes 2308
  6.1 5.0 %copy-start.5 = (f32[192]{0:T(256)S(1)}, f32[192]{0:T(256)}, u32[]{:S(2)}) copy-start(f32[192]{0:T(256)} %param.13) | copy-start | bytes 2308
  6.2 6.3 %copy-start.1 = (bf16[3,3,3,192,192]{4,3,2,1,0:T(8,128)(2,1)S(1)}, bf16[3,3,3,192,192]{4,3,2,1,0:T(8,128)(2,1)}, u32[]{:S(2)}) copy-start(bf16[3,3,3,192,192]{4,3,2,1,0:T(8,128)(2,1)} %w2_ref.3) | copy-start | bytes 5971972
  6.2 6.3 %copy-start.6 = (f32[192]{0:T(256)S(1)}, f32[192]{0:T(256)}, u32[]{:S(2)}) copy-start(f32[192]{0:T(256)} %param.15) | copy-start | bytes 2308
  6.2 6.3 %collective-permute-start.4 = (bf16[2,8,8,384]{3,2,1,0:T(8,128)(2,1)S(1)}, bf16[2,8,8,384]{3,2,1,0:T(8,128)(2,1)S(1)}, u32[]{:S(2)}, u32[]{:S(2)}) collective-permute-start(bf16[2,8,8,384]{3,2,1,0:T(8,128)(2,1)S(1)} %get-tuple-element.32), channel_id=1, source_target_pairs={{0,3},{3,0},{8,11},{11,8},{2,5},{5,2},{10,13},{13,10},{4,7},{7,4},... | collective-permute-start | bytes 294920 | tf_op jit(solution)/shard_map/ppermute | solution.py:538
  9.7 4.4 %collective-permute-start.3 = (bf16[8,8,384]{2,1,0:T(8,128)(2,1)S(1)}, bf16[8,8,384]{2,1,0:T(8,128)(2,1)S(1)}, u32[]{:S(2)}, u32[]{:S(2)}) collective-permute-start(bf16[8,8,384]{2,1,0:T(8,128)(2,1)S(1)} %get-tuple-element.31), channel_id=1, source_target_pairs={{0,11},{3,8},{2,13},{5,10},{4,15},{7,12},{16,27},{19,24},{18,29},{... | collective-permute-start | bytes 147464 | tf_op jit(solution)/shard_map/ppermute | solution.py:539
  12.3 1.8 %collective-permute-start.2 = (bf16[12,8,384]{2,1,0:T(8,128)(2,1)S(1)}, bf16[12,8,384]{2,1,0:T(8,128)(2,1)S(1)}, u32[]{:S(2)}, u32[]{:S(2)}) collective-permute-start(bf16[12,8,384]{2,1,0:T(8,128)(2,1)S(1)} %shard_map.85), channel_id=1, source_target_pairs={{0,1},{1,0},{2,3},{3,2},{4,5},{5,4},{6,7},{7,6},{8,9},{9,8},{10,11... | collective-permute-start | bytes 221192 | tf_op jit(solution)/shard_map/ppermute | solution.py:567
  16.3 1.5 %collective-permute-start.5 = (bf16[8,4,8,192]{3,2,1,0:T(8,128)(2,1)S(1)}, bf16[8,4,8,192]{3,2,1,0:T(8,128)(2,1)S(1)}, u32[]{:S(2)}, u32[]{:S(2)}) collective-permute-start(bf16[8,4,8,192]{3,2,1,0:T(8,128)(2,1)S(1)} %get-tuple-element.41), channel_id=1, source_target_pairs={{0,1},{1,0},{2,3},{3,2},{4,5},{5,4},{6,7},{7,6},{8,9},{9,8},{10,11... | collective-permute-start | bytes 294920 | tf_op jit(solution)/shard_map/ppermute | solution.py:605

commit v12 on v11

--- a/solution.py
+++ b/solution.py
@@ -261,18 +261,15 @@
     return jnp.where((row == (rows - 1) * core) & jnp.logical_not(inside), 0.0, 1.0)
 
 
-def other_rows_kernel(tail_ref, late_ref, rest_ref):
-    pairs, held = tail_ref.shape[0] // CACHE, rest_ref.shape[0] // CACHE
-    first = (1 - lower_part()) * (pairs - held)
-    for slot in range(CACHE):
-        rest_ref[slot * held:(slot + 1) * held] = tail_ref[pl.ds(slot * pairs + first, held)]
-
-
 def own_kernel(
-    marks_ref, mine_ref, other_ref, gain1_ref, w1_ref, bias1_ref, gain2_ref,
-    first_ref, late_ref, raw_ref,
+    marks_ref, tail_ref, mine_ref, other_ref, gain1_ref, w1_ref, bias1_ref, gain2_ref,
+    first_ref, late_ref, raw_ref, rest_ref,
 ):
     frames, pairs, side, packed = mine_ref.shape
+    whole = tail_ref.shape[0] // CACHE
+    place = (1 - lower_part()) * (whole - pairs)
+    for slot in range(CACHE):
+        rest_ref[slot * pairs:(slot + 1) * pairs] = tail_ref[pl.ds(slot * whole + place, pairs)]
     live = frame_flags(marks_ref[...], range(2, frames))
 
     def fill(start, end):
@@ -442,8 +439,8 @@
 
     @pl.when(jnp.logical_not(earlier))
     def _():
-        plane[:, 0:CACHE, pl.ds(middle, rows)] = jnp.zeros(
-            plane.shape[:1] + (CACHE, rows) + plane.shape[3:], plane.dtype
+        plane[:, 2:CACHE, pl.ds(middle, rows)] = jnp.zeros(
+            plane.shape[:1] + (CACHE - 2, rows) + plane.shape[3:], plane.dtype
         )
         operand[:, 0:2] = jnp.zeros(operand.shape[:1] + (2,) + operand.shape[2:], operand.dtype)
         border = convolved(late_operand_ref, w2_ref, bias2_ref, 0, late_border_ref.shape[0], 2, late_border)
@@ -545,25 +542,17 @@
     products = -(-(frames - 2) * half * width // OWN)
     each = -(-(frames - 2) // products)
     done = each * (products - 2)
-    first, late, raw = pl.pallas_call(
+    first, late, raw, rest = pl.pallas_call(
         own_kernel,
         out_shape=(
             shape(3, frames, half + 2, width, LANES), shape(3, done, half, width, LANES),
-            jax.ShapeDtypeStruct((each, half, width, channels), jnp.float32),
+            jax.ShapeDtypeStruct((each, half, width, channels), jnp.float32), shape(tiles, side, packed),
         ),
-        in_specs=[vmem] * 7,
-        out_specs=(vmem,) * 3,
+        in_specs=[vmem] * 8,
+        out_specs=(vmem,) * 4,
         compiler_params=limit,
         cost_estimate=cost(work * (frames - 2) * half, 4 * 2**20),
-    )(marks, mine, other, *weights[:4])
-    rest = pl.pallas_call(
-        other_rows_kernel,
-        out_shape=shape(tiles, side, packed),
-        in_specs=[vmem, pl.BlockSpec(memory_space=pl.ANY)],
-        out_specs=vmem,
-        compiler_params=limit,
-        cost_estimate=cost(1, 1),
-    )(tail_mine, late)
+    )(marks, tail_mine, mine, other, *weights[:4])
     tail_other = lax.ppermute(rest, "wa", swap)
     strip, hidden, keep, send, border, late = pl.pallas_call(
         edge_kernel,

time: 18.7 us -> 18.5 us (0.989)
  no operation moved by 1% of the time
where the time goes in v12:
time: 18.5 us; the launch traced here: 18.3 us
  starting transfers between devices  10.4 us (56%)
  Pallas kernels  6.41 us (35%)
  between operations  0.91 us (5%)
  waiting for transfers between devices  0.33 us (2%)
  local copies, waits for them, and re-layouts  0.31 us (2%)
    ppermute x1, starting transfers between devices, shards(): tail_mine = lax.ppermute(tail, axes, straight)  4.41 us
    ppermute x1, starting transfers between devices, shards(): own_edge = lax.ppermute(own_edge, axes, across)  3.56 us
    pallas_call x1, Pallas kernels, shards(): pl.pallas_call(early_kernel, out_shape=(shape(frames, half, side, channel...  2.04 us
    pallas_call x1, Pallas kernels, shards(): pl.pallas_call(edge_kernel, out_shape=(shape(3, 2, 2, width, LANES), shap...  1.61 us
    ppermute x1, starting transfers between devices, shards(): tail_edge = lax.ppermute(tail_edge, axes, diagonal)  1.29 us
    pallas_call x1, Pallas kernels, shards(): pl.pallas_call(own_kernel, out_shape=(shape(3, frames, half + 2, width, L...  1.22 us
    pallas_call x1, Pallas kernels, shards(): pl.pallas_call(keep_kernel, out_shape=shape(*features.shape), in_specs=[v...  0.66 us
    pallas_call x1, Pallas kernels, shards(): pl.pallas_call(got_kernel, out_shape=shape(*features.shape), in_specs=[vm...  0.66 us
  transfers between devices with their start and end apart: 6, of which 1 were waited for; matrix products, arithmetic and copies ran while one was open for 0% of the time, Pallas kernels for 19%

profile of v12, /device:TPU:0, one launch (start us, length us, event | category | flops | bytes accessed | tf_op | source)
XLA Modules:
  0.0 18.3 jit_solution(3943070393564858329)
XLA Ops:
  0.0 0.0 copy-start.2
  0.7 0.3 %copy-done.2 = bf16[8,8,8,192]{3,2,1,0:T(8,128)(2,1)S(1)} copy-done((bf16[8,8,8,192]{3,2,1,0:T(8,128)(2,1)S(1)}, bf16[8,8,8,192]{3,2,1,0:T(8,128)(2,1)}, u32[]{:S(2)}) %copy-start.2) | copy-done | bytes 196632
  1.0 0.1 shard_map.83
  1.1 0.5 %collective-permute-start.1 = (bf16[36,8,384]{2,1,0:T(8,128)(2,1)S(1)}, bf16[36,8,384]{2,1,0:T(8,128)(2,1)S(1)}, u32[]{:S(2)}, u32[]{:S(2)}) collective-permute-start(bf16[36,8,384]{2,1,0:T(8,128)(2,1)S(1)} %get-tuple-element.30), channel_id=1, source_target_pairs={{0,1},{1,0},{2,3},{3,2},{4,5},{5,4},{6,7},{7,6},{8,9},{9,8},{10,11... | collective-permute-start | bytes 663560 | tf_op jit(solution)/shard_map/ppermute | solution.py:526
  1.6 4.4 %collective-permute-start = (bf16[17,8,384]{2,1,0:T(8,128)(2,1)S(1)}, bf16[17,8,384]{2,1,0:T(8,128)(2,1)S(1)}, u32[]{:S(2)}, u32[]{:S(2)}) collective-permute-start(bf16[17,8,384]{2,1,0:T(8,128)(2,1)S(1)} %get-tuple-element.28.tail_ref), channel_id=1, source_target_pairs={{0,8},{1,9},{2,10},{3,11},{4,12},{5,13},{6,14},{7,15},{16,24},{17,... | collective-permute-start | bytes 313352 | tf_op jit(solution)/shard_map/ppermute | solution.py:525
  6.1 0.0 collective-permute-done.1.other_ref
  6.1 0.0 copy-start
  6.1 0.0 copy-start.3
  6.1 0.0 copy-start.4
  6.1 0.0 copy-start.5
  6.2 0.0 copy-start.1
  6.2 0.0 copy-start.6
  6.2 3.6 %collective-permute-start.4 = (bf16[2,8,8,384]{3,2,1,0:T(8,128)(2,1)S(1)}, bf16[2,8,8,384]{3,2,1,0:T(8,128)(2,1)S(1)}, u32[]{:S(2)}, u32[]{:S(2)}) collective-permute-start(bf16[2,8,8,384]{3,2,1,0:T(8,128)(2,1)S(1)} %get-tuple-element.33), channel_id=1, source_target_pairs={{0,3},{3,0},{8,11},{11,8},{2,5},{5,2},{10,13},{13,10},{4,7},{7,4},... | collective-permute-start | bytes 294920 | tf_op jit(solution)/shard_map/ppermute | solution.py:535
  9.7 1.3 %collective-permute-start.3 = (bf16[8,8,384]{2,1,0:T(8,128)(2,1)S(1)}, bf16[8,8,384]{2,1,0:T(8,128)(2,1)S(1)}, u32[]{:S(2)}, u32[]{:S(2)}) collective-permute-start(bf16[8,8,384]{2,1,0:T(8,128)(2,1)S(1)} %get-tuple-element.32), channel_id=1, source_target_pairs={{0,11},{3,8},{2,13},{5,10},{4,15},{7,12},{16,27},{19,24},{18,29},{... | collective-permute-start | bytes 147464 | tf_op jit(solution)/shard_map/ppermute | solution.py:536
  11.0 0.0 collective-permute-done.tail_ref.tail_mine_ref
  11.1 0.0 copy-done
  11.1 0.0 copy-done.3
  11.1 0.0 copy-done.4
  11.1 0.0 copy-done.5
  11.1 1.2 %shard_map.84 = (bf16[3,8,6,16,128]{4,3,2,1,0:T(8,128)(2,1)S(1)}, bf16[3,2,4,16,128]{4,3,2,1,0:T(8,128)(2,1)S(1)}, f32[2,4,16,192]{3,2,1,0:T(8,128)S(1)}, bf16[12,8,384]{2,1,0:T(8,128)(2,1)S(1)}) custom-call(bf16[8,384]{1,0:T(8,128)(2,1)S(1)} %get-tuple-element.27.marks_ref, bf16[17,8,384]{2,1,0:T(8,128)(2,1)S(1)} %collective-permute-done.tail_ref.tail_mine_ref, ...), custom_call_target="tpu_custom_call" | custom-call | flops 764411904 | bytes 4194304 | tf_op jit(solution)/shard_map/pallas_call | solution.py:545
  12.3 0.1 collective-permute-start.2
  12.4 0.0 collective-permute-done.4.edge_ref
  12.4 0.0 copy-done.1
  12.4 0.0 copy-done.6
  12.4 1.6 %shard_map.86 = (bf16[3,2,2,16,128]{4,3,2,1,0:T(8,128)(2,1)S(1)}, bf16[3,2,6,16,128]{4,3,2,1,0:T(8,128)(2,1)S(1)}, bf16[4,2,8,192]{3,2,1,0:T(8,128)(2,1)S(1)}, b...) custom-call(bf16[8,384]{1,0:T(8,128)(2,1)S(1)} %get-tuple-element.27.marks_, ...), custom_call_target="tpu_custom_call" | custom-call | flops 1048576 | bytes 1048576 | tf_op jit(solution)/shard_map/pallas_call | solution.py:557
  14.0 0.0 collective-permute-done.3.edge_ref
  14.1 0.0 collective-permute-done.2.tail_other_ref
  14.1 2.0 %shard_map.88 = (bf16[8,4,8,192]{3,2,1,0:T(8,128)(2,1)S(1)}, bf16[8,4,8,192]{3,2,1,0:T(8,128)(2,1)S(1)}) custom-call(bf16[8,384]{1,0:T(8,128)(2,1)S(1)} %get-tuple-element.27.marks_ref, bf16[17,8,384]{2,1,0:T(8,128)(2,1)S(1)} %collective-permute-done.tail_ref.tail_mine_ref, bf16[12,8,384]{2,1,0:T(8,128)(2,1)S(1)} %collective-permute-done.2.tail_other_ref, ...), custom_call_target="tpu_custom_call" | custom-call | flops 1274019840 | bytes 8388608 | tf_op jit(solution)/shard_map/pallas_call | solution.py:582
  16.1 0.5 %collective-permute-start.5 = (bf16[8,4,8,192]{3,2,1,0:T(8,128)(2,1)S(1)}, bf16[8,4,8,192]{3,2,1,0:T(8,128)(2,1)S(1)}, u32[]{:S(2)}, u32[]{:S(2)}) collective-permute-start(bf16[8,4,8,192]{3,2,1,0:T(8,128)(2,1)S(1)} %get-tuple-element.43), channel_id=1, source_target_pairs={{0,1},{1,0},{2,3},{3,2},{4,5},{5,4},{6,7},{7,6},{8,9},{9,8},{10,11... | collective-permute-start | bytes 294920 | tf_op jit(solution)/shard_map/ppermute | solution.py:594
  16.7 0.7 %shard_map.89.kept_ref = bf16[8,8,8,192]{3,2,1,0:T(8,128)(2,1)} custom-call(bf16[8,4,8,192]{3,2,1,0:T(8,128)(2,1)S(1)} %get-tuple-element.44.keep_ref), custom_call_target="tpu_custom_call" | custom-call | flops 268435456 | bytes 1048576 | tf_op jit(solution)/shard_map/pallas_call | solution.py:596
  17.3 0.3 %collective-permute-done.5.got_ref = bf16[8,4,8,192]{3,2,1,0:T(8,128)(2,1)S(1)} collective-permute-done((bf16[8,4,8,192]{3,2,1,0:T(8,128)(2,1)S(1)}, bf16[8,4,8,192]{3,2,1,0:T(8,128)(2,1)S(1)}, u32[]{:S(2)}, u32[]{:S(2)}) %collective-permute-start.5) | collective-permute-done | bytes 98336 | tf_op jit(solution)/shard_map/ppermute | solution.py:594
  17.7 0.7 %shard_map.90 = bf16[8,8,8,192]{3,2,1,0:T(8,128)(2,1)} custom-call(bf16[8,4,8,192]{3,2,1,0:T(8,128)(2,1)S(1)} %collective-permute-done.5.got_ref, bf16[8,8,8,192]{3,2,1,0:T(8,128)(2,1)} %shard_map.89.kept_ref), custom_call_target="tpu_custom_call", output_to_operand_aliasing={{}: (1, {})} | custom-call | tf_op jit(solution)/shard_map/pallas_call | solution.py:605
  (3 shorter events, 0.1 us)
Async XLA Ops:
  0.0 1.0 %copy-start.2 = (bf16[8,8,8,192]{3,2,1,0:T(8,128)(2,1)S(1)}, bf16[8,8,8,192]{3,2,1,0:T(8,128)(2,1)}, u32[]{:S(2)}) copy-start(bf16[8,8,8,192]{3,2,1,0:T(8,128)(2,1)} %raw.1) | copy-start | bytes 589828
  1.1 4.9 %collective-permute-start.1 = (bf16[36,8,384]{2,1,0:T(8,128)(2,1)S(1)}, bf16[36,8,384]{2,1,0:T(8,128)(2,1)S(1)}, u32[]{:S(2)}, u32[]{:S(2)}) collective-permute-start(bf16[36,8,384]{2,1,0:T(8,128)(2,1)S(1)} %get-tuple-element.30), channel_id=1, source_target_pairs={{0,1},{1,0},{2,3},{3,2},{4,5},{5,4},{6,7},{7,6},{8,9},{9,8},{10,11... | collective-permute-start | bytes 663560 | tf_op jit(solution)/shard_map/ppermute | solution.py:526
  1.6 9.4 %collective-permute-start = (bf16[17,8,384]{2,1,0:T(8,128)(2,1)S(1)}, bf16[17,8,384]{2,1,0:T(8,128)(2,1)S(1)}, u32[]{:S(2)}, u32[]{:S(2)}) collective-permute-start(bf16[17,8,384]{2,1,0:T(8,128)(2,1)S(1)} %get-tuple-element.28.tail_ref), channel_id=1, source_target_pairs={{0,8},{1,9},{2,10},{3,11},{4,12},{5,13},{6,14},{7,15},{16,24},{17,... | collective-permute-start | bytes 313352 | tf_op jit(solution)/shard_map/ppermute | solution.py:525
  6.1 5.0 %copy-start = (bf16[3,3,3,192,192]{4,3,2,1,0:T(8,128)(2,1)S(1)}, bf16[3,3,3,192,192]{4,3,2,1,0:T(8,128)(2,1)}, u32[]{:S(2)}) copy-start(bf16[3,3,3,192,192]{4,3,2,1,0:T(8,128)(2,1)} %w1_ref.5) | copy-start | bytes 5971972
  6.1 5.0 %copy-start.3 = (f32[192]{0:T(256)S(1)}, f32[192]{0:T(256)}, u32[]{:S(2)}) copy-start(f32[192]{0:T(256)} %param.10) | copy-start | bytes 2308
  6.1 5.0 %copy-start.4 = (f32[192]{0:T(256)S(1)}, f32[192]{0:T(256)}, u32[]{:S(2)}) copy-start(f32[192]{0:T(256)} %param.12) | copy-start | bytes 2308
  6.1 5.0 %copy-start.5 = (f32[192]{0:T(256)S(1)}, f32[192]{0:T(256)}, u32[]{:S(2)}) copy-start(f32[192]{0:T(256)} %param.13) | copy-start | bytes 2308
  6.2 6.3 %copy-start.1 = (bf16[3,3,3,192,192]{4,3,2,1,0:T(8,128)(2,1)S(1)}, bf16[3,3,3,192,192]{4,3,2,1,0:T(8,128)(2,1)}, u32[]{:S(2)}) copy-start(bf16[3,3,3,192,192]{4,3,2,1,0:T(8,128)(2,1)} %w2_ref.3) | copy-start | bytes 5971972
  6.2 6.3 %copy-start.6 = (f32[192]{0:T(256)S(1)}, f32[192]{0:T(256)}, u32[]{:S(2)}) copy-start(f32[192]{0:T(256)} %param.15) | copy-start | bytes 2308
  6.2 6.2 %collective-permute-start.4 = (bf16[2,8,8,384]{3,2,1,0:T(8,128)(2,1)S(1)}, bf16[2,8,8,384]{3,2,1,0:T(8,128)(2,1)S(1)}, u32[]{:S(2)}, u32[]{:S(2)}) collective-permute-start(bf16[2,8,8,384]{3,2,1,0:T(8,128)(2,1)S(1)} %get-tuple-element.33), channel_id=1, source_target_pairs={{0,3},{3,0},{8,11},{11,8},{2,5},{5,2},{10,13},{13,10},{4,7},{7,4},... | collective-permute-start | bytes 294920 | tf_op jit(solution)/shard_map/ppermute | solution.py:535
  9.7 4.3 %collective-permute-start.3 = (bf16[8,8,384]{2,1,0:T(8,128)(2,1)S(1)}, bf16[8,8,384]{2,1,0:T(8,128)(2,1)S(1)}, u32[]{:S(2)}, u32[]{:S(2)}) collective-permute-start(bf16[8,8,384]{2,1,0:T(8,128)(2,1)S(1)} %get-tuple-element.32), channel_id=1, source_target_pairs={{0,11},{3,8},{2,13},{5,10},{4,15},{7,12},{16,27},{19,24},{18,29},{... | collective-permute-start | bytes 147464 | tf_op jit(solution)/shard_map/ppermute | solution.py:536
  12.3 1.8 %collective-permute-start.2 = (bf16[12,8,384]{2,1,0:T(8,128)(2,1)S(1)}, bf16[12,8,384]{2,1,0:T(8,128)(2,1)S(1)}, u32[]{:S(2)}, u32[]{:S(2)}) collective-permute-start(bf16[12,8,384]{2,1,0:T(8,128)(2,1)S(1)} %get-tuple-element.31), channel_id=1, source_target_pairs={{0,1},{1,0},{2,3},{3,2},{4,5},{5,4},{6,7},{7,6},{8,9},{9,8},{10,11... | collective-permute-start | bytes 221192 | tf_op jit(solution)/shard_map/ppermute | solution.py:556
  16.1 1.5 %collective-permute-start.5 = (bf16[8,4,8,192]{3,2,1,0:T(8,128)(2,1)S(1)}, bf16[8,4,8,192]{3,2,1,0:T(8,128)(2,1)S(1)}, u32[]{:S(2)}, u32[]{:S(2)}) collective-permute-start(bf16[8,4,8,192]{3,2,1,0:T(8,128)(2,1)S(1)} %get-tuple-element.43), channel_id=1, source_target_pairs={{0,1},{1,0},{2,3},{3,2},{4,5},{5,4},{6,7},{7,6},{8,9},{9,8},{10,11... | collective-permute-start | bytes 294920 | tf_op jit(solution)/shard_map/ppermute | solution.py:594

commit v13 on v12

--- a/solution.py
+++ b/solution.py
@@ -313,6 +313,8 @@
         late_ref[:, 0:done] = done_ref[...]
         flag = jnp.concatenate(live[2 + done:2 + made], axis=0)
         late_ref[:, done:made] = second_rows(raw_ref[...], flag, gain2_ref, gain2_ref.shape[-1])
+        strip_ref[...] = strip[:, 0:2, outward]
+        hidden_ref[:, :, pl.ds(2 * (1 - core), rows - 2)] = late_ref[:, 0:2]
 
     def store_last(begin, end, values):
         late_ref[:, made + begin:made + end] = values
@@ -353,8 +355,6 @@
     def _():
         in_turn(steps(), activate)
 
-    strip_ref[...] = strip[:, 0:2, outward]
-    hidden_ref[:, :, pl.ds(2 * (1 - core), rows - 2)] = late_ref[:, 0:2]
     hidden_ref[:, :, pl.ds((rows - 2) * core, 2)] = operand[:, 0:2, outward]
 
 
@@ -389,7 +389,6 @@
 
     plane[:, CACHE:, pl.ds(middle, rows)] = first_ref[:, 0:2]
     plane[:, :, pl.ds(border, 2)] = edge_ref[...]
-    operand[:, CACHE:] = hidden_ref[...]
 
     def put(ref, offset=0):
         def store(frame, row, value):
@@ -402,6 +401,7 @@
         finish(mine_ref, other_ref, live, CACHE + start, ((held - 1) * core, 1), result, targets)
 
     def late_middle():
+        operand[:, CACHE:] = hidden_ref[...]
         for source, target in ((late_keep_ref, keep_ref), (late_send_ref, send_ref)):
             target[CACHE:, pl.ds(2 * (1 - core), rows - 4)] = source[...]
 
@@ -442,9 +442,13 @@
         plane[:, 2:CACHE, pl.ds(middle, rows)] = jnp.zeros(
             plane.shape[:1] + (CACHE - 2, rows) + plane.shape[3:], plane.dtype
         )
-        operand[:, 0:2] = jnp.zeros(operand.shape[:1] + (2,) + operand.shape[2:], operand.dtype)
+
+        def beside():
+            operand[:, 0:2] = jnp.zeros(operand.shape[:1] + (2,) + operand.shape[2:], operand.dtype)
+            late_middle()
+
         border = convolved(late_operand_ref, w2_ref, bias2_ref, 0, late_border_ref.shape[0], 2, late_border)
-        in_turn(hidden_steps(2, live[0:2]) + border + result_steps()[::-1], late_middle)
+        in_turn(hidden_steps(2, live[0:2]) + border + result_steps()[::-1], beside)
 
 
 def keep_kernel(keep_ref, result_ref, arrived):

time: 18.5 us -> 18.5 us (level)
  no operation moved by 1% of the time
where the time goes in v13:
time: 18.5 us; the launch traced here: 18.3 us
  starting transfers between devices  10.4 us (56%)
  Pallas kernels  6.39 us (35%)
  between operations  0.91 us (5%)
  waiting for transfers between devices  0.33 us (2%)
  local copies, waits for them, and re-layouts  0.31 us (2%)
    ppermute x1, starting transfers between devices, shards(): tail_mine = lax.ppermute(tail, axes, straight)  4.41 us
    ppermute x1, starting transfers between devices, shards(): own_edge = lax.ppermute(own_edge, axes, across)  3.56 us
    pallas_call x1, Pallas kernels, shards(): pl.pallas_call(early_kernel, out_shape=(shape(frames, half, side, channel...  2.04 us
    pallas_call x1, Pallas kernels, shards(): pl.pallas_call(edge_kernel, out_shape=(shape(3, 2, 2, width, LANES), shap...  1.59 us
    ppermute x1, starting transfers between devices, shards(): tail_edge = lax.ppermute(tail_edge, axes, diagonal)  1.29 us
    pallas_call x1, Pallas kernels, shards(): pl.pallas_call(own_kernel, out_shape=(shape(3, frames, half + 2, width, L...  1.22 us
    pallas_call x1, Pallas kernels, shards(): pl.pallas_call(keep_kernel, out_shape=shape(*features.shape), in_specs=[v...  0.66 us
    pallas_call x1, Pallas kernels, shards(): pl.pallas_call(got_kernel, out_shape=shape(*features.shape), in_specs=[vm...  0.66 us
  transfers between devices with their start and end apart: 6, of which 1 were waited for; matrix products, arithmetic and copies ran while one was open for 0% of the time, Pallas kernels for 19%

profile of v13, /device:TPU:0, one launch (start us, length us, event | category | flops | bytes accessed | tf_op | source)
XLA Modules:
  0.0 18.3 jit_solution(9033379503987787303)
XLA Ops:
  0.0 0.0 copy-start.2
  0.7 0.3 %copy-done.2 = bf16[8,8,8,192]{3,2,1,0:T(8,128)(2,1)S(1)} copy-done((bf16[8,8,8,192]{3,2,1,0:T(8,128)(2,1)S(1)}, bf16[8,8,8,192]{3,2,1,0:T(8,128)(2,1)}, u32[]{:S(2)}) %copy-start.2) | copy-done | bytes 196632
  1.0 0.1 shard_map.83
  1.1 0.5 %collective-permute-start.1 = (bf16[36,8,384]{2,1,0:T(8,128)(2,1)S(1)}, bf16[36,8,384]{2,1,0:T(8,128)(2,1)S(1)}, u32[]{:S(2)}, u32[]{:S(2)}) collective-permute-start(bf16[36,8,384]{2,1,0:T(8,128)(2,1)S(1)} %get-tuple-element.30), channel_id=1, source_target_pairs={{0,1},{1,0},{2,3},{3,2},{4,5},{5,4},{6,7},{7,6},{8,9},{9,8},{10,11... | collective-permute-start | bytes 663560 | tf_op jit(solution)/shard_map/ppermute | solution.py:530
  1.6 4.4 %collective-permute-start = (bf16[17,8,384]{2,1,0:T(8,128)(2,1)S(1)}, bf16[17,8,384]{2,1,0:T(8,128)(2,1)S(1)}, u32[]{:S(2)}, u32[]{:S(2)}) collective-permute-start(bf16[17,8,384]{2,1,0:T(8,128)(2,1)S(1)} %get-tuple-element.28.tail_ref), channel_id=1, source_target_pairs={{0,8},{1,9},{2,10},{3,11},{4,12},{5,13},{6,14},{7,15},{16,24},{17,... | collective-permute-start | bytes 313352 | tf_op jit(solution)/shard_map/ppermute | solution.py:529
  6.1 0.0 collective-permute-done.1.other_ref
  6.1 0.0 copy-start
  6.1 0.0 copy-start.3
  6.1 0.0 copy-start.4
  6.1 0.0 copy-start.5
  6.2 0.0 copy-start.1
  6.2 0.0 copy-start.6
  6.2 3.6 %collective-permute-start.4 = (bf16[2,8,8,384]{3,2,1,0:T(8,128)(2,1)S(1)}, bf16[2,8,8,384]{3,2,1,0:T(8,128)(2,1)S(1)}, u32[]{:S(2)}, u32[]{:S(2)}) collective-permute-start(bf16[2,8,8,384]{3,2,1,0:T(8,128)(2,1)S(1)} %get-tuple-element.33), channel_id=1, source_target_pairs={{0,3},{3,0},{8,11},{11,8},{2,5},{5,2},{10,13},{13,10},{4,7},{7,4},... | collective-permute-start | bytes 294920 | tf_op jit(solution)/shard_map/ppermute | solution.py:539
  9.7 1.3 %collective-permute-start.3 = (bf16[8,8,384]{2,1,0:T(8,128)(2,1)S(1)}, bf16[8,8,384]{2,1,0:T(8,128)(2,1)S(1)}, u32[]{:S(2)}, u32[]{:S(2)}) collective-permute-start(bf16[8,8,384]{2,1,0:T(8,128)(2,1)S(1)} %get-tuple-element.32), channel_id=1, source_target_pairs={{0,11},{3,8},{2,13},{5,10},{4,15},{7,12},{16,27},{19,24},{18,29},{... | collective-permute-start | bytes 147464 | tf_op jit(solution)/shard_map/ppermute | solution.py:540
  11.0 0.0 collective-permute-done.tail_ref.tail_mine_ref
  11.1 0.0 copy-done
  11.1 0.0 copy-done.3
  11.1 0.0 copy-done.4
  11.1 0.0 copy-done.5
  11.1 1.2 %shard_map.84 = (bf16[3,8,6,16,128]{4,3,2,1,0:T(8,128)(2,1)S(1)}, bf16[3,2,4,16,128]{4,3,2,1,0:T(8,128)(2,1)S(1)}, f32[2,4,16,192]{3,2,1,0:T(8,128)S(1)}, bf16[12,8,384]{2,1,0:T(8,128)(2,1)S(1)}) custom-call(bf16[8,384]{1,0:T(8,128)(2,1)S(1)} %get-tuple-element.27.marks_ref, bf16[17,8,384]{2,1,0:T(8,128)(2,1)S(1)} %collective-permute-done.tail_ref.tail_mine_ref, ...), custom_call_target="tpu_custom_call" | custom-call | flops 764411904 | bytes 4194304 | tf_op jit(solution)/shard_map/pallas_call | solution.py:549
  12.3 0.1 collective-permute-start.2
  12.4 0.0 collective-permute-done.4.edge_ref
  12.4 0.0 copy-done.1
  12.4 0.0 copy-done.6
  12.4 1.6 %shard_map.86 = (bf16[3,2,2,16,128]{4,3,2,1,0:T(8,128)(2,1)S(1)}, bf16[3,2,6,16,128]{4,3,2,1,0:T(8,128)(2,1)S(1)}, bf16[4,2,8,192]{3,2,1,0:T(8,128)(2,1)S(1)}, b...) custom-call(bf16[8,384]{1,0:T(8,128)(2,1)S(1)} %get-tuple-element.27.marks_, ...), custom_call_target="tpu_custom_call" | custom-call | flops 1048576 | bytes 1048576 | tf_op jit(solution)/shard_map/pallas_call | solution.py:561
  14.0 0.0 collective-permute-done.3.edge_ref
  14.1 0.0 collective-permute-done.2.tail_other_ref
  14.1 2.0 %shard_map.88 = (bf16[8,4,8,192]{3,2,1,0:T(8,128)(2,1)S(1)}, bf16[8,4,8,192]{3,2,1,0:T(8,128)(2,1)S(1)}) custom-call(bf16[8,384]{1,0:T(8,128)(2,1)S(1)} %get-tuple-element.27.marks_ref, bf16[17,8,384]{2,1,0:T(8,128)(2,1)S(1)} %collective-permute-done.tail_ref.tail_mine_ref, bf16[12,8,384]{2,1,0:T(8,128)(2,1)S(1)} %collective-permute-done.2.tail_other_ref, ...), custom_call_target="tpu_custom_call" | custom-call | flops 1274019840 | bytes 8388608 | tf_op jit(solution)/shard_map/pallas_call | solution.py:586
  16.1 0.5 %collective-permute-start.5 = (bf16[8,4,8,192]{3,2,1,0:T(8,128)(2,1)S(1)}, bf16[8,4,8,192]{3,2,1,0:T(8,128)(2,1)S(1)}, u32[]{:S(2)}, u32[]{:S(2)}) collective-permute-start(bf16[8,4,8,192]{3,2,1,0:T(8,128)(2,1)S(1)} %get-tuple-element.43), channel_id=1, source_target_pairs={{0,1},{1,0},{2,3},{3,2},{4,5},{5,4},{6,7},{7,6},{8,9},{9,8},{10,11... | collective-permute-start | bytes 294920 | tf_op jit(solution)/shard_map/ppermute | solution.py:598
  16.7 0.7 %shard_map.89.kept_ref = bf16[8,8,8,192]{3,2,1,0:T(8,128)(2,1)} custom-call(bf16[8,4,8,192]{3,2,1,0:T(8,128)(2,1)S(1)} %get-tuple-element.44.keep_ref), custom_call_target="tpu_custom_call" | custom-call | flops 268435456 | bytes 1048576 | tf_op jit(solution)/shard_map/pallas_call | solution.py:600
  17.3 0.3 %collective-permute-done.5.got_ref = bf16[8,4,8,192]{3,2,1,0:T(8,128)(2,1)S(1)} collective-permute-done((bf16[8,4,8,192]{3,2,1,0:T(8,128)(2,1)S(1)}, bf16[8,4,8,192]{3,2,1,0:T(8,128)(2,1)S(1)}, u32[]{:S(2)}, u32[]{:S(2)}) %collective-permute-start.5) | collective-permute-done | bytes 98336 | tf_op jit(solution)/shard_map/ppermute | solution.py:598
  17.7 0.7 %shard_map.90 = bf16[8,8,8,192]{3,2,1,0:T(8,128)(2,1)} custom-call(bf16[8,4,8,192]{3,2,1,0:T(8,128)(2,1)S(1)} %collective-permute-done.5.got_ref, bf16[8,8,8,192]{3,2,1,0:T(8,128)(2,1)} %shard_map.89.kept_ref), custom_call_target="tpu_custom_call", output_to_operand_aliasing={{}: (1, {})} | custom-call | tf_op jit(solution)/shard_map/pallas_call | solution.py:609
  (3 shorter events, 0.1 us)
Async XLA Ops:
  0.0 1.0 %copy-start.2 = (bf16[8,8,8,192]{3,2,1,0:T(8,128)(2,1)S(1)}, bf16[8,8,8,192]{3,2,1,0:T(8,128)(2,1)}, u32[]{:S(2)}) copy-start(bf16[8,8,8,192]{3,2,1,0:T(8,128)(2,1)} %raw.1) | copy-start | bytes 589828
  1.1 4.9 %collective-permute-start.1 = (bf16[36,8,384]{2,1,0:T(8,128)(2,1)S(1)}, bf16[36,8,384]{2,1,0:T(8,128)(2,1)S(1)}, u32[]{:S(2)}, u32[]{:S(2)}) collective-permute-start(bf16[36,8,384]{2,1,0:T(8,128)(2,1)S(1)} %get-tuple-element.30), channel_id=1, source_target_pairs={{0,1},{1,0},{2,3},{3,2},{4,5},{5,4},{6,7},{7,6},{8,9},{9,8},{10,11... | collective-permute-start | bytes 663560 | tf_op jit(solution)/shard_map/ppermute | solution.py:530
  1.6 9.4 %collective-permute-start = (bf16[17,8,384]{2,1,0:T(8,128)(2,1)S(1)}, bf16[17,8,384]{2,1,0:T(8,128)(2,1)S(1)}, u32[]{:S(2)}, u32[]{:S(2)}) collective-permute-start(bf16[17,8,384]{2,1,0:T(8,128)(2,1)S(1)} %get-tuple-element.28.tail_ref), channel_id=1, source_target_pairs={{0,8},{1,9},{2,10},{3,11},{4,12},{5,13},{6,14},{7,15},{16,24},{17,... | collective-permute-start | bytes 313352 | tf_op jit(solution)/shard_map/ppermute | solution.py:529
  6.1 5.0 %copy-start = (bf16[3,3,3,192,192]{4,3,2,1,0:T(8,128)(2,1)S(1)}, bf16[3,3,3,192,192]{4,3,2,1,0:T(8,128)(2,1)}, u32[]{:S(2)}) copy-start(bf16[3,3,3,192,192]{4,3,2,1,0:T(8,128)(2,1)} %w1_ref.5) | copy-start | bytes 5971972
  6.1 5.0 %copy-start.3 = (f32[192]{0:T(256)S(1)}, f32[192]{0:T(256)}, u32[]{:S(2)}) copy-start(f32[192]{0:T(256)} %param.10) | copy-start | bytes 2308
  6.1 5.0 %copy-start.4 = (f32[192]{0:T(256)S(1)}, f32[192]{0:T(256)}, u32[]{:S(2)}) copy-start(f32[192]{0:T(256)} %param.12) | copy-start | bytes 2308
  6.1 5.0 %copy-start.5 = (f32[192]{0:T(256)S(1)}, f32[192]{0:T(256)}, u32[]{:S(2)}) copy-start(f32[192]{0:T(256)} %param.13) | copy-start | bytes 2308
  6.2 6.3 %copy-start.1 = (bf16[3,3,3,192,192]{4,3,2,1,0:T(8,128)(2,1)S(1)}, bf16[3,3,3,192,192]{4,3,2,1,0:T(8,128)(2,1)}, u32[]{:S(2)}) copy-start(bf16[3,3,3,192,192]{4,3,2,1,0:T(8,128)(2,1)} %w2_ref.3) | copy-start | bytes 5971972
  6.2 6.3 %copy-start.6 = (f32[192]{0:T(256)S(1)}, f32[192]{0:T(256)}, u32[]{:S(2)}) copy-start(f32[192]{0:T(256)} %param.15) | copy-start | bytes 2308
  6.2 6.2 %collective-permute-start.4 = (bf16[2,8,8,384]{3,2,1,0:T(8,128)(2,1)S(1)}, bf16[2,8,8,384]{3,2,1,0:T(8,128)(2,1)S(1)}, u32[]{:S(2)}, u32[]{:S(2)}) collective-permute-start(bf16[2,8,8,384]{3,2,1,0:T(8,128)(2,1)S(1)} %get-tuple-element.33), channel_id=1, source_target_pairs={{0,3},{3,0},{8,11},{11,8},{2,5},{5,2},{10,13},{13,10},{4,7},{7,4},... | collective-permute-start | bytes 294920 | tf_op jit(solution)/shard_map/ppermute | solution.py:539
  9.7 4.3 %collective-permute-start.3 = (bf16[8,8,384]{2,1,0:T(8,128)(2,1)S(1)}, bf16[8,8,384]{2,1,0:T(8,128)(2,1)S(1)}, u32[]{:S(2)}, u32[]{:S(2)}) collective-permute-start(bf16[8,8,384]{2,1,0:T(8,128)(2,1)S(1)} %get-tuple-element.32), channel_id=1, source_target_pairs={{0,11},{3,8},{2,13},{5,10},{4,15},{7,12},{16,27},{19,24},{18,29},{... | collective-permute-start | bytes 147464 | tf_op jit(solution)/shard_map/ppermute | solution.py:540
  12.3 1.8 %collective-permute-start.2 = (bf16[12,8,384]{2,1,0:T(8,128)(2,1)S(1)}, bf16[12,8,384]{2,1,0:T(8,128)(2,1)S(1)}, u32[]{:S(2)}, u32[]{:S(2)}) collective-permute-start(bf16[12,8,384]{2,1,0:T(8,128)(2,1)S(1)} %get-tuple-element.31), channel_id=1, source_target_pairs={{0,1},{1,0},{2,3},{3,2},{4,5},{5,4},{6,7},{7,6},{8,9},{9,8},{10,11... | collective-permute-start | bytes 221192 | tf_op jit(solution)/shard_map/ppermute | solution.py:560
  16.1 1.5 %collective-permute-start.5 = (bf16[8,4,8,192]{3,2,1,0:T(8,128)(2,1)S(1)}, bf16[8,4,8,192]{3,2,1,0:T(8,128)(2,1)S(1)}, u32[]{:S(2)}, u32[]{:S(2)}) collective-permute-start(bf16[8,4,8,192]{3,2,1,0:T(8,128)(2,1)S(1)} %get-tuple-element.43), channel_id=1, source_target_pairs={{0,1},{1,0},{2,3},{3,2},{4,5},{5,4},{6,7},{7,6},{8,9},{9,8},{10,11... | collective-permute-start | bytes 294920 | tf_op jit(solution)/shard_map/ppermute | solution.py:598
